TPU v7x, 256 devices: a whole 4x4x8 slice. The times are simulated.
256 devices in a mesh: dp: 64 (over z, y, core), mp: 4 (over x).
Axes of the slice: x: 4, y: 4, z: 8, core: 2. Of those that a mesh axis runs over, the one named last changes fastest.
Arguments:
- query: bfloat16 [16384, 3072], P('dp', 'mp'), may hold values from -6 to 6
- key: bfloat16 [16384, 3072], P('dp', 'mp'), may hold values from -6 to 6
- value: bfloat16 [16384, 3072], P('dp', 'mp'), may hold values from -6 to 6
- send_to: int32 [16384], P('dp'), may hold values from 0 to 63, as said below
- recv_from: int32 [16384], P('dp'), may hold values from 0 to 63, as said below
- segment: int32 [16384], P('dp'), may hold values from 0 to 15, as said below
- out_weight: bfloat16 [3072, 3072], P('dp', 'mp'), may hold values from -0.109375 to 0.109375
- cotangent: bfloat16 [16384, 3072], P('dp', 'mp'), may hold values from -16 to 16
Outputs:
- grad_query: bfloat16 [16384, 3072], P('dp', 'mp')
- grad_key: bfloat16 [16384, 3072], P('dp', 'mp')
- grad_value: bfloat16 [16384, 3072], P('dp', 'mp')
- update: float32 [3072, 3072], P('dp', 'mp')
Inputs may be any that keep to these rules, and one draw needn't show every extreme that they name: `send_to`: the rows of one loader shard are grouped by destination in increasing order; at most 6 rows of one loader shard go to one sequence, and exactly 6 in some pair. `recv_from`: the positions of one sequence are grouped by source shard in increasing order; sequence d takes from shard s exactly as many positions as shard s has rows naming d. `segment`: within one sequence image ids start at 0 and never fall; some sequence reaches the largest id.
All inputs are finite; a program needn't handle non-finite values.
Results may differ from a plain program's by a relative error of at most 0.013.
Values may be sent and summed in bfloat16 or wider, within the bound.
No kernel may reach another device: no remote copies, remote signals or barrier semaphores. Data moves between devices by JAX's collectives and lax.ppermute only.
A program may use at most 128 MiB of HBM per device.

v0:
```python
import math

import jax
import jax.numpy as jnp
from jax import lax
from jax.sharding import PartitionSpec as P

D = 3072
HD = 128
NS_STEPS = 3


coef_a = 3.4445
coef_b = -4.775
coef_c = 2.0315
norm_eps = 1e-07


def run_ranks(labels, group_count):
    peers = jnp.arange(group_count, dtype=jnp.int32)
    hot = (labels[:, None] == peers[None, :]).astype(jnp.int32)
    total = jnp.sum(hot, axis=0)
    start = jnp.cumsum(total) - total
    position = jnp.arange(labels.shape[0], dtype=jnp.int32)
    return position - jnp.sum(hot * start[None, :], axis=1)


def ns_update(current, gram_now, final_sum):
    high = lax.Precision.HIGHEST
    for iteration in range(NS_STEPS):
        square = jnp.einsum("hij,hjk->hik", gram_now, gram_now, precision=high)
        mixer = coef_b * gram_now + coef_c * square
        current = coef_a * current + jnp.einsum("dhi,hij->dhj", current, mixer, precision=high)
        if iteration + 1 < NS_STEPS:
            gram_now = final_sum(current)
    return current


def shards(query, key, value, send_to, recv_from, segment, out_weight, cotangent):
    group_count = lax.axis_size("dp")
    row_count = query.shape[0]
    capacity = row_count // group_count + 2
    width_here = query.shape[1]
    heads_here = width_here // HD
    feat_here = out_weight.shape[0]
    scale = 1.0 / math.sqrt(HD)
    send_rank = run_ranks(send_to, group_count)

    def place(field):
        slots = jnp.zeros((group_count, capacity, field.shape[1]), field.dtype)
        return slots.at[send_to, send_rank].set(field)

    arrived = (
        lax.all_to_all(place(query), "dp", split_axis=0, concat_axis=0, tiled=True),
        lax.all_to_all(place(key), "dp", split_axis=0, concat_axis=0, tiled=True),
        lax.all_to_all(place(value), "dp", split_axis=0, concat_axis=0, tiled=True),
    )
    recv_rank = run_ranks(recv_from, group_count)
    packed_q = arrived[0][recv_from, recv_rank]
    packed_k = arrived[1][recv_from, recv_rank]
    packed_v = arrived[2][recv_from, recv_rank]
    q_heads = packed_q.reshape(row_count, heads_here, HD)
    k_heads = packed_k.reshape(row_count, heads_here, HD)
    v_heads = packed_v.reshape(row_count, heads_here, HD)
    scores = (
        jnp.einsum("qhd,khd->hqk", q_heads, k_heads, preferred_element_type=jnp.float32) * scale
    )
    same = segment[:, None] == segment[None, :]
    scores = jnp.where(same[None, :, :], scores, -jnp.inf)
    top = jnp.max(scores, axis=-1, keepdims=True)
    expo = jnp.exp(scores - top)
    prob_float = expo / jnp.sum(expo, axis=-1, keepdims=True)
    prob = prob_float.astype(jnp.bfloat16)
    attended = jnp.einsum("hqk,khd->qhd", prob, v_heads, preferred_element_type=jnp.float32).astype(
        jnp.bfloat16
    )
    attended = attended.reshape(row_count, width_here)
    full_cot = lax.all_gather(cotangent, "mp", axis=1, tiled=True)
    columns = full_cot
    d_attended = jnp.dot(
        columns,
        lax.all_gather(out_weight, "dp", axis=0, tiled=True),
        preferred_element_type=jnp.float32,
    ).astype(jnp.bfloat16)
    d_heads = d_attended.reshape(row_count, heads_here, HD)
    grad_value = jnp.einsum(
        "hqk,qhd->khd", prob, d_heads, preferred_element_type=jnp.float32
    ).astype(jnp.bfloat16)
    d_prob = jnp.einsum("qhd,khd->hqk", d_heads, v_heads, preferred_element_type=jnp.float32)
    delta = jnp.sum(d_prob * prob_float, axis=-1, keepdims=True)
    d_score = (prob_float * (d_prob - delta) * scale).astype(jnp.bfloat16)
    grad_query = jnp.einsum(
        "hqk,khd->qhd", d_score, k_heads, preferred_element_type=jnp.float32
    ).astype(jnp.bfloat16)
    grad_key = jnp.einsum(
        "hqk,qhd->khd", d_score, q_heads, preferred_element_type=jnp.float32
    ).astype(jnp.bfloat16)
    columns = full_cot
    grad_rows = lax.psum_scatter(
        lax.dot_general(
            columns, attended, (((0,), (0,)), ((), ())), preferred_element_type=jnp.float32
        ),
        "dp",
        scatter_dimension=0,
        tiled=True,
    )
    whole = (
        lax.all_gather(grad_rows.astype(jnp.bfloat16), "dp", axis=0, tiled=True)
        .astype(grad_rows.dtype)
        .reshape(D, heads_here, HD)
    )
    norm = jnp.sqrt(jnp.sum(whole * whole, axis=(0, 2)))
    current = whole / (norm[None, :, None] + norm_eps)

    def local_gram(field):
        return jnp.einsum("dhi,dhj->hij", field, field, precision=lax.Precision.HIGHEST)

    result = ns_update(current, local_gram(current), local_gram)
    result = lax.dynamic_slice_in_dim(result, lax.axis_index("dp") * feat_here, feat_here, 0)
    update = (math.sqrt(D) * result).reshape(feat_here, width_here)
    return (
        grad_query.reshape(row_count, width_here),
        grad_key.reshape(row_count, width_here),
        grad_value.reshape(row_count, width_here),
        update,
    )


def solution(mesh):
    return jax.shard_map(
        shards,
        mesh=mesh,
        in_specs=(
            P("dp", "mp"),
            P("dp", "mp"),
            P("dp", "mp"),
            P("dp"),
            P("dp"),
            P("dp"),
            P("dp", "mp"),
            P("dp", "mp"),
        ),
        out_specs=(P("dp", "mp"), P("dp", "mp"), P("dp", "mp"), P("dp", "mp")),
        check_vma=False,
    )
```

profile of v0, /device:TPU:1, one launch (start us, length us, event | category | flops | bytes accessed | tf_op | source)
XLA Modules:
  0.0 548.4 jit_solution(3326130393746158526)
XLA Ops:
  9.8 24.3 %scatter_fusion = bf16[64,6,768]{2,0,1:T(8,128)(2,1)S(1)} fusion(bf16[64,6,768]{2,0,1:T(8,128)(2,1)S(1)} %broadcast.90.clone, s32[256]{0:T(256)S(1)} %bitcast.67, bf16[256,768]{1,0:T(8,128)(2,1)} %param.9), kind=kCustom, calls=%fused_computation.3 | custom fusion | bytes 1181696 | tf_op jit(solution)/shard_map/scatter | solution.py:51
  35.3 13.1 %all-to-all-start = ((bf16[64,6,768]{2,1,0:T(8,128)(2,1)}), bf16[64,6,768]{2,1,0:T(8,128)(2,1)S(1)}, u32[]{:S(2)}, u32[]{:S(2)}) async-start(bf16[64,6,768]{2,1,0:T(8,128)(2,1)} %copy.137), calls=%async_computation | async-start | bytes 1572864 | tf_op jit(solution)/shard_map/all_to_all | solution.py:55
  48.6 14.9 %scatter_fusion.2 = bf16[64,6,768]{2,0,1:T(8,128)(2,1)S(1)} fusion(bf16[64,6,768]{2,0,1:T(8,128)(2,1)S(1)} %broadcast.90.clone.1, s32[256]{0:T(256)S(1)} %bitcast.68, bf16[256,768]{1,0:T(8,128)(2,1)S(1)} %copy-done.2), kind=kCustom, calls=%fused_computation.5 | custom fusion | bytes 1181696 | tf_op jit(solution)/shard_map/scatter | solution.py:51
  64.7 6.6 %all-to-all-done = bf16[64,6,768]{2,1,0:T(8,128)(2,1)S(1)} async-done(((bf16[64,6,768]{2,1,0:T(8,128)(2,1)}), bf16[64,6,768]{2,1,0:T(8,128)(2,1)S(1)}, u32[]{:S(2)}, u32[]{:S(2)}) %all-to-all-start) | async-done | bytes 589856 | tf_op jit(solution)/shard_map/all_to_all | solution.py:55
  71.2 6.2 %all-to-all-start.2 = ((bf16[64,6,768]{2,1,0:T(8,128)(2,1)}), bf16[64,6,768]{2,1,0:T(8,128)(2,1)S(1)}, u32[]{:S(2)}, u32[]{:S(2)}) async-start(bf16[64,6,768]{2,1,0:T(8,128)(2,1)} %copy.147), calls=%async_computation.2 | async-start | bytes 1572864 | tf_op jit(solution)/shard_map/all_to_all | solution.py:56
  78.3 14.9 %scatter_fusion.1 = bf16[64,6,768]{2,0,1:T(8,128)(2,1)S(1)} fusion(bf16[64,6,768]{2,0,1:T(8,128)(2,1)S(1)} %broadcast.90.clone.2, s32[256]{0:T(256)S(1)} %bitcast.69, bf16[256,768]{1,0:T(8,128)(2,1)S(1)} %copy-done.3), kind=kCustom, calls=%fused_computation.4 | custom fusion | bytes 1181696 | tf_op jit(solution)/shard_map/scatter | solution.py:51
  94.5 5.8 %all-to-all-done.2 = bf16[64,6,768]{2,1,0:T(8,128)(2,1)S(1)} async-done(((bf16[64,6,768]{2,1,0:T(8,128)(2,1)}), bf16[64,6,768]{2,1,0:T(8,128)(2,1)S(1)}, u32[]{:S(2)}, u32[]{:S(2)}) %all-to-all-start.2) | async-done | bytes 589856 | tf_op jit(solution)/shard_map/all_to_all | solution.py:56
  100.2 6.2 %all-to-all-start.1 = ((bf16[64,6,768]{2,1,0:T(8,128)(2,1)}), bf16[64,6,768]{2,1,0:T(8,128)(2,1)S(1)}, u32[]{:S(2)}, u32[]{:S(2)}) async-start(bf16[64,6,768]{2,1,0:T(8,128)(2,1)} %copy.141), calls=%async_computation.1 | async-start | bytes 1572864 | tf_op jit(solution)/shard_map/all_to_all | solution.py:54
  107.8 2.4 gather_fusion
  110.5 2.4 gather_fusion.2
  113.1 16.2 %all-to-all-done.1 = bf16[64,6,768]{2,1,0:T(8,128)(2,1)S(1)} async-done(((bf16[64,6,768]{2,1,0:T(8,128)(2,1)}), bf16[64,6,768]{2,1,0:T(8,128)(2,1)S(1)}, u32[]{:S(2)}, u32[]{:S(2)}) %all-to-all-start.1) | async-done | bytes 589856 | tf_op jit(solution)/shard_map/all_to_all | solution.py:54
  129.3 2.4 gather_fusion.1
  131.9 1.9 fusion.41
  133.8 1.7 convolution_convert_fusion
  135.5 6.5 %convolution_bitcast_fusion.1 = f32[3072,768]{0,1:T(8,128)} fusion(bf16[256,768]{0,1:T(8,128)(2,1)S(1)} %bitcast.77, bf16[256,3072]{1,0:T(8,128)(2,1)} %all-gather.4.cloned.1.call-done), kind=kOutput, calls=%fused_computation.12 | convolution fusion | flops 1207959552 | bytes 11403264 | tf_op jit(solution)/shard_map/dot_general | solution.py:100
  142.0 9.6 %copy.188 = f32[3072,768]{1,0:T(8,128)} copy(f32[3072,768]{0,1:T(8,128)} %convolution_bitcast_fusion.1) | data formatting | bytes 18874368
  152.6 145.9 %reduce-scatter.4.cloned.1.call-done = f32[48,768]{1,0:T(8,128)} async-done(((f32[3072,768]{1,0:T(8,128)}), f32[48,768]{1,0:T(8,128)}) %reduce-scatter.4.cloned.1.call-update) | async-done | bytes 147472 | tf_op jit(solution)/shard_map/reduce_scatter | solution.py:99
  298.5 1.6 convert_element_type.58
  300.1 83.9 %all-gather.6.cloned.1.call-done = bf16[3072,768]{1,0:T(8,128)(2,1)} async-done(((bf16[48,768]{1,0:T(8,128)(2,1)}), bf16[3072,768]{1,0:T(8,128)(2,1)}) %all-gather.6.cloned.1.call-update) | async-done | bytes 4718608 | tf_op jit(solution)/shard_map/all_gather | solution.py:82
  384.0 3.7 convolution_convert_fusion.2
  388.3 2.6 fusion.14
  391.8 2.6 fusion.17
  395.3 1.8 convolution_convert_fusion.1
  398.1 65.7 %all-gather.8.cloned.1.call-done = bf16[3072,768]{1,0:T(8,128)(2,1)} async-done(((bf16[48,768]{1,0:T(8,128)(2,1)}), bf16[3072,768]{1,0:T(8,128)(2,1)}) %all-gather.8.cloned.1.call-update) | async-done | bytes 4718608 | tf_op jit(solution)/shard_map/all_gather | solution.py:108
  463.8 3.3 multiply_reduce_fusion
  467.3 7.5 %copy.157 = f32[3072,768]{0,1:T(8,128)} copy(bf16[3072,768]{1,0:T(8,128)(2,1)} %all-gather.8.cloned.1.call-done) | data formatting | bytes 14155776 | tf_op jit(solution)/shard_map/convert_element_type | solution.py:109
  474.8 16.1 %fusion.3 = f32[6,128,128]{2,1,0:T(8,128)S(1)} fusion(f32[3072,6,128]{0,2,1:T(8,128)} %bitcast.70, f32[6]{0:T(128)S(1)} %sqrt_add_fusion), kind=kOutput, calls=%fused_computation.15 | convolution fusion | flops 3626237952 | bytes 9830424 | tf_op jit(solution)/shard_map/dhi,dhj->hij/dot_general | solution.py:116
  491.4 10.0 %bitcast_add_fusion.1 = f32[3072,6,128]{0,2,1:T(8,128)S(1)} fusion(f32[6,128,128]{2,1,0:T(8,128)S(1)} %fusion.22, f32[3072,6,128]{0,2,1:T(8,128)S(1)} %bitcast.71, f32[6]{0:T(128)S(1)} %sqrt_add_fusion), kind=kOutput, calls=%fused_computation.9 | convolution fusion | flops 3633315840 | bytes 19267608 | tf_op jit(solution)/shard_map/dhi,hij->dhj/dot_general | solution.py:33
  501.5 9.0 %fusion.43 = f32[6,128,128]{2,1,0:T(8,128)S(1)} fusion(f32[3072,6,128]{0,2,1:T(8,128)S(1)} %bitcast_add_fusion.1), kind=kOutput, calls=%fused_computation.73 | convolution fusion | flops 3623878656 | bytes 9830400 | tf_op jit(solution)/shard_map/dhi,dhj->hij/dot_general | solution.py:116
  511.0 10.5 %bitcast_add_fusion = f32[3072,6,128]{0,2,1:T(8,128)S(1)} fusion(f32[3072,6,128]{0,2,1:T(8,128)S(1)} %bitcast_add_fusion.1, f32[6,128,128]{2,1,0:T(8,128)S(1)} %fusion.21), kind=kOutput, calls=%fused_computation.8 | convolution fusion | flops 3628597248 | bytes 19267584 | tf_op jit(solution)/shard_map/dhi,hij->dhj/dot_general | solution.py:33
  521.6 8.9 %fusion.44 = f32[6,128,128]{2,1,0:T(8,128)S(1)} fusion(f32[3072,6,128]{0,2,1:T(8,128)S(1)} %bitcast_add_fusion), kind=kOutput, calls=%fused_computation.74 | convolution fusion | flops 3623878656 | bytes 9830400 | tf_op jit(solution)/shard_map/dhi,dhj->hij/dot_general | solution.py:116
  531.0 9.5 %convolution_bitcast_fusion = f32[3072,6,128]{0,2,1:T(8,128)S(1)} fusion(f32[6,128,128]{2,1,0:T(8,128)S(1)} %fusion.20, f32[3072,6,128]{0,2,1:T(8,128)S(1)} %bitcast_add_fusion), kind=kOutput, calls=%fused_computation.11 | convolution fusion | flops 3623878656 | bytes 19267584 | tf_op jit(solution)/shard_map/dhi,hij->dhj/dot_general | solution.py:33
  (62 shorter events, 16.2 us)
Async XLA Ops:
  34.1 14.5 %copy-start.2 = (bf16[256,768]{1,0:T(8,128)(2,1)S(1)}, bf16[256,768]{1,0:T(8,128)(2,1)}, u32[]{:S(2)}) copy-start(bf16[256,768]{1,0:T(8,128)(2,1)} %param.10) | copy-start | bytes 1179652
  35.3 35.9 %all-to-all-start = ((bf16[64,6,768]{2,1,0:T(8,128)(2,1)}), bf16[64,6,768]{2,1,0:T(8,128)(2,1)S(1)}, u32[]{:S(2)}, u32[]{:S(2)}) async-start(bf16[64,6,768]{2,1,0:T(8,128)(2,1)} %copy.137), calls=%async_computation | async-start | bytes 1572864 | tf_op jit(solution)/shard_map/all_to_all | solution.py:55
  64.7 13.6 %copy-start.3 = (bf16[256,768]{1,0:T(8,128)(2,1)S(1)}, bf16[256,768]{1,0:T(8,128)(2,1)}, u32[]{:S(2)}) copy-start(bf16[256,768]{1,0:T(8,128)(2,1)} %param.8) | copy-start | bytes 1179652
  71.2 29.0 %all-to-all-start.2 = ((bf16[64,6,768]{2,1,0:T(8,128)(2,1)}), bf16[64,6,768]{2,1,0:T(8,128)(2,1)S(1)}, u32[]{:S(2)}, u32[]{:S(2)}) async-start(bf16[64,6,768]{2,1,0:T(8,128)(2,1)} %copy.147), calls=%async_computation.2 | async-start | bytes 1572864 | tf_op jit(solution)/shard_map/all_to_all | solution.py:56
  77.5 58.0 %all-gather.4.cloned.1.call-start = ((), (), s32[]{:S(2)}) async-start(), calls=%async_computation.4 | async-start | bytes 1966080 | tf_op jit(solution)/shard_map/all_gather | solution.py:78
  93.2 13.8 %copy-start.5 = (s32[256]{0:T(256)S(1)}, s32[256]{0:T(256)}, u32[]{:S(2)}) copy-start(s32[256]{0:T(256)} %param.12) | copy-start | bytes 3076
  93.2 14.4 %copy-start.4 = (s32[256]{0:T(256)S(1)}, s32[256]{0:T(256)}, u32[]{:S(2)}) copy-start(s32[256]{0:T(256)} %param.13) | copy-start | bytes 3076
  100.2 29.0 %all-to-all-start.1 = ((bf16[64,6,768]{2,1,0:T(8,128)(2,1)}), bf16[64,6,768]{2,1,0:T(8,128)(2,1)S(1)}, u32[]{:S(2)}, u32[]{:S(2)}) async-start(bf16[64,6,768]{2,1,0:T(8,128)(2,1)} %copy.141), calls=%async_computation.1 | async-start | bytes 1572864 | tf_op jit(solution)/shard_map/all_to_all | solution.py:54
  106.5 192.0 %reduce-scatter.4.cloned.1.call-start = ((), (), s32[]{:S(2)}) async-start(), calls=%async_computation.7 | async-start | bytes 9584640 | tf_op jit(solution)/shard_map/reduce_scatter | solution.py:99
  151.6 232.4 %copy-start.1 = (bf16[256,3072]{1,0:T(8,128)(2,1)S(1)}, bf16[256,3072]{1,0:T(8,128)(2,1)}, u32[]{:S(2)}) copy-start(bf16[256,3072]{1,0:T(8,128)(2,1)} %all-gather.4.cloned.1.call-done) | copy-start | bytes 4718596
  151.6 232.4 %all-gather.6.cloned.1.call-start = ((), (), s32[]{:S(2)}) async-start(), calls=%async_computation.5 | async-start | bytes 4792320 | tf_op jit(solution)/shard_map/all_gather | solution.py:82
  152.4 311.5 %all-gather.8.cloned.1.call-start = ((), (), s32[]{:S(2)}) async-start(), calls=%async_computation.6 | async-start | bytes 4792320 | tf_op jit(solution)/shard_map/all_gather | solution.py:108
  474.8 16.6 %copy-start = (f32[3072,768]{0,1:T(8,128)S(1)}, f32[3072,768]{0,1:T(8,128)}, u32[]{:S(2)}) copy-start(f32[3072,768]{0,1:T(8,128)} %copy.157) | copy-start | bytes 28311556
Sparse Core Ops, SparseCore 0:
  80.1 29.9 all-gather.3
  151.7 146.6 reduce-scatter.3
  301.2 82.7 all-gather.5
  387.2 76.6 all-gather.7
where the time goes:
time: 555 us; the launch traced here: 548 us
  waiting for transfers between devices  326 us (59%)
  local copies, waits for them, and re-layouts  87 us (16%)
  matrix products  86.7 us (16%)
  starting transfers between devices  26.4 us (5%)
  between operations  14.4 us (3%)
  other arithmetic  8.31 us (1%)
    reduce_scatter x1, waiting for transfers between devices, shards(): lax.psum_scatter(lax.dot_general(columns, attended, (((0,), (0,)), ((), (...  146 us
    all_gather x1, waiting for transfers between devices, shards(): lax.all_gather(out_weight, 'dp', axis=0, tiled=True)  83.9 us
    all_gather x1, waiting for transfers between devices, shards(): lax.all_gather(grad_rows.astype(jnp.bfloat16), 'dp', axis=0, tiled=True)  65.7 us
    scatter x6, local copies, waits for them, and re-layouts, place(): return slots.at[send_to, send_rank].set(field)  57.8 us
    dot_general x3, matrix products, local_gram(): jnp.einsum('dhi,dhj->hij', field, field, precision=lax.Precision.HIGHEST)  34 us
    dot_general x3, matrix products, ns_update(): jnp.einsum('dhi,hij->dhj', current, mixer, precision=high)  30.1 us
    all_to_all x1, waiting for transfers between devices, shards(): lax.all_to_all(place(query), 'dp', split_axis=0, concat_axis=0, tiled=True)  16.2 us
    unnamed x17, local copies, waits for them, and re-layouts  13.2 us
  transfers between devices with their start and end apart: 7, of which 6 were waited for; matrix products, arithmetic and copies ran while one was open for 11% of the time, Pallas kernels for 0%

commit v1 on v0

v1 whole, which is shorter than its diff:
```python
import math

import jax
import jax.numpy as jnp
from jax import lax
from jax.experimental import pallas as pl
from jax.experimental.pallas import tpu as pltpu
from jax.sharding import Mesh, PartitionSpec as P

D = 3072
HD = 128
ROWS = 256
GROUPS = 64
SLOTS = 6
HEADS_HERE = 6
BLOCKS = 3 * HEADS_HERE
TILE = 16
TILES = 7
FLAT = GROUPS * TILE
Z, Y, C, X = 8, 4, 2, 4
FEAT = 48
HALF = HEADS_HERE * HD // 2
NS_STEPS = 3

coef_a = 3.4445
coef_b = -4.775
coef_c = 2.0315
norm_eps = 1e-07
scale = 1.0 / math.sqrt(HD)
f32 = jnp.float32
bf16 = jnp.bfloat16


def find_patterns():
    found = []
    for tile in range(3):
        rows = [tile * TILE + i for i in range(TILE)]
        for block in sorted({r // SLOTS for r in rows}):
            found.append((tile, block))
    return found


PATTERNS = find_patterns()


def pattern_users(tile, block):
    return [
        (tile + 3 * n, block + 8 * n)
        for n in range(3)
        if tile + 3 * n < TILES and block + 8 * n < BLOCKS
    ]


def place_kernel(label_ref, q_hbm, k_hbm, v_hbm, out_ref, q_ref, k_ref, v_ref, sems):
    fields = (q_ref, k_ref, v_ref)
    copies = [
        pltpu.make_async_copy(source, target, sems.at[n])
        for n, (source, target) in enumerate(zip((q_hbm, k_hbm, v_hbm), fields))
    ]
    for copy in copies:
        copy.start()

    label = label_ref[...]
    group = lax.broadcasted_iota(jnp.int32, (GROUPS, ROWS), 0)
    before = jnp.sum(jnp.where(label < group, 1, 0), axis=1, keepdims=True)
    start = jnp.sum(jnp.where(label == group, before, 0), axis=0, keepdims=True)
    code = 8 * label + lax.broadcasted_iota(jnp.int32, (1, ROWS), 1) - start

    def block_of(j):
        return fields[j // HEADS_HERE][:, (j % HEADS_HERE) * HD : (j % HEADS_HERE + 1) * HD]

    row = lax.broadcasted_iota(jnp.int32, (TILE, ROWS), 0)
    eights = 8 * lax.broadcasted_iota(jnp.int32, (GROUPS, TILE, ROWS), 0)
    for copy in copies:
        copy.wait()
    for first in range(3):
        total = {}
        for tile, block in PATTERNS:
            if tile != first:
                continue
            slot = row + (TILE * tile - SLOTS * block)
            wanted = jnp.where((slot >= 0) & (slot < SLOTS), code - slot, -1)
            hot = jnp.where(eights == wanted[None], 1.0, 0.0).astype(bf16).reshape(FLAT, ROWS)
            users = pattern_users(tile, block)
            wide = jnp.concatenate([block_of(j) for _, j in users], axis=1)
            got = jnp.dot(hot, wide, preferred_element_type=f32)
            for n, (t, _) in enumerate(users):
                part = got[:, n * HD : (n + 1) * HD]
                total[t] = part if t not in total else total[t] + part
        for t, rows in total.items():
            out_ref[:, t * TILE : (t + 1) * TILE, :] = rows.astype(bf16).reshape(GROUPS, TILE, HD)


def parts_kernel(cot_ref, weight_ref, *out_refs):
    weight = weight_ref[...]
    for k, out_ref in enumerate(out_refs):
        out_ref[...] = lax.dot_general(
            cot_ref[k], weight, (((0,), (0,)), ((), ())), preferred_element_type=f32
        ).astype(bf16)


def soft(q, k, same):
    scores = (
        lax.dot_general(q, k, (((1,), (1,)), ((), ())), preferred_element_type=f32) * scale
    )
    scores = jnp.where(same, scores, -jnp.inf)
    top = jnp.max(scores, axis=-1, keepdims=True)
    expo = jnp.exp(scores - top)
    return expo / jnp.sum(expo, axis=-1, keepdims=True)


def forward_kernel(
    core_ref, from_row, from_col, row_ref, col_ref, slots_ref, packed_ref, own_ref, other_ref
):
    before = jnp.sum(jnp.where(from_row[...] < from_col[...], 1, 0), axis=1, keepdims=True)
    code = 8 * from_col[...] + lax.broadcasted_iota(jnp.int32, (ROWS, 1), 0) - before
    lane = lax.broadcasted_iota(jnp.int32, (1, FLAT), 1)
    group = lane // TILE
    total = {}
    for tile, block in PATTERNS:
        slot = lane - TILE * group + (TILE * tile - SLOTS * block)
        wanted = jnp.where((slot >= 0) & (slot < SLOTS), 8 * group + slot, -1)
        hot = jnp.where(code == wanted, 1.0, 0.0).astype(bf16)
        users = pattern_users(tile, block)
        wide = jnp.concatenate(
            [
                slots_ref[:, t * TILE : (t + 1) * TILE, :].reshape(FLAT, HD)
                for t, _ in users
            ],
            axis=1,
        )
        got = jnp.dot(hot, wide, preferred_element_type=f32)
        for n, (_, j) in enumerate(users):
            part = got[:, n * HD : (n + 1) * HD]
            if j in total:
                packed_ref[:, j * HD : (j + 1) * HD] = (total.pop(j) + part).astype(bf16)
            elif SLOTS * j // TILE != (SLOTS * j + SLOTS - 1) // TILE:
                total[j] = part
            else:
                packed_ref[:, j * HD : (j + 1) * HD] = part.astype(bf16)
    same = row_ref[...] == col_ref[...]
    core = core_ref[0]
    for side, out_ref in enumerate((own_ref, other_ref)):
        first = 3 * (core if side == 0 else 1 - core)
        for i in range(3):

            def block_at(base):
                at = pl.multiple_of((first + i + base) * HD, HD)
                return packed_ref[:, pl.ds(at, HD)]

            prob = soft(block_at(0), block_at(HEADS_HERE), same).astype(bf16)
            value = block_at(2 * HEADS_HERE)
            out_ref[:, i * HD : (i + 1) * HD] = jnp.dot(
                prob, value, preferred_element_type=f32
            ).astype(bf16)


def grad_near_kernel(own_cot, other_cot, own, up, down, swap, swap_up, swap_down, out_ref):
    terms = (
        (own_cot, 0, own),
        (own_cot, 1, up),
        (own_cot, 3, down),
        (other_cot, 0, swap),
        (other_cot, 1, swap_up),
        (other_cot, 3, swap_down),
    )
    total = None
    for cot, k, field in terms:
        product = jnp.dot(cot[k], field[...], preferred_element_type=f32)
        total = product if total is None else total + product
    out_ref[...] = total


def grad_far_kernel(own_cot, other_cot, own_far, swap_far, near_ref, out_ref):
    total = near_ref[...] + jnp.dot(own_cot[2], own_far[...], preferred_element_type=f32)
    total = total + jnp.dot(other_cot[2], swap_far[...], preferred_element_type=f32)
    out_ref[...] = total.astype(bf16).reshape(out_ref.shape)


def gram_kernel(parts_ref, grad_ref, gram_ref):
    grad = jnp.sum(parts_ref[...].astype(f32), axis=0)
    grad_ref[...] = grad
    for h in range(3):
        head = grad[:, h * HD : (h + 1) * HD]
        gram_ref[h * HD : (h + 1) * HD, :] = lax.dot_general(
            head,
            head,
            (((0,), (0,)), ((), ())),
            precision=lax.Precision.HIGHEST,
            preferred_element_type=f32,
        )


def update_kernel(core_ref, gram_ref, grad_ref, here_ref, there_ref, hold_ref):
    def mul(a, b):
        return jnp.dot(a, b, precision=lax.Precision.HIGHEST, preferred_element_type=f32)

    row = lax.broadcasted_iota(jnp.int32, (HD, HD), 0)
    col = lax.broadcasted_iota(jnp.int32, (HD, HD), 1)
    eye = jnp.where(row == col, 1.0, 0.0).astype(f32)
    grams, norms = [], []
    for h in range(3):
        gram = gram_ref[h * HD : (h + 1) * HD, :]
        norm = jnp.sqrt(jnp.sum(gram * eye, axis=(0, 1), keepdims=True)) + norm_eps
        grams.append(gram / norm / norm)
        norms.append(norm)
    results = [None] * 3
    for step in range(NS_STEPS):
        squares = [mul(g, g) for g in grams]
        mixers = [
            coef_a * eye + coef_b * g + coef_c * s for g, s in zip(grams, squares)
        ]
        results = [m if r is None else mul(r, m) for r, m in zip(results, mixers)]
        if step + 1 < NS_STEPS:
            grams = [mul(g, m) for g, m in zip(grams, mixers)]
            grams = [mul(g, m) for g, m in zip(grams, mixers)]
    for h in range(3):
        field = grad_ref[:, h * HD : (h + 1) * HD] / norms[h]
        final = mul(field, results[h]) * math.sqrt(D)
        hold_ref[:, :, h * HD : (h + 1) * HD] = final.reshape(C, FEAT, HD)
    core = core_ref[0]
    here_ref[...] = hold_ref[core]
    there_ref[...] = hold_ref[1 - core]


def join_kernel(core_ref, here_ref, there_ref, out_ref):
    core = core_ref[0]
    out_ref[:, pl.ds(pl.multiple_of(core * HALF, HD), HALF)] = here_ref[...]
    out_ref[:, pl.ds(pl.multiple_of((1 - core) * HALF, HD), HALF)] = there_ref[...]


def backward_kernel(row_ref, col_ref, q_ref, k_ref, v_ref, d0, d1, d2, d3, gq_ref, gk_ref, gv_ref):
    same = row_ref[...] == col_ref[...]
    q, k, v = q_ref[...], k_ref[...], v_ref[...]
    near = d0[...].astype(f32) + d1[...].astype(f32)
    d_out = (near + (d2[...].astype(f32) + d3[...].astype(f32))).astype(bf16)
    prob = soft(q, k, same)
    first = (((0,), (0,)), ((), ()))
    gv_ref[...] = lax.dot_general(
        prob.astype(bf16), d_out, first, preferred_element_type=f32
    ).astype(bf16)
    d_prob = lax.dot_general(d_out, v, (((1,), (1,)), ((), ())), preferred_element_type=f32)
    delta = jnp.sum(d_prob * prob, axis=-1, keepdims=True)
    d_score = (prob * (d_prob - delta) * scale).astype(bf16)
    gq_ref[...] = jnp.dot(d_score, k, preferred_element_type=f32).astype(bf16)
    gk_ref[...] = lax.dot_general(d_score, q, first, preferred_element_type=f32).astype(bf16)


def shift(field, axis, step):
    size = lax.axis_size(axis)
    return lax.ppermute(field, axis, [(i, (i + step) % size) for i in range(size)])


def local(kernel, name, out_shape, *operands, scalars=0, **options):
    smem = pl.BlockSpec(memory_space=pltpu.SMEM)
    vmem = pl.BlockSpec(memory_space=pltpu.VMEM)
    return pl.pallas_call(
        kernel,
        in_specs=[smem] * scalars + [vmem] * (len(operands) - scalars),
        out_shape=out_shape,
        compiler_params=pltpu.CompilerParams(vmem_limit_bytes=48 * 1024 * 1024),
        name=name,
        **options,
    )(*operands)


def array(shape, kind):
    return jax.ShapeDtypeStruct(shape, kind)


def shards(query, key, value, send_to, recv_from, segment, out_weight, cotangent):
    core = lax.axis_index("c")
    core_row = core.astype(jnp.int32).reshape(1)
    big = pltpu.CompilerParams(vmem_limit_bytes=48 * 1024 * 1024)
    everything = ("z", "y", "c")

    vmem = pl.BlockSpec(memory_space=pltpu.VMEM)
    hbm = pl.BlockSpec(memory_space=pltpu.HBM)
    field = pltpu.VMEM((ROWS, HEADS_HERE * HD), bf16)
    slots = pl.pallas_call(
        place_kernel,
        in_specs=[vmem, hbm, hbm, hbm],
        out_shape=array((GROUPS, TILES * TILE, HD), bf16),
        scratch_shapes=[field, field, field, pltpu.SemaphoreType.DMA((3,))],
        compiler_params=pltpu.CompilerParams(vmem_limit_bytes=60 * 1024 * 1024),
        name="place",
    )(send_to[None, :], query, key, value)
    arrived = lax.all_to_all(slots, everything, split_axis=0, concat_axis=0, tiled=True)

    cotangent, slots = lax.optimization_barrier((cotangent, slots))
    feature = jnp.arange(X * FEAT * Y, dtype=jnp.int32).reshape(2, Y, C, FEAT)
    feature = feature.transpose(1, 0, 2, 3).reshape(Y, -1)
    feature = jnp.roll(feature, -lax.axis_index("y"), axis=0).reshape(-1)
    perm = (feature[:, None] == jnp.arange(feature.size)[None, :]).astype(bf16)
    turned = lax.dot_general(
        perm, cotangent, (((1,), (1,)), ((), ())), preferred_element_type=f32
    ).astype(bf16)
    turned = turned.reshape(Y, 4 * FEAT, ROWS)
    turned = jnp.stack([turned[0]] + [shift(turned[k], "y", k) for k in range(1, Y)])
    cot_own = lax.all_gather(turned, "x", axis=1, tiled=True)
    cot_other = shift(cot_own, "c", 1)

    weight = lax.all_gather(out_weight, ("z", "c"), axis=0, tiled=True)
    part = array((ROWS, HEADS_HERE * HD), bf16)
    d_parts = local(parts_kernel, "d_parts", (part,) * Y, cot_own, weight)

    seg_row = segment[None, :]
    seg_col = segment[:, None]
    packed, own, other = local(
        forward_kernel,
        "forward",
        (
            array((ROWS, BLOCKS * HD), bf16),
            array((ROWS, HALF), bf16),
            array((ROWS, HALF), bf16),
        ),
        core_row,
        recv_from[None, :],
        recv_from[:, None],
        seg_row,
        seg_col,
        arrived,
        scalars=1,
    )

    own_up = shift(own, "y", 1)
    own_down = shift(own, "y", -1)
    swap = shift(other, "c", 1)
    swap_up = shift(swap, "y", 1)
    swap_down = shift(swap, "y", -1)
    own_far = shift(own_up, "y", 1)
    swap_far = shift(swap_down, "y", -1)
    grad = local(
        grad_near_kernel,
        "grad_near",
        array((Z * C * FEAT, HALF), f32),
        cot_own,
        cot_other,
        own,
        own_up,
        own_down,
        swap,
        swap_up,
        swap_down,
    )
    grad = local(
        grad_far_kernel,
        "grad_far",
        array((Z, C * FEAT, HALF), bf16),
        cot_own,
        cot_other,
        own_far,
        swap_far,
        grad,
    )
    parts = lax.all_to_all(grad, "z", split_axis=0, concat_axis=0, tiled=True)
    parts, *d_parts = lax.optimization_barrier((parts, *d_parts))
    d_parts = [d_parts[0]] + [shift(d_parts[k], "y", -k) for k in range(1, Y)]

    def column(base):
        return pl.BlockSpec((ROWS, HD), lambda h, base=base: (0, base + h))

    out = jax.ShapeDtypeStruct((ROWS, HEADS_HERE * HD), bf16)
    grads = pl.pallas_call(
        backward_kernel,
        grid=(HEADS_HERE,),
        in_specs=[
            pl.BlockSpec((1, ROWS), lambda h: (0, 0)),
            pl.BlockSpec((ROWS, 1), lambda h: (0, 0)),
            column(0),
            column(HEADS_HERE),
            column(2 * HEADS_HERE),
            column(0),
            column(0),
            column(0),
            column(0),
        ],
        out_specs=(column(0), column(0), column(0)),
        out_shape=(out, out, out),
        compiler_params=big,
        name="backward",
    )(seg_row, seg_col, packed, packed, packed, *d_parts)
    grad, gram = local(
        gram_kernel,
        "gram",
        (array((C * FEAT, HALF), f32), array((3 * HD, HD), f32)),
        parts,
    )
    gram = gram.reshape(Z, -1, HD)
    gram = jnp.sum(lax.all_to_all(gram, "z", split_axis=0, concat_axis=0, tiled=True), axis=0)
    gram = gram + lax.ppermute(gram, "y", [(i, i ^ 1) for i in range(Y)])
    gram = gram + lax.ppermute(gram, "y", [(i, Y - 1 - i) for i in range(Y)])
    gram = jnp.broadcast_to(gram[None], (Z, *gram.shape))
    gram = lax.all_to_all(gram, "z", split_axis=0, concat_axis=0, tiled=True)
    gram, *grads = lax.optimization_barrier((gram, *grads))
    half = array((FEAT, HALF), f32)
    here, there = local(
        update_kernel,
        "update",
        (half, half),
        core_row,
        gram.reshape(3 * HD, HD),
        grad,
        scalars=1,
        scratch_shapes=[pltpu.VMEM((C, FEAT, HALF), f32)],
    )
    there = shift(there, "c", 1)
    update = local(
        join_kernel, "join", array((FEAT, 2 * HALF), f32), core_row, here, there, scalars=1
    )

    return (*grads, update)


def solution(mesh):
    fine = Mesh(mesh.devices.reshape(Z, Y, C, X), ("z", "y", "c", "x"))
    everything = ("z", "y", "c")
    both = P(everything, "x")
    rows = P(everything)
    return jax.shard_map(
        shards,
        mesh=fine,
        in_specs=(both, both, both, rows, rows, rows, both, both),
        out_specs=(both, both, both, both),
        check_vma=False,
    )
```

time: 555 us -> 185 us (0.33); the launches traced: 548 us -> 184 us
  waiting for transfers between devices: 326 us -> 76.8 us
  matrix products: 86.7 us -> 0.57 us
  local copies, waits for them, and re-layouts: 87 us -> 6.35 us
  Pallas kernels: 0 us -> 29.3 us
  starting transfers between devices: 26.4 us -> 54.4 us
  other arithmetic: 8.31 us -> 0.86 us
    reduce_scatter x1 -> x0, waiting for transfers between devices: 146 us -> none  [shards(): lax.psum_scatter(lax.dot_general(columns, attended, (((0,), (0,)), ((), (...]
    all_gather x3 -> x2, waiting for transfers between devices: 150 us -> 42.8 us  [the longest x1 33.3 us: shards(): cot_own = lax.all_gather(turned, 'x', axis=1, tiled=True)]
    dot_general x16 -> x1, matrix products: 84.9 us -> 0.57 us  [shards(): lax.dot_general(perm, cotangent, (((1,), (1,)), ((), ())), preferred_elem...]
    scatter x6 -> x0, local copies, waits for them, and re-layouts: 57.8 us -> none  [place(): return slots.at[send_to, send_rank].set(field)]
    pallas_call x0 -> x9, Pallas kernels: none -> 29.3 us  [the longest x7 16.3 us: local(): pl.pallas_call(kernel, in_specs=[smem] * scalars + [vmem] * (len(operands...]
    ppermute x0 -> x17, waiting for transfers between devices: none -> 25.7 us  [the longest x15 12.5 us: shift(): lax.ppermute(field, axis, [(i, (i + step) % size) for i in range(size)])]
    ppermute x0 -> x17, starting transfers between devices: none -> 23.5 us  [the longest x15 21.3 us: shift(): lax.ppermute(field, axis, [(i, (i + step) % size) for i in range(size)])]
    all_to_all x3 -> x4, waiting for transfers between devices: 28.5 us -> 8.27 us  [the longest x1 4.79 us: shards(): lax.all_to_all(gram, 'z', split_axis=0, concat_axis=0, tiled=True)]
  transfers between devices with their start and end apart: 7 -> 23, of which waited for: 6 -> 17; matrix products, arithmetic and copies ran while one was open for 11% -> 1% of each run, Pallas kernels for 0% -> 10%
where the time goes in v1:
time: 185 us; the launch traced here: 184 us
  waiting for transfers between devices  76.8 us (42%)
  starting transfers between devices  54.4 us (29%)
  Pallas kernels  29.3 us (16%)
  between operations  15.7 us (8%)
  local copies, waits for them, and re-layouts  6.35 us (3%)
    all_gather x1, waiting for transfers between devices, shards(): cot_own = lax.all_gather(turned, 'x', axis=1, tiled=True)  33.3 us
    ppermute x15, starting transfers between devices, shift(): lax.ppermute(field, axis, [(i, (i + step) % size) for i in range(size)])  21.3 us
    pallas_call x7, Pallas kernels, local(): pl.pallas_call(kernel, in_specs=[smem] * scalars + [vmem] * (len(operands...  16.3 us
    all_to_all x1, starting transfers between devices, shards(): lax.all_to_all(slots, everything, split_axis=0, concat_axis=0, tiled=True)  13.3 us
    ppermute x15, waiting for transfers between devices, shift(): lax.ppermute(field, axis, [(i, (i + step) % size) for i in range(size)])  12.5 us
    all_gather x1, waiting for transfers between devices, shards(): weight = lax.all_gather(out_weight, ('z', 'c'), axis=0, tiled=True)  9.53 us
    ppermute x1, waiting for transfers between devices, shards(): gram = gram + lax.ppermute(gram, 'y', [(i, i ^ 1) for i in range(Y)])  8.56 us
    pallas_call x1, Pallas kernels, shards(): pl.pallas_call(backward_kernel, grid=(HEADS_HERE,), in_specs=[pl.BlockSpe...  8 us
  transfers between devices with their start and end apart: 23, of which 17 were waited for; matrix products, arithmetic and copies ran while one was open for 1% of the time, Pallas kernels for 10%

profile of v1, /device:TPU:1, one launch (start us, length us, event | category | flops | bytes accessed | tf_op | source)
XLA Modules:
  0.0 183.9 jit_solution(8834824688708389570)
XLA Ops:
  8.0 5.0 %place.1 = bf16[64,112,128]{2,1,0:T(8,128)(2,1)} custom-call(s32[1,256]{1,0:T(1,128)} %bitcast.23, bf16[256,768]{1,0:T(8,128)(2,1)} %q_hbm.1, bf16[256,768]{1,0:T(8,128)(2,1)} %k_hbm.1, bf16[256,768]{1,0:T(8,128)(2,1)} %v_hbm.1), custom_call_target="tpu_custom_call" | custom-call | tf_op jit(solution)/shard_map/place/pallas_call | solution.py:280
  13.0 13.3 %all-to-all-start = ((bf16[64,112,128]{2,1,0:T(8,128)(2,1)}), bf16[64,112,128]{2,1,0:T(8,128)(2,1)}, u32[]{:S(2)}, u32[]{:S(2)}) async-start(bf16[64,112,128]{2,1,0:T(8,128)(2,1)} %place.1), calls=%async_computation | async-start | bytes 3670016 | tf_op jit(solution)/shard_map/all_to_all | solution.py:288
  27.4 1.5 collective-permute-start
  28.8 2.4 %collective-permute-start.1 = (bf16[192,256]{1,0:T(8,128)(2,1)S(1)}, bf16[192,256]{1,0:T(8,128)(2,1)S(1)}, u32[]{:S(2)}, u32[]{:S(2)}) collective-permute-start(bf16[192,256]{1,0:T(8,128)(2,1)S(1)} %get-tuple-element.54), channel_id=1, source_target_pairs={{0,16},{8,24},{16,0},{24,8},{1,17},{9,25},{17,1},{25,9},{2,18},{10... | collective-permute-start | bytes 294920 | tf_op jit(solution)/shard_map/ppermute | solution.py:251
  31.2 1.2 collective-permute-start.2
  32.4 3.2 %collective-permute-done = bf16[192,256]{1,0:T(8,128)(2,1)S(1)} collective-permute-done((bf16[192,256]{1,0:T(8,128)(2,1)S(1)}, bf16[192,256]{1,0:T(8,128)(2,1)S(1)}, u32[]{:S(2)}, u32[]{:S(2)}) %collective-permute-start) | collective-permute-done | bytes 98336 | tf_op jit(solution)/shard_map/ppermute | solution.py:251
  35.6 3.8 %collective-permute-done.1 = bf16[192,256]{1,0:T(8,128)(2,1)S(1)} collective-permute-done((bf16[192,256]{1,0:T(8,128)(2,1)S(1)}, bf16[192,256]{1,0:T(8,128)(2,1)S(1)}, u32[]{:S(2)}, u32[]{:S(2)}) %collective-permute-start.1) | collective-permute-done | bytes 98336 | tf_op jit(solution)/shard_map/ppermute | solution.py:251
  40.5 33.3 %all-gather.3.cloned.1.call-done.own_cot.cot_ref = bf16[4,768,256]{2,1,0:T(8,128)(2,1)} async-done(((bf16[4,192,256]{2,1,0:T(8,128)(2,1)}), bf16[4,768,256]{2,1,0:T(8,128)(2,1)}) %all-gather.3.cloned.1.call-update) | async-done | bytes 1572880 | tf_op jit(solution)/shard_map/all_gather | solution.py:300
  74.8 4.7 %forward.1 = (bf16[256,2304]{1,0:T(8,128)(2,1)S(1)}, bf16[256,384]{1,0:T(8,128)(2,1)S(1)}, bf16[256,384]{1,0:T(8,128)(2,1)S(1)}) custom-call(s32[1]{0:T(128)} %bitcast.5.core_ref, s32[1,256]{1,0:T(1,128)S(1)} %bitcast.19, s32[256,1]{1,0:T(8,128)S(1)} %copy.12.from_col, s32[1,256]{1,0:T(1,128)S(1)} %bitcast.16, s32[256,1]{1,0:T(8,128)S(1)} %copy.13.col_ref, ...), custom_call_target="tpu_custom_call" | custom-call | tf_op jit(solution)/shard_map/forward/pallas_call | solution.py:257
  79.7 1.2 collective-permute-start.4
  81.0 2.5 %collective-permute-start.7 = (bf16[256,384]{1,0:T(8,128)(2,1)S(1)}, bf16[256,384]{1,0:T(8,128)(2,1)S(1)}, u32[]{:S(2)}, u32[]{:S(2)}) collective-permute-start(bf16[256,384]{1,0:T(8,128)(2,1)S(1)} %collective-permute-done.6.swap), channel_id=1, source_target_pairs={{0,24},{8,0},{16,8},{24,16},{1,25},{9,1},{17,9},{25,17},{2,26},{10... | collective-permute-start | bytes 589832 | tf_op jit(solution)/shard_map/ppermute | solution.py:251
  84.9 2.0 %collective-permute-done.4.up = bf16[256,384]{1,0:T(8,128)(2,1)S(1)} collective-permute-done((bf16[256,384]{1,0:T(8,128)(2,1)S(1)}, bf16[256,384]{1,0:T(8,128)(2,1)S(1)}, u32[]{:S(2)}, u32[]{:S(2)}) %collective-permute-start.4) | collective-permute-done | bytes 196640 | tf_op jit(solution)/shard_map/ppermute | solution.py:251
  87.6 3.4 %collective-permute-start.8 = (bf16[256,384]{1,0:T(8,128)(2,1)S(1)}, bf16[256,384]{1,0:T(8,128)(2,1)S(1)}, u32[]{:S(2)}, u32[]{:S(2)}) collective-permute-start(bf16[256,384]{1,0:T(8,128)(2,1)S(1)} %collective-permute-done.7.swap_down), channel_id=1, source_target_pairs={{0,24},{8,0},{16,8},{24,16},{1,25},{9,1},{17,9},{25,17},{2,26},{10... | collective-permute-start | bytes 589832 | tf_op jit(solution)/shard_map/ppermute | solution.py:251
  91.9 2.8 %grad_near.1.near_ref = f32[768,384]{1,0:T(8,128)S(1)} custom-call(bf16[4,768,256]{2,1,0:T(8,128)(2,1)S(1)} %copy-done.1, bf16[4,768,256]{2,1,0:T(8,128)(2,1)} %collective-permute-done.3.other_cot, bf16[256,384]{1,0:T(8,128)(2,1)S(1)} %get-tuple-element.29.own, bf16[256,384]{1,0:T(8,128)(2,1)S(1)} %collective-permute-done.4.up, ...), custom_call_target="tpu_custom_call" | custom-call | tf_op jit(solution)/shard_map/grad_near/pallas_call | solution.py:257
  95.4 2.0 %grad_far.1 = bf16[8,96,384]{2,1,0:T(8,128)(2,1)S(1)} custom-call(bf16[4,768,256]{2,1,0:T(8,128)(2,1)S(1)} %copy-done.1, bf16[4,768,256]{2,1,0:T(8,128)(2,1)} %collective-permute-done.3.other_cot, bf16[256,384]{1,0:T(8,128)(2,1)S(1)} %collective-permute-done.5.own_far, bf16[256,384]{1,0:T(8,128)(2,1)S(1)} %collective-permute-done.8.swap_far, ...), custom_call_target="tpu_custom_call" | custom-call | tf_op jit(solution)/shard_map/grad_far/pallas_call | solution.py:257
  98.3 6.7 %all-to-all-start.1 = ((bf16[8,96,384]{2,1,0:T(8,128)(2,1)}), bf16[8,96,384]{2,1,0:T(8,128)(2,1)}, u32[]{:S(2)}, u32[]{:S(2)}) async-start(bf16[8,96,384]{2,1,0:T(8,128)(2,1)} %copy-done.2), calls=%async_computation.1 | async-start | bytes 1179648 | tf_op jit(solution)/shard_map/all_to_all | solution.py:356
  105.0 9.5 %all-gather.5.cloned.1.call-done.weight_ref = bf16[768,768]{1,0:T(8,128)(2,1)} async-done(((bf16[48,768]{1,0:T(8,128)(2,1)}), bf16[768,768]{1,0:T(8,128)(2,1)}) %all-gather.5.cloned.1.call-update) | async-done | bytes 1179664 | tf_op jit(solution)/shard_map/all_gather | solution.py:303
  114.5 1.3 copy-done.3
  115.8 1.4 d_parts.1
  120.2 2.8 %all-to-all-done.1.parts_ref = bf16[8,96,384]{2,1,0:T(8,128)(2,1)} async-done(((bf16[8,96,384]{2,1,0:T(8,128)(2,1)}), bf16[8,96,384]{2,1,0:T(8,128)(2,1)}, u32[]{:S(2)}, u32[]{:S(2)}) %all-to-all-start.1) | async-done | bytes 589856 | tf_op jit(solution)/shard_map/all_to_all | solution.py:356
  123.1 2.2 %gram.1 = (f32[96,384]{1,0:T(8,128)S(1)}, f32[384,128]{1,0:T(8,128)}) custom-call(bf16[8,96,384]{2,1,0:T(8,128)(2,1)} %all-to-all-done.1.parts_ref), custom_call_target="tpu_custom_call" | custom-call | tf_op jit(solution)/shard_map/gram/pallas_call | solution.py:257
  125.3 3.4 %all-to-all-start.2 = ((f32[8,48,128]{2,1,0:T(8,128)}), f32[8,48,128]{2,1,0:T(8,128)S(1)}, u32[]{:S(2)}, u32[]{:S(2)}) async-start(f32[8,48,128]{2,1,0:T(8,128)} %bitcast.10), calls=%async_computation.2 | async-start | bytes 393216 | tf_op jit(solution)/shard_map/all_to_all | solution.py:390
  128.7 3.6 %collective-permute-start.13 = (bf16[256,768]{1,0:T(8,128)(2,1)}, bf16[256,768]{1,0:T(8,128)(2,1)S(1)}, u32[]{:S(2)}, u32[]{:S(2)}) collective-permute-start(bf16[256,768]{1,0:T(8,128)(2,1)} %copy-done.10), channel_id=1, source_target_pairs={{0,24},{8,0},{16,8},{24,16},{1,25},{9,1},{17,9},{25,17},{2,26},{10... | collective-permute-start | bytes 1179656 | tf_op jit(solution)/shard_map/ppermute | solution.py:251
  132.2 4.8 %all-to-all-done.2 = f32[8,48,128]{2,1,0:T(8,128)S(1)} async-done(((f32[8,48,128]{2,1,0:T(8,128)}), f32[8,48,128]{2,1,0:T(8,128)S(1)}, u32[]{:S(2)}, u32[]{:S(2)}) %all-to-all-start.2) | async-done | bytes 196640 | tf_op jit(solution)/shard_map/all_to_all | solution.py:390
  137.1 1.2 collective-permute-start.11
  138.6 8.6 %collective-permute-done.11 = f32[48,128]{1,0:T(8,128)S(1)} collective-permute-done((f32[48,128]{1,0:T(8,128)S(1)}, f32[48,128]{1,0:T(8,128)S(1)}, u32[]{:S(2)}, u32[]{:S(2)}) %collective-permute-start.11) | collective-permute-done | bytes 24608 | tf_op jit(solution)/shard_map/ppermute | solution.py:391
  147.2 1.0 collective-permute-start.12
  148.2 4.6 %collective-permute-done.12 = f32[48,128]{1,0:T(8,128)S(1)} collective-permute-done((f32[48,128]{1,0:T(8,128)S(1)}, f32[48,128]{1,0:T(8,128)S(1)}, u32[]{:S(2)}, u32[]{:S(2)}) %collective-permute-start.12) | collective-permute-done | bytes 24608 | tf_op jit(solution)/shard_map/ppermute | solution.py:392
  153.5 7.4 %all-to-all-start.3 = ((f32[8,48,128]{2,1,0:T(8,128)}), f32[8,48,128]{2,1,0:T(8,128)S(1)}, u32[]{:S(2)}, u32[]{:S(2)}) async-start(f32[8,48,128]{2,1,0:T(8,128)} %broadcast_in_dim.27), calls=%async_computation.3 | async-start | bytes 393216 | tf_op jit(solution)/shard_map/all_to_all | solution.py:394
  160.9 8.0 %backward.1 = (bf16[256,768]{1,0:T(8,128)(2,1)}, bf16[256,768]{1,0:T(8,128)(2,1)}, bf16[256,768]{1,0:T(8,128)(2,1)}) custom-call(s32[1,256]{1,0:T(1,128)S(1)} %bitcast.17, s32[256,1]{1,0:T(8,128)S(1)} %copy.13.col_ref, bf16[256,2304]{1,0:T(8,128)(2,1)S(1)} %get-tuple-element.37.q_ref.k_ref.v_ref, bf16[256,2304]{1,0:T(8,128)(2,1)S(1)} %get-tuple-element.37.q_ref.k_ref.v_ref, ...), custom_call_target="tpu_custom_call" | custom-call | tf_op jit(solution)/shard_map/backward/pallas_call | solution.py:364
  169.6 2.5 %update.1 = (f32[48,384]{1,0:T(8,128)S(1)}, f32[48,384]{1,0:T(8,128)S(1)}) custom-call(s32[1]{0:T(128)} %bitcast.5.core_ref, f32[384,128]{1,0:T(8,128)S(1)} %bitcast.14, f32[96,384]{1,0:T(8,128)S(1)} %get-tuple-element.49.grad_ref), custom_call_target="tpu_custom_call" | custom-call | tf_op jit(solution)/shard_map/update/pallas_call | solution.py:257
  172.1 2.8 %collective-permute-start.16 = (f32[48,384]{1,0:T(8,128)S(1)}, f32[48,384]{1,0:T(8,128)S(1)}, u32[]{:S(2)}, u32[]{:S(2)}) collective-permute-start(f32[48,384]{1,0:T(8,128)S(1)} %get-tuple-element.51), channel_id=1, source_target_pairs={{0,4},{4,0},{1,5},{5,1},{2,6},{6,2},{3,7},{7,3},{8,12},{12,8},{9,1... | collective-permute-start | bytes 221192 | tf_op jit(solution)/shard_map/ppermute | solution.py:251
  (63 shorter events, 14.1 us)
Async XLA Ops:
  8.0 18.8 %copy-start = (bf16[256,768]{1,0:T(8,128)(2,1)S(1)}, bf16[256,768]{1,0:T(8,128)(2,1)}, u32[]{:S(2)}) copy-start(bf16[256,768]{1,0:T(8,128)(2,1)} %param.15) | copy-start | bytes 1179652
  13.0 61.7 %all-to-all-start = ((bf16[64,112,128]{2,1,0:T(8,128)(2,1)}), bf16[64,112,128]{2,1,0:T(8,128)(2,1)}, u32[]{:S(2)}, u32[]{:S(2)}) async-start(bf16[64,112,128]{2,1,0:T(8,128)(2,1)} %place.1), calls=%async_computation | async-start | bytes 3670016 | tf_op jit(solution)/shard_map/all_to_all | solution.py:288
  26.4 47.4 %all-gather.3.cloned.1.call-start = ((), (), s32[]{:S(2)}) async-start(), calls=%async_computation.4 | async-start | bytes 1966080 | tf_op jit(solution)/shard_map/all_gather | solution.py:300
  26.8 47.7 %copy-start.6 = (s32[256]{0:T(256)S(1)}, s32[256]{0:T(256)}, u32[]{:S(2)}) copy-start(s32[256]{0:T(256)} %param.13) | copy-start | bytes 3076
  26.8 47.9 %copy-start.7 = (s32[256]{0:T(256)S(1)}, s32[256]{0:T(256)}, u32[]{:S(2)}) copy-start(s32[256]{0:T(256)} %param.12) | copy-start | bytes 3076
  27.4 8.3 %collective-permute-start = (bf16[192,256]{1,0:T(8,128)(2,1)S(1)}, bf16[192,256]{1,0:T(8,128)(2,1)S(1)}, u32[]{:S(2)}, u32[]{:S(2)}) collective-permute-start(bf16[192,256]{1,0:T(8,128)(2,1)S(1)} %get-tuple-element.55), channel_id=1, source_target_pairs={{0,8},{8,16},{16,24},{24,0},{1,9},{9,17},{17,25},{25,1},{2,10},{10... | collective-permute-start | bytes 294920 | tf_op jit(solution)/shard_map/ppermute | solution.py:251
  28.8 10.6 %collective-permute-start.1 = (bf16[192,256]{1,0:T(8,128)(2,1)S(1)}, bf16[192,256]{1,0:T(8,128)(2,1)S(1)}, u32[]{:S(2)}, u32[]{:S(2)}) collective-permute-start(bf16[192,256]{1,0:T(8,128)(2,1)S(1)} %get-tuple-element.54), channel_id=1, source_target_pairs={{0,16},{8,24},{16,0},{24,8},{1,17},{9,25},{17,1},{25,9},{2,18},{10... | collective-permute-start | bytes 294920 | tf_op jit(solution)/shard_map/ppermute | solution.py:251
  31.2 8.4 %collective-permute-start.2 = (bf16[192,256]{1,0:T(8,128)(2,1)S(1)}, bf16[192,256]{1,0:T(8,128)(2,1)S(1)}, u32[]{:S(2)}, u32[]{:S(2)}) collective-permute-start(bf16[192,256]{1,0:T(8,128)(2,1)S(1)} %get-tuple-element.53), channel_id=1, source_target_pairs={{0,24},{8,0},{16,8},{24,16},{1,25},{9,1},{17,9},{25,17},{2,26},{10... | collective-permute-start | bytes 294920 | tf_op jit(solution)/shard_map/ppermute | solution.py:251
  40.4 74.1 %all-gather.5.cloned.1.call-start = ((), (), s32[]{:S(2)}) async-start(), calls=%async_computation.5 | async-start | bytes 1253376 | tf_op jit(solution)/shard_map/all_gather | solution.py:303
  73.8 18.1 %copy-start.1 = (bf16[4,768,256]{2,1,0:T(8,128)(2,1)S(1)}, bf16[4,768,256]{2,1,0:T(8,128)(2,1)}, u32[]{:S(2)}) copy-start(bf16[4,768,256]{2,1,0:T(8,128)(2,1)} %all-gather.3.cloned.1.call-done.own_cot.cot_ref) | copy-start | bytes 4718596
  73.8 18.1 %collective-permute-start.3 = (bf16[4,768,256]{2,1,0:T(8,128)(2,1)}, bf16[4,768,256]{2,1,0:T(8,128)(2,1)}, u32[]{:S(2)}, u32[]{:S(2)}) collective-permute-start(bf16[4,768,256]{2,1,0:T(8,128)(2,1)} %all-gather.3.cloned.1.call-done.own_cot.cot_ref), channel_id=1, source_target_pairs={{0,4},{4,0},{1,5},{5,1},{2,6},{6,2},{3,7},{7,3},{8,12},{12,8},{9,1... | collective-permute-start | bytes 4718600 | tf_op jit(solution)/shard_map/ppermute | solution.py:251
  79.5 1.5 collective-permute-start.6
  79.7 7.3 %collective-permute-start.4 = (bf16[256,384]{1,0:T(8,128)(2,1)S(1)}, bf16[256,384]{1,0:T(8,128)(2,1)S(1)}, u32[]{:S(2)}, u32[]{:S(2)}) collective-permute-start(bf16[256,384]{1,0:T(8,128)(2,1)S(1)} %get-tuple-element.29.own), channel_id=1, source_target_pairs={{0,8},{8,16},{16,24},{24,0},{1,9},{9,17},{17,25},{25,1},{2,10},{10... | collective-permute-start | bytes 589832 | tf_op jit(solution)/shard_map/ppermute | solution.py:251
  81.0 6.6 %collective-permute-start.7 = (bf16[256,384]{1,0:T(8,128)(2,1)S(1)}, bf16[256,384]{1,0:T(8,128)(2,1)S(1)}, u32[]{:S(2)}, u32[]{:S(2)}) collective-permute-start(bf16[256,384]{1,0:T(8,128)(2,1)S(1)} %collective-permute-done.6.swap), channel_id=1, source_target_pairs={{0,24},{8,0},{16,8},{24,16},{1,25},{9,1},{17,9},{25,17},{2,26},{10... | collective-permute-start | bytes 589832 | tf_op jit(solution)/shard_map/ppermute | solution.py:251
  83.5 8.4 %collective-permute-start.9 = (bf16[256,384]{1,0:T(8,128)(2,1)S(1)}, bf16[256,384]{1,0:T(8,128)(2,1)S(1)}, u32[]{:S(2)}, u32[]{:S(2)}) collective-permute-start(bf16[256,384]{1,0:T(8,128)(2,1)S(1)} %get-tuple-element.29.own), channel_id=1, source_target_pairs={{0,24},{8,0},{16,8},{24,16},{1,25},{9,1},{17,9},{25,17},{2,26},{10... | collective-permute-start | bytes 589832 | tf_op jit(solution)/shard_map/ppermute | solution.py:251
  84.0 7.8 %collective-permute-start.10 = (bf16[256,384]{1,0:T(8,128)(2,1)S(1)}, bf16[256,384]{1,0:T(8,128)(2,1)S(1)}, u32[]{:S(2)}, u32[]{:S(2)}) collective-permute-start(bf16[256,384]{1,0:T(8,128)(2,1)S(1)} %collective-permute-done.6.swap), channel_id=1, source_target_pairs={{0,8},{8,16},{16,24},{24,0},{1,9},{9,17},{17,25},{25,1},{2,10},{10... | collective-permute-start | bytes 589832 | tf_op jit(solution)/shard_map/ppermute | solution.py:251
  87.0 8.2 %collective-permute-start.5 = (bf16[256,384]{1,0:T(8,128)(2,1)S(1)}, bf16[256,384]{1,0:T(8,128)(2,1)S(1)}, u32[]{:S(2)}, u32[]{:S(2)}) collective-permute-start(bf16[256,384]{1,0:T(8,128)(2,1)S(1)} %collective-permute-done.4.up), channel_id=1, source_target_pairs={{0,8},{8,16},{16,24},{24,0},{1,9},{9,17},{17,25},{25,1},{2,10},{10... | collective-permute-start | bytes 589832 | tf_op jit(solution)/shard_map/ppermute | solution.py:251
  87.6 7.8 %collective-permute-start.8 = (bf16[256,384]{1,0:T(8,128)(2,1)S(1)}, bf16[256,384]{1,0:T(8,128)(2,1)S(1)}, u32[]{:S(2)}, u32[]{:S(2)}) collective-permute-start(bf16[256,384]{1,0:T(8,128)(2,1)S(1)} %collective-permute-done.7.swap_down), channel_id=1, source_target_pairs={{0,24},{8,0},{16,8},{24,16},{1,25},{9,1},{17,9},{25,17},{2,26},{10... | collective-permute-start | bytes 589832 | tf_op jit(solution)/shard_map/ppermute | solution.py:251
  97.5 0.8 copy-start.2
  98.3 24.8 %all-to-all-start.1 = ((bf16[8,96,384]{2,1,0:T(8,128)(2,1)}), bf16[8,96,384]{2,1,0:T(8,128)(2,1)}, u32[]{:S(2)}, u32[]{:S(2)}) async-start(bf16[8,96,384]{2,1,0:T(8,128)(2,1)} %copy-done.2), calls=%async_computation.1 | async-start | bytes 1179648 | tf_op jit(solution)/shard_map/all_to_all | solution.py:356
  114.5 1.3 copy-start.3
  117.2 0.7 copy-start.4
  118.0 0.8 copy-start.8
  123.1 37.9 %copy-start.5 = (bf16[256,768]{1,0:T(8,128)(2,1)S(1)}, bf16[256,768]{1,0:T(8,128)(2,1)}, u32[]{:S(2)}) copy-start(bf16[256,768]{1,0:T(8,128)(2,1)} %copy-done.4) | copy-start | bytes 1179652
  125.3 11.8 %all-to-all-start.2 = ((f32[8,48,128]{2,1,0:T(8,128)}), f32[8,48,128]{2,1,0:T(8,128)S(1)}, u32[]{:S(2)}, u32[]{:S(2)}) async-start(f32[8,48,128]{2,1,0:T(8,128)} %bitcast.10), calls=%async_computation.2 | async-start | bytes 393216 | tf_op jit(solution)/shard_map/all_to_all | solution.py:390
  128.7 32.3 %collective-permute-start.13 = (bf16[256,768]{1,0:T(8,128)(2,1)}, bf16[256,768]{1,0:T(8,128)(2,1)S(1)}, u32[]{:S(2)}, u32[]{:S(2)}) collective-permute-start(bf16[256,768]{1,0:T(8,128)(2,1)} %copy-done.10), channel_id=1, source_target_pairs={{0,24},{8,0},{16,8},{24,16},{1,25},{9,1},{17,9},{25,17},{2,26},{10... | collective-permute-start | bytes 1179656 | tf_op jit(solution)/shard_map/ppermute | solution.py:251
  132.2 28.7 %collective-permute-start.14 = (bf16[256,768]{1,0:T(8,128)(2,1)}, bf16[256,768]{1,0:T(8,128)(2,1)S(1)}, u32[]{:S(2)}, u32[]{:S(2)}) collective-permute-start(bf16[256,768]{1,0:T(8,128)(2,1)} %copy-done.9), channel_id=1, source_target_pairs={{0,16},{8,24},{16,0},{24,8},{1,17},{9,25},{17,1},{25,9},{2,18},{10... | collective-permute-start | bytes 1179656 | tf_op jit(solution)/shard_map/ppermute | solution.py:251
  137.1 10.1 %collective-permute-start.11 = (f32[48,128]{1,0:T(8,128)S(1)}, f32[48,128]{1,0:T(8,128)S(1)}, u32[]{:S(2)}, u32[]{:S(2)}) collective-permute-start(f32[48,128]{1,0:T(8,128)S(1)} %reduce_sum.9), channel_id=1, source_target_pairs={{0,8},{8,0},{16,24},{24,16},{1,9},{9,1},{17,25},{25,17},{2,10},{10... | collective-permute-start | bytes 73736 | tf_op jit(solution)/shard_map/ppermute | solution.py:391
  138.2 22.7 %collective-permute-start.15 = (bf16[256,768]{1,0:T(8,128)(2,1)}, bf16[256,768]{1,0:T(8,128)(2,1)}, u32[]{:S(2)}, u32[]{:S(2)}) collective-permute-start(bf16[256,768]{1,0:T(8,128)(2,1)} %copy-done.8), channel_id=1, source_target_pairs={{0,8},{8,16},{16,24},{24,0},{1,9},{9,17},{17,25},{25,1},{2,10},{10... | collective-permute-start | bytes 1179656 | tf_op jit(solution)/shard_map/ppermute | solution.py:251
  147.2 5.7 %collective-permute-start.12 = (f32[48,128]{1,0:T(8,128)S(1)}, f32[48,128]{1,0:T(8,128)S(1)}, u32[]{:S(2)}, u32[]{:S(2)}) collective-permute-start(f32[48,128]{1,0:T(8,128)S(1)} %add.29), channel_id=1, source_target_pairs={{0,24},{8,16},{16,8},{24,0},{1,25},{9,17},{17,9},{25,1},{2,26},{10... | collective-permute-start | bytes 73736 | tf_op jit(solution)/shard_map/ppermute | solution.py:392
  153.5 16.1 %all-to-all-start.3 = ((f32[8,48,128]{2,1,0:T(8,128)}), f32[8,48,128]{2,1,0:T(8,128)S(1)}, u32[]{:S(2)}, u32[]{:S(2)}) async-start(f32[8,48,128]{2,1,0:T(8,128)} %broadcast_in_dim.27), calls=%async_computation.3 | async-start | bytes 393216 | tf_op jit(solution)/shard_map/all_to_all | solution.py:394
  172.1 3.8 %collective-permute-start.16 = (f32[48,384]{1,0:T(8,128)S(1)}, f32[48,384]{1,0:T(8,128)S(1)}, u32[]{:S(2)}, u32[]{:S(2)}) collective-permute-start(f32[48,384]{1,0:T(8,128)S(1)} %get-tuple-element.51), channel_id=1, source_target_pairs={{0,4},{4,0},{1,5},{5,1},{2,6},{6,2},{3,7},{7,3},{8,12},{12,8},{9,1... | collective-permute-start | bytes 221192 | tf_op jit(solution)/shard_map/ppermute | solution.py:251
  (2 other events, 1.5 us)
Sparse Core Ops, SparseCore 0:
  40.5 33.1 all-gather.2
Sparse Core Ops, SparseCore 1:
  74.5 39.9 all-gather.4

commit v2 on v1

--- a/solution.py
+++ b/solution.py
@@ -51,7 +51,7 @@
     ]
 
 
-def place_kernel(label_ref, q_hbm, k_hbm, v_hbm, out_ref, q_ref, k_ref, v_ref, sems):
+def place_kernel(q_hbm, k_hbm, v_hbm, label_ref, out_ref, q_ref, k_ref, v_ref, sems):
     fields = (q_ref, k_ref, v_ref)
     copies = [
         pltpu.make_async_copy(source, target, sems.at[n])
@@ -91,6 +91,14 @@
             out_ref[:, t * TILE : (t + 1) * TILE, :] = rows.astype(bf16).reshape(GROUPS, TILE, HD)
 
 
+def join_cot_kernel(x_ref, *refs):
+    *pieces, out_ref = refs
+    for n, piece in enumerate(pieces):
+        at = lax.rem(x_ref[0] + X - n % X, X) * (4 * FEAT)
+        pair = n // X * 2
+        out_ref[pair : pair + 2, pl.ds(pl.multiple_of(at, 4 * FEAT), 4 * FEAT), :] = piece[...]
+
+
 def parts_kernel(cot_ref, weight_ref, *out_refs):
     weight = weight_ref[...]
     for k, out_ref in enumerate(out_refs):
@@ -110,23 +118,43 @@
 
 
 def forward_kernel(
-    core_ref, from_row, from_col, row_ref, col_ref, slots_ref, packed_ref, own_ref, other_ref
+    core_ref,
+    slots_hbm,
+    from_row,
+    from_col,
+    row_ref,
+    col_ref,
+    packed_ref,
+    own_ref,
+    other_ref,
+    slots_ref,
+    sems,
 ):
+    copies = []
+    for t in range(TILES):
+        rows = pl.ds(t * TILE, TILE)
+        copies.append(pltpu.make_async_copy(slots_hbm.at[:, rows, :], slots_ref.at[t], sems.at[t]))
+    for first in range(3):
+        for copy in copies[first::3]:
+            copy.start()
+
     before = jnp.sum(jnp.where(from_row[...] < from_col[...], 1, 0), axis=1, keepdims=True)
     code = 8 * from_col[...] + lax.broadcasted_iota(jnp.int32, (ROWS, 1), 0) - before
     lane = lax.broadcasted_iota(jnp.int32, (1, FLAT), 1)
     group = lane // TILE
     total = {}
+    landed = set()
     for tile, block in PATTERNS:
+        if tile not in landed:
+            for copy in copies[tile::3]:
+                copy.wait()
+            landed.add(tile)
         slot = lane - TILE * group + (TILE * tile - SLOTS * block)
         wanted = jnp.where((slot >= 0) & (slot < SLOTS), 8 * group + slot, -1)
         hot = jnp.where(code == wanted, 1.0, 0.0).astype(bf16)
         users = pattern_users(tile, block)
         wide = jnp.concatenate(
-            [
-                slots_ref[:, t * TILE : (t + 1) * TILE, :].reshape(FLAT, HD)
-                for t, _ in users
-            ],
+            [slots_ref[t].reshape(FLAT, HD) for t, _ in users],
             axis=1,
         )
         got = jnp.dot(hot, wide, preferred_element_type=f32)
@@ -155,25 +183,17 @@
             ).astype(bf16)
 
 
-def grad_near_kernel(own_cot, other_cot, own, up, down, swap, swap_up, swap_down, out_ref):
-    terms = (
-        (own_cot, 0, own),
-        (own_cot, 1, up),
-        (own_cot, 3, down),
-        (other_cot, 0, swap),
-        (other_cot, 1, swap_up),
-        (other_cot, 3, swap_down),
-    )
+def grad_near_kernel(*refs):
     total = None
-    for cot, k, field in terms:
-        product = jnp.dot(cot[k], field[...], preferred_element_type=f32)
+    for left, right in zip(refs[:6], refs[6:12]):
+        product = jnp.dot(left[...], right[...], preferred_element_type=f32)
         total = product if total is None else total + product
-    out_ref[...] = total
+    refs[12][...] = total
 
 
 def grad_far_kernel(own_cot, other_cot, own_far, swap_far, near_ref, out_ref):
-    total = near_ref[...] + jnp.dot(own_cot[2], own_far[...], preferred_element_type=f32)
-    total = total + jnp.dot(other_cot[2], swap_far[...], preferred_element_type=f32)
+    total = near_ref[...] + jnp.dot(own_cot[...], own_far[...], preferred_element_type=f32)
+    total = total + jnp.dot(other_cot[...], swap_far[...], preferred_element_type=f32)
     out_ref[...] = total.astype(bf16).reshape(out_ref.shape)
 
 
@@ -229,7 +249,8 @@
     out_ref[:, pl.ds(pl.multiple_of((1 - core) * HALF, HD), HALF)] = there_ref[...]
 
 
-def backward_kernel(row_ref, col_ref, q_ref, k_ref, v_ref, d0, d1, d2, d3, gq_ref, gk_ref, gv_ref):
+def backward_kernel(row_ref, col_ref, q_ref, k_ref, v_ref, d0, d1, d2, d3, *refs):
+    gq_ref, gk_ref, gv_ref = refs[-3:]
     same = row_ref[...] == col_ref[...]
     q, k, v = q_ref[...], k_ref[...], v_ref[...]
     near = d0[...].astype(f32) + d1[...].astype(f32)
@@ -251,14 +272,20 @@
     return lax.ppermute(field, axis, [(i, (i + step) % size) for i in range(size)])
 
 
-def local(kernel, name, out_shape, *operands, scalars=0, **options):
+def cross(field, step):
+    pairs = [(y * C + c, (y + step) % Y * C + 1 - c) for y in range(Y) for c in range(C)]
+    return lax.ppermute(field, ("y", "c"), pairs)
+
+
+def local(kernel, name, out_shape, *operands, scalars=0, far=0, room=24, **options):
     smem = pl.BlockSpec(memory_space=pltpu.SMEM)
     vmem = pl.BlockSpec(memory_space=pltpu.VMEM)
+    hbm = pl.BlockSpec(memory_space=pltpu.HBM)
     return pl.pallas_call(
         kernel,
-        in_specs=[smem] * scalars + [vmem] * (len(operands) - scalars),
+        in_specs=[smem] * scalars + [hbm] * far + [vmem] * (len(operands) - scalars - far),
         out_shape=out_shape,
-        compiler_params=pltpu.CompilerParams(vmem_limit_bytes=48 * 1024 * 1024),
+        compiler_params=pltpu.CompilerParams(vmem_limit_bytes=room * 1024 * 1024),
         name=name,
         **options,
     )(*operands)
@@ -271,20 +298,21 @@
 def shards(query, key, value, send_to, recv_from, segment, out_weight, cotangent):
     core = lax.axis_index("c")
     core_row = core.astype(jnp.int32).reshape(1)
-    big = pltpu.CompilerParams(vmem_limit_bytes=48 * 1024 * 1024)
     everything = ("z", "y", "c")
 
-    vmem = pl.BlockSpec(memory_space=pltpu.VMEM)
-    hbm = pl.BlockSpec(memory_space=pltpu.HBM)
     field = pltpu.VMEM((ROWS, HEADS_HERE * HD), bf16)
-    slots = pl.pallas_call(
+    slots = local(
         place_kernel,
-        in_specs=[vmem, hbm, hbm, hbm],
-        out_shape=array((GROUPS, TILES * TILE, HD), bf16),
+        "place",
+        array((GROUPS, TILES * TILE, HD), bf16),
+        query,
+        key,
+        value,
+        send_to[None, :],
+        far=3,
+        room=60,
         scratch_shapes=[field, field, field, pltpu.SemaphoreType.DMA((3,))],
-        compiler_params=pltpu.CompilerParams(vmem_limit_bytes=60 * 1024 * 1024),
-        name="place",
-    )(send_to[None, :], query, key, value)
+    )
     arrived = lax.all_to_all(slots, everything, split_axis=0, concat_axis=0, tiled=True)
 
     cotangent, slots = lax.optimization_barrier((cotangent, slots))
@@ -296,13 +324,36 @@
         perm, cotangent, (((1,), (1,)), ((), ())), preferred_element_type=f32
     ).astype(bf16)
     turned = turned.reshape(Y, 4 * FEAT, ROWS)
-    turned = jnp.stack([turned[0]] + [shift(turned[k], "y", k) for k in range(1, Y)])
-    cot_own = lax.all_gather(turned, "x", axis=1, tiled=True)
+    turned = [turned[0]] + [shift(turned[k], "y", k) for k in range(1, Y)]
+    one, two = jnp.stack(turned[:2]), jnp.stack(turned[2:])
+    one_up, two_down = shift(one, "x", 1), shift(two, "x", -1)
+    two_up, one_down = shift(two, "x", 1), shift(one, "x", -1)
+    one_far, two_far = shift(one_up, "x", 1), shift(two_down, "x", -1)
+    cot_own = local(
+        join_cot_kernel,
+        "join_cot",
+        array((Y, X * 4 * FEAT, ROWS), bf16),
+        lax.axis_index("x").astype(jnp.int32).reshape(1),
+        one,
+        one_up,
+        one_far,
+        one_down,
+        two,
+        two_up,
+        two_far,
+        two_down,
+        scalars=1,
+        room=60,
+    )
     cot_other = shift(cot_own, "c", 1)
 
     weight = lax.all_gather(out_weight, ("z", "c"), axis=0, tiled=True)
     part = array((ROWS, HEADS_HERE * HD), bf16)
-    d_parts = local(parts_kernel, "d_parts", (part,) * Y, cot_own, weight)
+    work = pl.CostEstimate(flops=18 * 10**9, bytes_accessed=54 * 10**6, transcendentals=0)
+    d_parts = local(parts_kernel, "d_parts", (part,) * Y, cot_own, weight, room=60, cost_estimate=work)
+    arrived, cot_own, cot_other, *d_parts = lax.optimization_barrier(
+        (arrived, cot_own, cot_other, *d_parts)
+    )
 
     seg_row = segment[None, :]
     seg_col = segment[:, None]
@@ -315,27 +366,32 @@
             array((ROWS, HALF), bf16),
         ),
         core_row,
+        arrived,
         recv_from[None, :],
         recv_from[:, None],
         seg_row,
         seg_col,
-        arrived,
         scalars=1,
+        far=1,
+        scratch_shapes=[
+            pltpu.VMEM((TILES, GROUPS, TILE, HD), bf16),
+            pltpu.SemaphoreType.DMA((TILES,)),
+        ],
     )
 
     own_up = shift(own, "y", 1)
     own_down = shift(own, "y", -1)
     swap = shift(other, "c", 1)
-    swap_up = shift(swap, "y", 1)
-    swap_down = shift(swap, "y", -1)
+    swap_up = cross(other, 1)
+    swap_down = cross(other, -1)
     own_far = shift(own_up, "y", 1)
     swap_far = shift(swap_down, "y", -1)
     grad = local(
         grad_near_kernel,
         "grad_near",
         array((Z * C * FEAT, HALF), f32),
-        cot_own,
-        cot_other,
+        *[cot_own[k] for k in (0, 1, 3)],
+        *[cot_other[k] for k in (0, 1, 3)],
         own,
         own_up,
         own_down,
@@ -347,39 +403,43 @@
         grad_far_kernel,
         "grad_far",
         array((Z, C * FEAT, HALF), bf16),
-        cot_own,
-        cot_other,
+        cot_own[2],
+        cot_other[2],
         own_far,
         swap_far,
         grad,
     )
+    grad, *d_parts = lax.optimization_barrier((grad, *d_parts))
+    d_parts = [d_parts[0]] + [shift(d_parts[k], "y", -k) for k in range(1, Y)]
     parts = lax.all_to_all(grad, "z", split_axis=0, concat_axis=0, tiled=True)
-    parts, *d_parts = lax.optimization_barrier((parts, *d_parts))
-    d_parts = [d_parts[0]] + [shift(d_parts[k], "y", -k) for k in range(1, Y)]
-
-    def column(base):
-        return pl.BlockSpec((ROWS, HD), lambda h, base=base: (0, base + h))
-
-    out = jax.ShapeDtypeStruct((ROWS, HEADS_HERE * HD), bf16)
-    grads = pl.pallas_call(
-        backward_kernel,
-        grid=(HEADS_HERE,),
-        in_specs=[
-            pl.BlockSpec((1, ROWS), lambda h: (0, 0)),
-            pl.BlockSpec((ROWS, 1), lambda h: (0, 0)),
-            column(0),
-            column(HEADS_HERE),
-            column(2 * HEADS_HERE),
-            column(0),
-            column(0),
-            column(0),
-            column(0),
-        ],
-        out_specs=(column(0), column(0), column(0)),
-        out_shape=(out, out, out),
-        compiler_params=big,
-        name="backward",
-    )(seg_row, seg_col, packed, packed, packed, *d_parts)
+
+    out = array((ROWS, HEADS_HERE * HD), bf16)
+
+    def backward(heads, held):
+        def column(base):
+            return pl.BlockSpec((ROWS, HD), lambda h: (0, base + heads + h))
+
+        return pl.pallas_call(
+            backward_kernel,
+            grid=(3,),
+            in_specs=[
+                pl.BlockSpec((1, ROWS), lambda h: (0, 0)),
+                pl.BlockSpec((ROWS, 1), lambda h: (0, 0)),
+                column(0),
+                column(HEADS_HERE),
+                column(2 * HEADS_HERE),
+                *[column(0)] * Y,
+                *[pl.BlockSpec(memory_space=pl.ANY)] * len(held),
+            ],
+            out_specs=(column(0),) * 3,
+            out_shape=(out,) * 3,
+            input_output_aliases={5 + Y + n: n for n in range(len(held))},
+            compiler_params=pltpu.CompilerParams(vmem_limit_bytes=24 * 1024 * 1024),
+            name="backward",
+        )(seg_row, seg_col, packed, packed, packed, *d_parts, *held)
+
+    grads = backward(0, ())
+
     grad, gram = local(
         gram_kernel,
         "gram",
@@ -388,10 +448,11 @@
     )
     gram = gram.reshape(Z, -1, HD)
     gram = jnp.sum(lax.all_to_all(gram, "z", split_axis=0, concat_axis=0, tiled=True), axis=0)
-    gram = gram + lax.ppermute(gram, "y", [(i, i ^ 1) for i in range(Y)])
-    gram = gram + lax.ppermute(gram, "y", [(i, Y - 1 - i) for i in range(Y)])
+    gram, *grads = lax.optimization_barrier((gram, *grads))
+    gram = sum([shift(gram, "y", k) for k in range(1, Y)], gram)
     gram = jnp.broadcast_to(gram[None], (Z, *gram.shape))
     gram = lax.all_to_all(gram, "z", split_axis=0, concat_axis=0, tiled=True)
+    grads = backward(3, grads)
     gram, *grads = lax.optimization_barrier((gram, *grads))
     half = array((FEAT, HALF), f32)
     here, there = local(

time: 185 us -> 172 us (0.930)
  waiting for transfers between devices: 76.8 us -> 62.3 us
  Pallas kernels: 29.3 us -> 31.2 us
    all_gather x1 -> x0, waiting for transfers between devices: 33.3 us -> none  [shards(): cot_own = lax.all_gather(turned, 'x', axis=1, tiled=True)]
    all_to_all x1, waiting for transfers between devices: 2.84 us -> 16.7 us  [shards(): parts = lax.all_to_all(grad, 'z', split_axis=0, concat_axis=0, tiled=True)]
    all_to_all x1, waiting for transfers between devices: 0.01 us -> 10.2 us  [shards(): lax.all_to_all(slots, everything, split_axis=0, concat_axis=0, tiled=True)]
    ppermute x15 -> x22, waiting for transfers between devices: 12.5 us -> 22.4 us  [shift(): lax.ppermute(field, axis, [(i, (i + step) % size) for i in range(size)])]
    ppermute x2, waiting for transfers between devices: 13.2 us -> 3.53 us  [cross(): return lax.ppermute(field, ('y', 'c'), pairs)]
    all_gather x1, waiting for transfers between devices: 9.53 us -> 0.01 us  [shards(): weight = lax.all_gather(out_weight, ('z', 'c'), axis=0, tiled=True)]
    ppermute x15 -> x22, starting transfers between devices: 21.3 us -> 28.7 us  [shift(): lax.ppermute(field, axis, [(i, (i + step) % size) for i in range(size)])]
    all_to_all x1, starting transfers between devices: 7.38 us -> 3.39 us  [shards(): gram = lax.all_to_all(gram, 'z', split_axis=0, concat_axis=0, tiled=True)]
  transfers between devices with their start and end apart: 23 -> 29, of which waited for: 17 -> 17; matrix products, arithmetic and copies ran while one was open for 1% -> 2% of each run, Pallas kernels for 10% -> 13%
where the time goes in v2:
time: 172 us
  waiting for transfers between devices  62.3 us (36%)
  starting transfers between devices  56.2 us (33%)
  Pallas kernels  31.2 us (18%)
  between operations  14.3 us (8%)
  local copies, waits for them, and re-layouts  6.85 us (4%)
    ppermute x22, starting transfers between devices, shift(): lax.ppermute(field, axis, [(i, (i + step) % size) for i in range(size)])  28.7 us
    ppermute x22, waiting for transfers between devices, shift(): lax.ppermute(field, axis, [(i, (i + step) % size) for i in range(size)])  22.4 us
    pallas_call x9, Pallas kernels, local(): pl.pallas_call(kernel, in_specs=[smem] * scalars + [hbm] * far + [vmem] *...  21.8 us
    all_to_all x1, waiting for transfers between devices, shards(): parts = lax.all_to_all(grad, 'z', split_axis=0, concat_axis=0, tiled=True)  16.7 us
    all_to_all x1, starting transfers between devices, shards(): lax.all_to_all(slots, everything, split_axis=0, concat_axis=0, tiled=True)  13.2 us
    all_to_all x1, waiting for transfers between devices, shards(): lax.all_to_all(slots, everything, split_axis=0, concat_axis=0, tiled=True)  10.2 us
    pallas_call x2, Pallas kernels, backward(): pl.pallas_call(backward_kernel, grid=(3,), in_specs=[pl.BlockSpec((1, ROW...  9.39 us
    all_to_all x1, waiting for transfers between devices, shards(): lax.all_to_all(gram, 'z', split_axis=0, concat_axis=0, tiled=True)  4.87 us
  transfers between devices with their start and end apart: 29, of which 17 were waited for; matrix products, arithmetic and copies ran while one was open for 2% of the time, Pallas kernels for 13%

profile of v2, /device:TPU:1, one launch (start us, length us, event | category | flops | bytes accessed | tf_op | source)
XLA Modules:
  0.0 171.5 jit_solution(17979852014335647116)
XLA Ops:
  7.9 5.0 %place.1 = bf16[64,112,128]{2,1,0:T(8,128)(2,1)} custom-call(bf16[256,768]{1,0:T(8,128)(2,1)} %q_hbm.1, bf16[256,768]{1,0:T(8,128)(2,1)} %k_hbm.1, bf16[256,768]{1,0:T(8,128)(2,1)} %v_hbm.1, s32[1,256]{1,0:T(1,128)} %bitcast.42), custom_call_target="tpu_custom_call" | custom-call | tf_op jit(solution)/shard_map/place/pallas_call | solution.py:284
  12.9 13.2 %all-to-all-start = ((bf16[64,112,128]{2,1,0:T(8,128)(2,1)}), bf16[64,112,128]{2,1,0:T(8,128)(2,1)S(1)}, u32[]{:S(2)}, u32[]{:S(2)}) async-start(bf16[64,112,128]{2,1,0:T(8,128)(2,1)} %place.1), calls=%async_computation | async-start | bytes 3670016 | tf_op jit(solution)/shard_map/all_to_all | solution.py:316
  27.1 3.0 %collective-permute-start.4 = (bf16[192,256]{1,0:T(8,128)(2,1)S(1)}, bf16[192,256]{1,0:T(8,128)(2,1)S(1)}, u32[]{:S(2)}, u32[]{:S(2)}) collective-permute-start(bf16[192,256]{1,0:T(8,128)(2,1)S(1)} %get-tuple-element.88), channel_id=1, source_target_pairs={{0,16},{8,24},{16,0},{24,8},{1,17},{9,25},{17,1},{25,9},{2,18},{10... | collective-permute-start | bytes 294920 | tf_op jit(solution)/shard_map/ppermute | solution.py:272
  31.5 4.2 %collective-permute-done.4 = bf16[192,256]{1,0:T(8,128)(2,1)S(1)} collective-permute-done((bf16[192,256]{1,0:T(8,128)(2,1)S(1)}, bf16[192,256]{1,0:T(8,128)(2,1)S(1)}, u32[]{:S(2)}, u32[]{:S(2)}) %collective-permute-start.4) | collective-permute-done | bytes 98336 | tf_op jit(solution)/shard_map/ppermute | solution.py:272
  35.7 3.3 %collective-permute-done.5 = bf16[192,256]{1,0:T(8,128)(2,1)S(1)} collective-permute-done((bf16[192,256]{1,0:T(8,128)(2,1)S(1)}, bf16[192,256]{1,0:T(8,128)(2,1)S(1)}, u32[]{:S(2)}, u32[]{:S(2)}) %collective-permute-start.5) | collective-permute-done | bytes 98336 | tf_op jit(solution)/shard_map/ppermute | solution.py:272
  39.0 2.6 %collective-permute-start.7 = (bf16[2,192,256]{2,1,0:T(8,128)(2,1)S(1)}, bf16[2,192,256]{2,1,0:T(8,128)(2,1)S(1)}, u32[]{:S(2)}, u32[]{:S(2)}) collective-permute-start(bf16[2,192,256]{2,1,0:T(8,128)(2,1)S(1)} %pad_maximum_fusion.1.refs_4_), channel_id=1, source_target_pairs={{0,3},{1,0},{2,1},{3,2},{4,7},{5,4},{6,5},{7,6},{8,11},{9,8},{10,9... | collective-permute-start | bytes 589832 | tf_op jit(solution)/shard_map/ppermute | solution.py:272
  42.1 2.3 %collective-permute-start.3 = (bf16[2,192,256]{2,1,0:T(8,128)(2,1)S(1)}, bf16[2,192,256]{2,1,0:T(8,128)(2,1)}, u32[]{:S(2)}, u32[]{:S(2)}) collective-permute-start(bf16[2,192,256]{2,1,0:T(8,128)(2,1)S(1)} %pad_maximum_fusion.refs_0_), channel_id=1, source_target_pairs={{0,3},{1,0},{2,1},{3,2},{4,7},{5,4},{6,5},{7,6},{8,11},{9,8},{10,9... | collective-permute-start | bytes 589832 | tf_op jit(solution)/shard_map/ppermute | solution.py:272
  45.3 3.4 %collective-permute-start.8 = (bf16[2,192,256]{2,1,0:T(8,128)(2,1)S(1)}, bf16[2,192,256]{2,1,0:T(8,128)(2,1)}, u32[]{:S(2)}, u32[]{:S(2)}) collective-permute-start(bf16[2,192,256]{2,1,0:T(8,128)(2,1)S(1)} %collective-permute-done.7.refs_7_), channel_id=1, source_target_pairs={{0,3},{1,0},{2,1},{3,2},{4,7},{5,4},{6,5},{7,6},{8,11},{9,8},{10,9... | collective-permute-start | bytes 589832 | tf_op jit(solution)/shard_map/ppermute | solution.py:272
  49.7 3.0 %collective-permute-done.6.refs_5_ = bf16[2,192,256]{2,1,0:T(8,128)(2,1)S(1)} collective-permute-done((bf16[2,192,256]{2,1,0:T(8,128)(2,1)S(1)}, bf16[2,192,256]{2,1,0:T(8,128)(2,1)S(1)}, u32[]{:S(2)}, u32[]{:S(2)}) %collective-permute-start.6) | collective-permute-done | bytes 196640 | tf_op jit(solution)/shard_map/ppermute | solution.py:272
  53.5 2.9 %collective-permute-done.2.refs_2_ = bf16[2,192,256]{2,1,0:T(8,128)(2,1)} collective-permute-done((bf16[2,192,256]{2,1,0:T(8,128)(2,1)S(1)}, bf16[2,192,256]{2,1,0:T(8,128)(2,1)}, u32[]{:S(2)}, u32[]{:S(2)}) %collective-permute-start.2) | collective-permute-done | bytes 196640 | tf_op jit(solution)/shard_map/ppermute | solution.py:272
  56.4 2.7 %join_cot.1.cot_ref = bf16[4,768,256]{2,1,0:T(8,128)(2,1)} custom-call(s32[1]{0:T(128)} %bitcast.1.x_ref, bf16[2,192,256]{2,1,0:T(8,128)(2,1)} %copy-done.10, bf16[2,192,256]{2,1,0:T(8,128)(2,1)} %copy-done.12, bf16[2,192,256]{2,1,0:T(8,128)(2,1)} %collective-permute-done.2.refs_2_, bf16[2,192,256]{2,1,0:T(8,128)(2,1)} %collective-permute-done.3.refs_3_, ...), custom_call_target="tpu_custom_call" | custom-call | tf_op jit(solution)/shard_map/join_cot/pallas_call | solution.py:284
  59.1 2.3 %collective-permute-start.9 = (bf16[4,768,256]{2,1,0:T(8,128)(2,1)}, bf16[4,768,256]{2,1,0:T(8,128)(2,1)}, u32[]{:S(2)}, u32[]{:S(2)}) collective-permute-start(bf16[4,768,256]{2,1,0:T(8,128)(2,1)} %join_cot.1.cot_ref), channel_id=1, source_target_pairs={{0,4},{4,0},{1,5},{5,1},{2,6},{6,2},{3,7},{7,3},{8,12},{12,8},{9,1... | collective-permute-start | bytes 4718600 | tf_op jit(solution)/shard_map/ppermute | solution.py:272
  61.5 3.9 %d_parts.1 = (bf16[256,768]{1,0:T(8,128)(2,1)}, bf16[256,768]{1,0:T(8,128)(2,1)}, bf16[256,768]{1,0:T(8,128)(2,1)}, bf16[256,768]{1,0:T(8,128)(2,1)}) custom-call(bf16[4,768,256]{2,1,0:T(8,128)(2,1)} %join_cot.1.cot_ref, bf16[768,768]{1,0:T(8,128)(2,1)} %all-gather.2.cloned.1.call-done.weight_ref), custom_call_target="tpu_custom_call" | custom-call | flops 17999998976 | bytes 54000000 | tf_op jit(solution)/shard_map/d_parts/pallas_call | solution.py:284
  65.4 10.2 %all-to-all-done.slots_hbm = bf16[64,112,128]{2,1,0:T(8,128)(2,1)S(1)} async-done(((bf16[64,112,128]{2,1,0:T(8,128)(2,1)}), bf16[64,112,128]{2,1,0:T(8,128)(2,1)S(1)}, u32[]{:S(2)}, u32[]{:S(2)}) %all-to-all-start) | async-done | bytes 1835040 | tf_op jit(solution)/shard_map/all_to_all | solution.py:316
  76.5 3.8 %forward.1 = (bf16[256,2304]{1,0:T(8,128)(2,1)S(1)}, bf16[256,384]{1,0:T(8,128)(2,1)S(1)}, bf16[256,384]{1,0:T(8,128)(2,1)S(1)}) custom-call(s32[1]{0:T(128)} %bitcast.8.core_ref, bf16[64,112,128]{2,1,0:T(8,128)(2,1)S(1)} %all-to-all-done.slots_hbm, s32[1,256]{1,0:T(1,128)S(1)} %bitcast.38, s32[256,1]{1,0:T(8,128)S(1)} %copy-done.2, s32[1,256]{1,0:T(1,128)S(1)} %bitcast.34, ...), custom_call_target="tpu_custom_call" | custom-call | tf_op jit(solution)/shard_map/forward/pallas_call | solution.py:284
  81.5 3.2 %collective-permute-start.12 = (bf16[256,384]{1,0:T(8,128)(2,1)S(1)}, bf16[256,384]{1,0:T(8,128)(2,1)S(1)}, u32[]{:S(2)}, u32[]{:S(2)}) collective-permute-start(bf16[256,384]{1,0:T(8,128)(2,1)S(1)} %get-tuple-element.51), channel_id=1, source_target_pairs={{0,28},{4,24},{8,4},{12,0},{16,12},{20,8},{24,20},{28,16},{1,29},{... | collective-permute-start | bytes 589832 | tf_op jit(solution)/shard_map/ppermute | solution.py:277
  86.6 3.5 %collective-permute-done.12.refs_11_ = bf16[256,384]{1,0:T(8,128)(2,1)S(1)} collective-permute-done((bf16[256,384]{1,0:T(8,128)(2,1)S(1)}, bf16[256,384]{1,0:T(8,128)(2,1)S(1)}, u32[]{:S(2)}, u32[]{:S(2)}) %collective-permute-start.12) | collective-permute-done | bytes 196640 | tf_op jit(solution)/shard_map/ppermute | solution.py:277
  90.7 1.8 %slice_bitcast_fusion = (bf16[768,256]{1,0:T(8,128)(2,1)S(1)}, bf16[768,256]{1,0:T(8,128)(2,1)S(1)}, bf16[768,256]{1,0:T(8,128)(2,1)S(1)}, bf16[768,256]{1,0:T(8...) fusion(bf16[4,768,256]{2,1,0:T(8,128)(2,1)} %collective-permute, ...), kind=kLoop, calls=%fused_computation.4 | loop fusion | bytes 6291456 | tf_op jit(solution)/shard_map/squeeze | solution.py:394
  92.4 1.9 %collective-permute-done.14.refs_8_ = bf16[256,384]{1,0:T(8,128)(2,1)S(1)} collective-permute-done((bf16[256,384]{1,0:T(8,128)(2,1)S(1)}, bf16[256,384]{1,0:T(8,128)(2,1)S(1)}, u32[]{:S(2)}, u32[]{:S(2)}) %collective-permute-start.14) | collective-permute-done | bytes 196640 | tf_op jit(solution)/shard_map/ppermute | solution.py:272
  95.7 2.8 %collective-permute-done.11.own_far = bf16[256,384]{1,0:T(8,128)(2,1)S(1)} collective-permute-done((bf16[256,384]{1,0:T(8,128)(2,1)S(1)}, bf16[256,384]{1,0:T(8,128)(2,1)S(1)}, u32[]{:S(2)}, u32[]{:S(2)}) %collective-permute-start.11) | collective-permute-done | bytes 196640 | tf_op jit(solution)/shard_map/ppermute | solution.py:272
  100.0 3.7 %all-to-all-start.1 = ((bf16[8,96,384]{2,1,0:T(8,128)(2,1)}), bf16[8,96,384]{2,1,0:T(8,128)(2,1)S(1)}, u32[]{:S(2)}, u32[]{:S(2)}) async-start(bf16[8,96,384]{2,1,0:T(8,128)(2,1)} %grad_far.1), calls=%async_computation.1 | async-start | bytes 1179648 | tf_op jit(solution)/shard_map/all_to_all | solution.py:414
  104.7 1.5 collective-permute-start.18
  106.2 16.7 %all-to-all-done.1.parts_ref = bf16[8,96,384]{2,1,0:T(8,128)(2,1)S(1)} async-done(((bf16[8,96,384]{2,1,0:T(8,128)(2,1)}), bf16[8,96,384]{2,1,0:T(8,128)(2,1)S(1)}, u32[]{:S(2)}, u32[]{:S(2)}) %all-to-all-start.1) | async-done | bytes 589856 | tf_op jit(solution)/shard_map/all_to_all | solution.py:414
  124.7 3.4 %all-to-all-start.2 = ((f32[8,48,128]{2,1,0:T(8,128)}), f32[8,48,128]{2,1,0:T(8,128)S(1)}, u32[]{:S(2)}, u32[]{:S(2)}) async-start(f32[8,48,128]{2,1,0:T(8,128)} %bitcast.32), calls=%async_computation.2 | async-start | bytes 393216 | tf_op jit(solution)/shard_map/all_to_all | solution.py:450
  128.1 4.7 %backward.2 = (bf16[256,768]{1,0:T(8,128)(2,1)}, bf16[256,768]{1,0:T(8,128)(2,1)}, bf16[256,768]{1,0:T(8,128)(2,1)}) custom-call(s32[1,256]{1,0:T(1,128)S(1)} %bitcast.35, s32[256,1]{1,0:T(8,128)S(1)} %copy.16.col_ref, bf16[256,2304]{1,0:T(8,128)(2,1)S(1)} %get-tuple-element.58.q_ref.k_ref.v_ref, bf16[256,2304]{1,0:T(8,128)(2,1)S(1)} %get-tuple-element.58.q_ref.k_ref.v_ref, ...), custom_call_target="tpu_custom_call" | custom-call | tf_op jit(solution)/shard_map/backward/pallas_call | solution.py:422
  132.8 4.9 %all-to-all-done.2 = f32[8,48,128]{2,1,0:T(8,128)S(1)} async-done(((f32[8,48,128]{2,1,0:T(8,128)}), f32[8,48,128]{2,1,0:T(8,128)S(1)}, u32[]{:S(2)}, u32[]{:S(2)}) %all-to-all-start.2) | async-done | bytes 196640 | tf_op jit(solution)/shard_map/all_to_all | solution.py:450
  139.0 2.0 %collective-permute-start.22 = (f32[48,128]{1,0:T(8,128)S(1)}, f32[48,128]{1,0:T(8,128)S(1)}, u32[]{:S(2)}, u32[]{:S(2)}) collective-permute-start(f32[48,128]{1,0:T(8,128)S(1)} %reduce_sum.9), channel_id=1, source_target_pairs={{0,24},{8,0},{16,8},{24,16},{1,25},{9,1},{17,9},{25,17},{2,26},{10... | collective-permute-start | bytes 73736 | tf_op jit(solution)/shard_map/ppermute | solution.py:272
  143.4 3.4 %all-to-all-start.3 = ((f32[8,48,128]{2,1,0:T(8,128)}), f32[8,48,128]{2,1,0:T(8,128)S(1)}, u32[]{:S(2)}, u32[]{:S(2)}) async-start(f32[8,48,128]{2,1,0:T(8,128)} %broadcast_in_dim.27), calls=%async_computation.3 | async-start | bytes 393216 | tf_op jit(solution)/shard_map/all_to_all | solution.py:454
  146.8 4.7 %backward.3 = (bf16[256,768]{1,0:T(8,128)(2,1)}, bf16[256,768]{1,0:T(8,128)(2,1)}, bf16[256,768]{1,0:T(8,128)(2,1)}) custom-call(s32[1,256]{1,0:T(1,128)S(1)} %bitcast.36, s32[256,1]{1,0:T(8,128)S(1)} %copy.16.col_ref, bf16[256,2304]{1,0:T(8,128)(2,1)S(1)} %get-tuple-element.58.q_ref.k_ref.v_ref, ...), custom_call_target="tpu_custom_call", output_to_operand_aliasing={{0}: (9, {}), {1}: (10, {}), {2}: (11, {})} | custom-call | tf_op jit(solution)/shard_map/backward/pallas_call | solution.py:422
  151.5 3.9 %all-to-all-done.3 = f32[8,48,128]{2,1,0:T(8,128)S(1)} async-done(((f32[8,48,128]{2,1,0:T(8,128)}), f32[8,48,128]{2,1,0:T(8,128)S(1)}, u32[]{:S(2)}, u32[]{:S(2)}) %all-to-all-start.3) | async-done | bytes 196640 | tf_op jit(solution)/shard_map/all_to_all | solution.py:454
  156.3 2.5 %update.1 = (f32[48,384]{1,0:T(8,128)S(1)}, f32[48,384]{1,0:T(8,128)S(1)}) custom-call(s32[1]{0:T(128)} %bitcast.8.core_ref, f32[384,128]{1,0:T(8,128)S(1)} %bitcast.31, f32[96,384]{1,0:T(8,128)S(1)} %copy-done.5), custom_call_target="tpu_custom_call" | custom-call | tf_op jit(solution)/shard_map/update/pallas_call | solution.py:284
  158.8 4.3 %collective-permute-start.23 = (f32[48,384]{1,0:T(8,128)S(1)}, f32[48,384]{1,0:T(8,128)S(1)}, u32[]{:S(2)}, u32[]{:S(2)}) collective-permute-start(f32[48,384]{1,0:T(8,128)S(1)} %get-tuple-element.79), channel_id=1, source_target_pairs={{0,4},{4,0},{1,5},{5,1},{2,6},{6,2},{3,7},{7,3},{8,12},{12,8},{9,1... | collective-permute-start | bytes 221192 | tf_op jit(solution)/shard_map/ppermute | solution.py:272
  (83 shorter events, 22.6 us)
Async XLA Ops:
  7.2 54.3 %all-gather.2.cloned.1.call-start = ((), (), s32[]{:S(2)}) async-start(), calls=%async_computation.4 | async-start | bytes 1253376 | tf_op jit(solution)/shard_map/all_gather | solution.py:350
  12.9 62.6 %all-to-all-start = ((bf16[64,112,128]{2,1,0:T(8,128)(2,1)}), bf16[64,112,128]{2,1,0:T(8,128)(2,1)S(1)}, u32[]{:S(2)}, u32[]{:S(2)}) async-start(bf16[64,112,128]{2,1,0:T(8,128)(2,1)} %place.1), calls=%async_computation | async-start | bytes 3670016 | tf_op jit(solution)/shard_map/all_to_all | solution.py:316
  26.4 22.3 %copy-start.6 = (s32[256]{0:T(256)S(1)}, s32[256]{0:T(256)}, u32[]{:S(2)}) copy-start(s32[256]{0:T(256)} %param.13) | copy-start | bytes 3076
  26.4 22.4 %copy-start.7 = (s32[256]{0:T(256)S(1)}, s32[256]{0:T(256)}, u32[]{:S(2)}) copy-start(s32[256]{0:T(256)} %param.12) | copy-start | bytes 3076
  27.1 8.6 %collective-permute-start.4 = (bf16[192,256]{1,0:T(8,128)(2,1)S(1)}, bf16[192,256]{1,0:T(8,128)(2,1)S(1)}, u32[]{:S(2)}, u32[]{:S(2)}) collective-permute-start(bf16[192,256]{1,0:T(8,128)(2,1)S(1)} %get-tuple-element.88), channel_id=1, source_target_pairs={{0,16},{8,24},{16,0},{24,8},{1,17},{9,25},{17,1},{25,9},{2,18},{10... | collective-permute-start | bytes 294920 | tf_op jit(solution)/shard_map/ppermute | solution.py:272
  30.0 8.9 %collective-permute-start.5 = (bf16[192,256]{1,0:T(8,128)(2,1)S(1)}, bf16[192,256]{1,0:T(8,128)(2,1)S(1)}, u32[]{:S(2)}, u32[]{:S(2)}) collective-permute-start(bf16[192,256]{1,0:T(8,128)(2,1)S(1)} %get-tuple-element.89), channel_id=1, source_target_pairs={{0,24},{8,0},{16,8},{24,16},{1,25},{9,1},{17,9},{25,17},{2,26},{10... | collective-permute-start | bytes 294920 | tf_op jit(solution)/shard_map/ppermute | solution.py:272
  30.9 10.6 %collective-permute-start = (bf16[192,256]{1,0:T(8,128)(2,1)S(1)}, bf16[192,256]{1,0:T(8,128)(2,1)S(1)}, u32[]{:S(2)}, u32[]{:S(2)}) collective-permute-start(bf16[192,256]{1,0:T(8,128)(2,1)S(1)} %get-tuple-element.90), channel_id=1, source_target_pairs={{0,8},{8,16},{16,24},{24,0},{1,9},{9,17},{17,25},{25,1},{2,10},{10... | collective-permute-start | bytes 294920 | tf_op jit(solution)/shard_map/ppermute | solution.py:272
  39.0 6.3 %collective-permute-start.7 = (bf16[2,192,256]{2,1,0:T(8,128)(2,1)S(1)}, bf16[2,192,256]{2,1,0:T(8,128)(2,1)S(1)}, u32[]{:S(2)}, u32[]{:S(2)}) collective-permute-start(bf16[2,192,256]{2,1,0:T(8,128)(2,1)S(1)} %pad_maximum_fusion.1.refs_4_), channel_id=1, source_target_pairs={{0,3},{1,0},{2,1},{3,2},{4,7},{5,4},{6,5},{7,6},{8,11},{9,8},{10,9... | collective-permute-start | bytes 589832 | tf_op jit(solution)/shard_map/ppermute | solution.py:272
  41.6 7.1 %collective-permute-start.1 = (bf16[2,192,256]{2,1,0:T(8,128)(2,1)S(1)}, bf16[2,192,256]{2,1,0:T(8,128)(2,1)S(1)}, u32[]{:S(2)}, u32[]{:S(2)}) collective-permute-start(bf16[2,192,256]{2,1,0:T(8,128)(2,1)S(1)} %pad_maximum_fusion.refs_0_), channel_id=1, source_target_pairs={{0,1},{1,2},{2,3},{3,0},{4,5},{5,6},{6,7},{7,4},{8,9},{9,10},{10,1... | collective-permute-start | bytes 589832 | tf_op jit(solution)/shard_map/ppermute | solution.py:272
  41.7 11.0 %collective-permute-start.6 = (bf16[2,192,256]{2,1,0:T(8,128)(2,1)S(1)}, bf16[2,192,256]{2,1,0:T(8,128)(2,1)S(1)}, u32[]{:S(2)}, u32[]{:S(2)}) collective-permute-start(bf16[2,192,256]{2,1,0:T(8,128)(2,1)S(1)} %pad_maximum_fusion.1.refs_4_), channel_id=1, source_target_pairs={{0,1},{1,2},{2,3},{3,0},{4,5},{5,6},{6,7},{7,4},{8,9},{9,10},{10,1... | collective-permute-start | bytes 589832 | tf_op jit(solution)/shard_map/ppermute | solution.py:272
  42.1 10.6 %collective-permute-start.3 = (bf16[2,192,256]{2,1,0:T(8,128)(2,1)S(1)}, bf16[2,192,256]{2,1,0:T(8,128)(2,1)}, u32[]{:S(2)}, u32[]{:S(2)}) collective-permute-start(bf16[2,192,256]{2,1,0:T(8,128)(2,1)S(1)} %pad_maximum_fusion.refs_0_), channel_id=1, source_target_pairs={{0,3},{1,0},{2,1},{3,2},{4,7},{5,4},{6,5},{7,6},{8,11},{9,8},{10,9... | collective-permute-start | bytes 589832 | tf_op jit(solution)/shard_map/ppermute | solution.py:272
  45.3 8.2 %collective-permute-start.8 = (bf16[2,192,256]{2,1,0:T(8,128)(2,1)S(1)}, bf16[2,192,256]{2,1,0:T(8,128)(2,1)}, u32[]{:S(2)}, u32[]{:S(2)}) collective-permute-start(bf16[2,192,256]{2,1,0:T(8,128)(2,1)S(1)} %collective-permute-done.7.refs_7_), channel_id=1, source_target_pairs={{0,3},{1,0},{2,1},{3,2},{4,7},{5,4},{6,5},{7,6},{8,11},{9,8},{10,9... | collective-permute-start | bytes 589832 | tf_op jit(solution)/shard_map/ppermute | solution.py:272
  48.7 7.7 %collective-permute-start.2 = (bf16[2,192,256]{2,1,0:T(8,128)(2,1)S(1)}, bf16[2,192,256]{2,1,0:T(8,128)(2,1)}, u32[]{:S(2)}, u32[]{:S(2)}) collective-permute-start(bf16[2,192,256]{2,1,0:T(8,128)(2,1)S(1)} %collective-permute-done.1.refs_1_), channel_id=1, source_target_pairs={{0,1},{1,2},{2,3},{3,0},{4,5},{5,6},{6,7},{7,4},{8,9},{9,10},{10,1... | collective-permute-start | bytes 589832 | tf_op jit(solution)/shard_map/ppermute | solution.py:272
  59.1 6.3 %collective-permute-start.9 = (bf16[4,768,256]{2,1,0:T(8,128)(2,1)}, bf16[4,768,256]{2,1,0:T(8,128)(2,1)}, u32[]{:S(2)}, u32[]{:S(2)}) collective-permute-start(bf16[4,768,256]{2,1,0:T(8,128)(2,1)} %join_cot.1.cot_ref), channel_id=1, source_target_pairs={{0,4},{4,0},{1,5},{5,1},{2,6},{6,2},{3,7},{7,3},{8,12},{12,8},{9,1... | collective-permute-start | bytes 4718600 | tf_op jit(solution)/shard_map/ppermute | solution.py:272
  80.3 6.3 %collective-permute-start.10 = (bf16[256,384]{1,0:T(8,128)(2,1)S(1)}, bf16[256,384]{1,0:T(8,128)(2,1)S(1)}, u32[]{:S(2)}, u32[]{:S(2)}) collective-permute-start(bf16[256,384]{1,0:T(8,128)(2,1)S(1)} %get-tuple-element.50.refs_6_), channel_id=1, source_target_pairs={{0,8},{8,16},{16,24},{24,0},{1,9},{9,17},{17,25},{25,1},{2,10},{10... | collective-permute-start | bytes 589832 | tf_op jit(solution)/shard_map/ppermute | solution.py:272
  81.5 8.6 %collective-permute-start.12 = (bf16[256,384]{1,0:T(8,128)(2,1)S(1)}, bf16[256,384]{1,0:T(8,128)(2,1)S(1)}, u32[]{:S(2)}, u32[]{:S(2)}) collective-permute-start(bf16[256,384]{1,0:T(8,128)(2,1)S(1)} %get-tuple-element.51), channel_id=1, source_target_pairs={{0,28},{4,24},{8,4},{12,0},{16,12},{20,8},{24,20},{28,16},{1,29},{... | collective-permute-start | bytes 589832 | tf_op jit(solution)/shard_map/ppermute | solution.py:277
  84.7 9.6 %collective-permute-start.14 = (bf16[256,384]{1,0:T(8,128)(2,1)S(1)}, bf16[256,384]{1,0:T(8,128)(2,1)S(1)}, u32[]{:S(2)}, u32[]{:S(2)}) collective-permute-start(bf16[256,384]{1,0:T(8,128)(2,1)S(1)} %get-tuple-element.50.refs_6_), channel_id=1, source_target_pairs={{0,24},{8,0},{16,8},{24,16},{1,25},{9,1},{17,9},{25,17},{2,26},{10... | collective-permute-start | bytes 589832 | tf_op jit(solution)/shard_map/ppermute | solution.py:272
  86.0 8.4 %collective-permute-start.15 = (bf16[256,384]{1,0:T(8,128)(2,1)S(1)}, bf16[256,384]{1,0:T(8,128)(2,1)S(1)}, u32[]{:S(2)}, u32[]{:S(2)}) collective-permute-start(bf16[256,384]{1,0:T(8,128)(2,1)S(1)} %get-tuple-element.51), channel_id=1, source_target_pairs={{0,4},{4,0},{1,5},{5,1},{2,6},{6,2},{3,7},{7,3},{8,12},{12,8},{9,1... | collective-permute-start | bytes 589832 | tf_op jit(solution)/shard_map/ppermute | solution.py:272
  86.0 8.4 %collective-permute-start.16 = (bf16[256,384]{1,0:T(8,128)(2,1)S(1)}, bf16[256,384]{1,0:T(8,128)(2,1)S(1)}, u32[]{:S(2)}, u32[]{:S(2)}) collective-permute-start(bf16[256,384]{1,0:T(8,128)(2,1)S(1)} %get-tuple-element.51), channel_id=1, source_target_pairs={{0,12},{4,8},{8,20},{12,16},{16,28},{20,24},{24,4},{28,0},{1,13},{... | collective-permute-start | bytes 589832 | tf_op jit(solution)/shard_map/ppermute | solution.py:277
  86.6 11.9 %collective-permute-start.11 = (bf16[256,384]{1,0:T(8,128)(2,1)S(1)}, bf16[256,384]{1,0:T(8,128)(2,1)S(1)}, u32[]{:S(2)}, u32[]{:S(2)}) collective-permute-start(bf16[256,384]{1,0:T(8,128)(2,1)S(1)} %collective-permute-done.10.refs_7_), channel_id=1, source_target_pairs={{0,8},{8,16},{16,24},{24,0},{1,9},{9,17},{17,25},{25,1},{2,10},{10... | collective-permute-start | bytes 589832 | tf_op jit(solution)/shard_map/ppermute | solution.py:272
  90.1 8.4 %collective-permute-start.13 = (bf16[256,384]{1,0:T(8,128)(2,1)S(1)}, bf16[256,384]{1,0:T(8,128)(2,1)S(1)}, u32[]{:S(2)}, u32[]{:S(2)}) collective-permute-start(bf16[256,384]{1,0:T(8,128)(2,1)S(1)} %collective-permute-done.12.refs_11_), channel_id=1, source_target_pairs={{0,24},{8,0},{16,8},{24,16},{1,25},{9,1},{17,9},{25,17},{2,26},{10... | collective-permute-start | bytes 589832 | tf_op jit(solution)/shard_map/ppermute | solution.py:272
  100.0 28.1 %copy-start.1 = (bf16[256,768]{1,0:T(8,128)(2,1)S(1)}, bf16[256,768]{1,0:T(8,128)(2,1)}, u32[]{:S(2)}) copy-start(bf16[256,768]{1,0:T(8,128)(2,1)} %get-tuple-element.59.d0) | copy-start | bytes 1179652
  100.0 23.0 %all-to-all-start.1 = ((bf16[8,96,384]{2,1,0:T(8,128)(2,1)}), bf16[8,96,384]{2,1,0:T(8,128)(2,1)S(1)}, u32[]{:S(2)}, u32[]{:S(2)}) async-start(bf16[8,96,384]{2,1,0:T(8,128)(2,1)} %grad_far.1), calls=%async_computation.1 | async-start | bytes 1179648 | tf_op jit(solution)/shard_map/all_to_all | solution.py:414
  103.6 24.4 %collective-permute-start.17 = (bf16[256,768]{1,0:T(8,128)(2,1)}, bf16[256,768]{1,0:T(8,128)(2,1)S(1)}, u32[]{:S(2)}, u32[]{:S(2)}) collective-permute-start(bf16[256,768]{1,0:T(8,128)(2,1)} %get-tuple-element.60), channel_id=1, source_target_pairs={{0,24},{8,0},{16,8},{24,16},{1,25},{9,1},{17,9},{25,17},{2,26},{10... | collective-permute-start | bytes 1179656 | tf_op jit(solution)/shard_map/ppermute | solution.py:272
  104.7 23.4 %collective-permute-start.18 = (bf16[256,768]{1,0:T(8,128)(2,1)}, bf16[256,768]{1,0:T(8,128)(2,1)S(1)}, u32[]{:S(2)}, u32[]{:S(2)}) collective-permute-start(bf16[256,768]{1,0:T(8,128)(2,1)} %get-tuple-element.61), channel_id=1, source_target_pairs={{0,16},{8,24},{16,0},{24,8},{1,17},{9,25},{17,1},{25,9},{2,18},{10... | collective-permute-start | bytes 1179656 | tf_op jit(solution)/shard_map/ppermute | solution.py:272
  106.2 21.9 %collective-permute-start.19 = (bf16[256,768]{1,0:T(8,128)(2,1)}, bf16[256,768]{1,0:T(8,128)(2,1)}, u32[]{:S(2)}, u32[]{:S(2)}) collective-permute-start(bf16[256,768]{1,0:T(8,128)(2,1)} %get-tuple-element.62), channel_id=1, source_target_pairs={{0,8},{8,16},{16,24},{24,0},{1,9},{9,17},{17,25},{25,1},{2,10},{10... | collective-permute-start | bytes 1179656 | tf_op jit(solution)/shard_map/ppermute | solution.py:272
  124.7 13.0 %all-to-all-start.2 = ((f32[8,48,128]{2,1,0:T(8,128)}), f32[8,48,128]{2,1,0:T(8,128)S(1)}, u32[]{:S(2)}, u32[]{:S(2)}) async-start(f32[8,48,128]{2,1,0:T(8,128)} %bitcast.32), calls=%async_computation.2 | async-start | bytes 393216 | tf_op jit(solution)/shard_map/all_to_all | solution.py:450
  137.7 4.0 %collective-permute-start.20 = (f32[48,128]{1,0:T(8,128)S(1)}, f32[48,128]{1,0:T(8,128)S(1)}, u32[]{:S(2)}, u32[]{:S(2)}) collective-permute-start(f32[48,128]{1,0:T(8,128)S(1)} %reduce_sum.9), channel_id=1, source_target_pairs={{0,8},{8,16},{16,24},{24,0},{1,9},{9,17},{17,25},{25,1},{2,10},{10... | collective-permute-start | bytes 73736 | tf_op jit(solution)/shard_map/ppermute | solution.py:272
  138.5 4.2 %collective-permute-start.21 = (f32[48,128]{1,0:T(8,128)S(1)}, f32[48,128]{1,0:T(8,128)S(1)}, u32[]{:S(2)}, u32[]{:S(2)}) collective-permute-start(f32[48,128]{1,0:T(8,128)S(1)} %reduce_sum.9), channel_id=1, source_target_pairs={{0,16},{8,24},{16,0},{24,8},{1,17},{9,25},{17,1},{25,9},{2,18},{10... | collective-permute-start | bytes 73736 | tf_op jit(solution)/shard_map/ppermute | solution.py:272
  139.0 3.7 %collective-permute-start.22 = (f32[48,128]{1,0:T(8,128)S(1)}, f32[48,128]{1,0:T(8,128)S(1)}, u32[]{:S(2)}, u32[]{:S(2)}) collective-permute-start(f32[48,128]{1,0:T(8,128)S(1)} %reduce_sum.9), channel_id=1, source_target_pairs={{0,24},{8,0},{16,8},{24,16},{1,25},{9,1},{17,9},{25,17},{2,26},{10... | collective-permute-start | bytes 73736 | tf_op jit(solution)/shard_map/ppermute | solution.py:272
  143.4 12.0 %all-to-all-start.3 = ((f32[8,48,128]{2,1,0:T(8,128)}), f32[8,48,128]{2,1,0:T(8,128)S(1)}, u32[]{:S(2)}, u32[]{:S(2)}) async-start(f32[8,48,128]{2,1,0:T(8,128)} %broadcast_in_dim.27), calls=%async_computation.3 | async-start | bytes 393216 | tf_op jit(solution)/shard_map/all_to_all | solution.py:454
  158.8 5.2 %collective-permute-start.23 = (f32[48,384]{1,0:T(8,128)S(1)}, f32[48,384]{1,0:T(8,128)S(1)}, u32[]{:S(2)}, u32[]{:S(2)}) collective-permute-start(f32[48,384]{1,0:T(8,128)S(1)} %get-tuple-element.79), channel_id=1, source_target_pairs={{0,4},{4,0},{1,5},{5,1},{2,6},{6,2},{3,7},{7,3},{8,12},{12,8},{9,1... | collective-permute-start | bytes 221192 | tf_op jit(solution)/shard_map/ppermute | solution.py:272
  (11 other events, 91.4 us)
Sparse Core Ops, SparseCore 0:
  9.8 46.4 all-gather.1

commit v3 on v2

--- a/solution.py
+++ b/solution.py
@@ -16,7 +16,8 @@
 BLOCKS = 3 * HEADS_HERE
 TILE = 16
 TILES = 7
-FLAT = GROUPS * TILE
+EIGHT = 8
+FLAT = GROUPS * EIGHT
 Z, Y, C, X = 8, 4, 2, 4
 FEAT = 48
 HALF = HEADS_HERE * HD // 2
@@ -29,26 +30,6 @@
 scale = 1.0 / math.sqrt(HD)
 f32 = jnp.float32
 bf16 = jnp.bfloat16
-
-
-def find_patterns():
-    found = []
-    for tile in range(3):
-        rows = [tile * TILE + i for i in range(TILE)]
-        for block in sorted({r // SLOTS for r in rows}):
-            found.append((tile, block))
-    return found
-
-
-PATTERNS = find_patterns()
-
-
-def pattern_users(tile, block):
-    return [
-        (tile + 3 * n, block + 8 * n)
-        for n in range(3)
-        if tile + 3 * n < TILES and block + 8 * n < BLOCKS
-    ]
 
 
 def place_kernel(q_hbm, k_hbm, v_hbm, label_ref, out_ref, q_ref, k_ref, v_ref, sems):
@@ -66,29 +47,32 @@
     start = jnp.sum(jnp.where(label == group, before, 0), axis=0, keepdims=True)
     code = 8 * label + lax.broadcasted_iota(jnp.int32, (1, ROWS), 1) - start
 
-    def block_of(j):
-        return fields[j // HEADS_HERE][:, (j % HEADS_HERE) * HD : (j % HEADS_HERE + 1) * HD]
-
-    row = lax.broadcasted_iota(jnp.int32, (TILE, ROWS), 0)
-    eights = 8 * lax.broadcasted_iota(jnp.int32, (GROUPS, TILE, ROWS), 0)
-    for copy in copies:
-        copy.wait()
-    for first in range(3):
-        total = {}
-        for tile, block in PATTERNS:
-            if tile != first:
-                continue
-            slot = row + (TILE * tile - SLOTS * block)
-            wanted = jnp.where((slot >= 0) & (slot < SLOTS), code - slot, -1)
-            hot = jnp.where(eights == wanted[None], 1.0, 0.0).astype(bf16).reshape(FLAT, ROWS)
-            users = pattern_users(tile, block)
-            wide = jnp.concatenate([block_of(j) for _, j in users], axis=1)
-            got = jnp.dot(hot, wide, preferred_element_type=f32)
-            for n, (t, _) in enumerate(users):
-                part = got[:, n * HD : (n + 1) * HD]
-                total[t] = part if t not in total else total[t] + part
-        for t, rows in total.items():
-            out_ref[:, t * TILE : (t + 1) * TILE, :] = rows.astype(bf16).reshape(GROUPS, TILE, HD)
+    row = lax.broadcasted_iota(jnp.int32, (FLAT, ROWS), 0)
+    hot = jnp.where(row == code, 1.0, 0.0).astype(bf16)
+    place = lax.broadcasted_iota(jnp.int32, (GROUPS, EIGHT, HD), 1)
+    rolled = [None] * BLOCKS
+    tiles = []
+    for pair in range(BLOCKS // 2):
+        which, at = divmod(pair, 3)
+        if at == 0:
+            copies[which].wait()
+        wide = fields[which][:, at * 2 * HD : (at + 1) * 2 * HD]
+        got = jnp.dot(hot, wide, preferred_element_type=f32)
+        for j in (2 * pair, 2 * pair + 1):
+            block = got[:, j % 2 * HD : (j % 2 + 1) * HD].reshape(GROUPS, EIGHT, HD)
+            rolled[j] = pltpu.roll(block, SLOTS * j % EIGHT, 1) if SLOTS * j % EIGHT else block
+        while len(tiles) < 2 * TILES:
+            j = EIGHT * len(tiles) // SLOTS
+            later = j + 1 if j + 1 < BLOCKS else j
+            if rolled[later] is None:
+                break
+            split = SLOTS * (j + 1) - EIGHT * len(tiles)
+            rest = rolled[later] if later > j else 0.0
+            tiles.append(jnp.where(place < split, rolled[j], rest))
+            if len(tiles) % 2 == 0:
+                t = len(tiles) // 2 - 1
+                both = jnp.concatenate(tiles[-2:], axis=1)
+                out_ref[:, t * TILE : (t + 1) * TILE, :] = both.astype(bf16)
 
 
 def join_cot_kernel(x_ref, *refs):
@@ -118,54 +102,30 @@
 
 
 def forward_kernel(
-    core_ref,
-    slots_hbm,
-    from_row,
-    from_col,
-    row_ref,
-    col_ref,
-    packed_ref,
-    own_ref,
-    other_ref,
-    slots_ref,
-    sems,
+    core_ref, slots_ref, from_row, from_col, row_ref, col_ref, packed_ref, own_ref, other_ref
 ):
-    copies = []
-    for t in range(TILES):
-        rows = pl.ds(t * TILE, TILE)
-        copies.append(pltpu.make_async_copy(slots_hbm.at[:, rows, :], slots_ref.at[t], sems.at[t]))
-    for first in range(3):
-        for copy in copies[first::3]:
-            copy.start()
-
     before = jnp.sum(jnp.where(from_row[...] < from_col[...], 1, 0), axis=1, keepdims=True)
     code = 8 * from_col[...] + lax.broadcasted_iota(jnp.int32, (ROWS, 1), 0) - before
-    lane = lax.broadcasted_iota(jnp.int32, (1, FLAT), 1)
-    group = lane // TILE
-    total = {}
-    landed = set()
-    for tile, block in PATTERNS:
-        if tile not in landed:
-            for copy in copies[tile::3]:
-                copy.wait()
-            landed.add(tile)
-        slot = lane - TILE * group + (TILE * tile - SLOTS * block)
-        wanted = jnp.where((slot >= 0) & (slot < SLOTS), 8 * group + slot, -1)
-        hot = jnp.where(code == wanted, 1.0, 0.0).astype(bf16)
-        users = pattern_users(tile, block)
-        wide = jnp.concatenate(
-            [slots_ref[t].reshape(FLAT, HD) for t, _ in users],
-            axis=1,
-        )
+    lane = lax.broadcasted_iota(jnp.int32, (ROWS, FLAT), 1)
+    hot = jnp.where(code == lane, 1.0, 0.0).astype(bf16)
+    place = lax.broadcasted_iota(jnp.int32, (GROUPS, EIGHT, HD), 1)
+    tiles = []
+    for t in range(TILES):
+        both = slots_ref[:, t * TILE : (t + 1) * TILE, :].astype(f32)
+        tiles += [both[:, :EIGHT], both[:, EIGHT:]]
+    for pair in range(BLOCKS // 2):
+        blocks = []
+        for j in (2 * pair, 2 * pair + 1):
+            t, start = divmod(SLOTS * j, EIGHT)
+            block = tiles[t]
+            if start + SLOTS > EIGHT:
+                block = jnp.where(place < start, tiles[t + 1], block)
+            if start:
+                block = pltpu.roll(block, EIGHT - start, 1)
+            blocks.append(block.reshape(FLAT, HD).astype(bf16))
+        wide = jnp.concatenate(blocks, axis=1)
         got = jnp.dot(hot, wide, preferred_element_type=f32)
-        for n, (_, j) in enumerate(users):
-            part = got[:, n * HD : (n + 1) * HD]
-            if j in total:
-                packed_ref[:, j * HD : (j + 1) * HD] = (total.pop(j) + part).astype(bf16)
-            elif SLOTS * j // TILE != (SLOTS * j + SLOTS - 1) // TILE:
-                total[j] = part
-            else:
-                packed_ref[:, j * HD : (j + 1) * HD] = part.astype(bf16)
+        packed_ref[:, pair * 2 * HD : (pair + 1) * 2 * HD] = got.astype(bf16)
     same = row_ref[...] == col_ref[...]
     core = core_ref[0]
     for side, out_ref in enumerate((own_ref, other_ref)):
@@ -372,11 +332,6 @@
         seg_row,
         seg_col,
         scalars=1,
-        far=1,
-        scratch_shapes=[
-            pltpu.VMEM((TILES, GROUPS, TILE, HD), bf16),
-            pltpu.SemaphoreType.DMA((TILES,)),
-        ],
     )
 
     own_up = shift(own, "y", 1)

time: 172 us -> 170 us (0.988)
  Pallas kernels: 31.2 us -> 28.9 us
    pallas_call x9, Pallas kernels: 21.8 us -> 19.5 us  [local(): pl.pallas_call(kernel, in_specs=[smem] * scalars + [hbm] * far + [vmem] *...]
where the time goes in v3:
time: 170 us
  waiting for transfers between devices  62.4 us (37%)
  starting transfers between devices  56.5 us (33%)
  Pallas kernels  28.9 us (17%)
  between operations  14.3 us (8%)
  local copies, waits for them, and re-layouts  6.85 us (4%)
    ppermute x22, starting transfers between devices, shift(): lax.ppermute(field, axis, [(i, (i + step) % size) for i in range(size)])  29.3 us
    ppermute x22, waiting for transfers between devices, shift(): lax.ppermute(field, axis, [(i, (i + step) % size) for i in range(size)])  22.8 us
    pallas_call x9, Pallas kernels, local(): pl.pallas_call(kernel, in_specs=[smem] * scalars + [hbm] * far + [vmem] *...  19.5 us
    all_to_all x1, waiting for transfers between devices, shards(): parts = lax.all_to_all(grad, 'z', split_axis=0, concat_axis=0, tiled=True)  16.7 us
    all_to_all x1, starting transfers between devices, shards(): lax.all_to_all(slots, everything, split_axis=0, concat_axis=0, tiled=True)  13.2 us
    all_to_all x1, waiting for transfers between devices, shards(): lax.all_to_all(slots, everything, split_axis=0, concat_axis=0, tiled=True)  10.6 us
    pallas_call x2, Pallas kernels, backward(): pl.pallas_call(backward_kernel, grid=(3,), in_specs=[pl.BlockSpec((1, ROW...  9.39 us
    all_to_all x1, waiting for transfers between devices, shards(): lax.all_to_all(gram, 'z', split_axis=0, concat_axis=0, tiled=True)  4.87 us
  transfers between devices with their start and end apart: 29, of which 17 were waited for; matrix products, arithmetic and copies ran while one was open for 2% of the time, Pallas kernels for 13%

profile of v3, /device:TPU:1, one launch (start us, length us, event | category | flops | bytes accessed | tf_op | source)
XLA Modules:
  0.0 169.8 jit_solution(10041992124518476842)
XLA Ops:
  7.9 4.2 %place.1 = bf16[64,112,128]{2,1,0:T(8,128)(2,1)} custom-call(bf16[256,768]{1,0:T(8,128)(2,1)} %q_hbm.1, bf16[256,768]{1,0:T(8,128)(2,1)} %k_hbm.1, bf16[256,768]{1,0:T(8,128)(2,1)} %v_hbm.1, s32[1,256]{1,0:T(1,128)} %bitcast.42), custom_call_target="tpu_custom_call" | custom-call | tf_op jit(solution)/shard_map/place/pallas_call | solution.py:244
  12.2 13.2 %all-to-all-start = ((bf16[64,112,128]{2,1,0:T(8,128)(2,1)}), bf16[64,112,128]{2,1,0:T(8,128)(2,1)S(1)}, u32[]{:S(2)}, u32[]{:S(2)}) async-start(bf16[64,112,128]{2,1,0:T(8,128)(2,1)} %place.1), calls=%async_computation | async-start | bytes 3670016 | tf_op jit(solution)/shard_map/all_to_all | solution.py:276
  26.3 3.0 %collective-permute-start.4 = (bf16[192,256]{1,0:T(8,128)(2,1)S(1)}, bf16[192,256]{1,0:T(8,128)(2,1)S(1)}, u32[]{:S(2)}, u32[]{:S(2)}) collective-permute-start(bf16[192,256]{1,0:T(8,128)(2,1)S(1)} %get-tuple-element.88), channel_id=1, source_target_pairs={{0,16},{8,24},{16,0},{24,8},{1,17},{9,25},{17,1},{25,9},{2,18},{10... | collective-permute-start | bytes 294920 | tf_op jit(solution)/shard_map/ppermute | solution.py:232
  30.7 3.7 %collective-permute-done.4 = bf16[192,256]{1,0:T(8,128)(2,1)S(1)} collective-permute-done((bf16[192,256]{1,0:T(8,128)(2,1)S(1)}, bf16[192,256]{1,0:T(8,128)(2,1)S(1)}, u32[]{:S(2)}, u32[]{:S(2)}) %collective-permute-start.4) | collective-permute-done | bytes 98336 | tf_op jit(solution)/shard_map/ppermute | solution.py:232
  34.5 3.9 %collective-permute-done.5 = bf16[192,256]{1,0:T(8,128)(2,1)S(1)} collective-permute-done((bf16[192,256]{1,0:T(8,128)(2,1)S(1)}, bf16[192,256]{1,0:T(8,128)(2,1)S(1)}, u32[]{:S(2)}, u32[]{:S(2)}) %collective-permute-start.5) | collective-permute-done | bytes 98336 | tf_op jit(solution)/shard_map/ppermute | solution.py:232
  38.4 2.5 %collective-permute-start.7 = (bf16[2,192,256]{2,1,0:T(8,128)(2,1)S(1)}, bf16[2,192,256]{2,1,0:T(8,128)(2,1)S(1)}, u32[]{:S(2)}, u32[]{:S(2)}) collective-permute-start(bf16[2,192,256]{2,1,0:T(8,128)(2,1)S(1)} %pad_maximum_fusion.1.refs_4_), channel_id=1, source_target_pairs={{0,3},{1,0},{2,1},{3,2},{4,7},{5,4},{6,5},{7,6},{8,11},{9,8},{10,9... | collective-permute-start | bytes 589832 | tf_op jit(solution)/shard_map/ppermute | solution.py:232
  41.9 2.0 %collective-permute-start.3 = (bf16[2,192,256]{2,1,0:T(8,128)(2,1)S(1)}, bf16[2,192,256]{2,1,0:T(8,128)(2,1)}, u32[]{:S(2)}, u32[]{:S(2)}) collective-permute-start(bf16[2,192,256]{2,1,0:T(8,128)(2,1)S(1)} %pad_maximum_fusion.refs_0_), channel_id=1, source_target_pairs={{0,3},{1,0},{2,1},{3,2},{4,7},{5,4},{6,5},{7,6},{8,11},{9,8},{10,9... | collective-permute-start | bytes 589832 | tf_op jit(solution)/shard_map/ppermute | solution.py:232
  44.9 3.4 %collective-permute-start.8 = (bf16[2,192,256]{2,1,0:T(8,128)(2,1)S(1)}, bf16[2,192,256]{2,1,0:T(8,128)(2,1)}, u32[]{:S(2)}, u32[]{:S(2)}) collective-permute-start(bf16[2,192,256]{2,1,0:T(8,128)(2,1)S(1)} %collective-permute-done.7.refs_7_), channel_id=1, source_target_pairs={{0,3},{1,0},{2,1},{3,2},{4,7},{5,4},{6,5},{7,6},{8,11},{9,8},{10,9... | collective-permute-start | bytes 589832 | tf_op jit(solution)/shard_map/ppermute | solution.py:232
  49.3 3.1 %collective-permute-done.6.refs_5_ = bf16[2,192,256]{2,1,0:T(8,128)(2,1)S(1)} collective-permute-done((bf16[2,192,256]{2,1,0:T(8,128)(2,1)S(1)}, bf16[2,192,256]{2,1,0:T(8,128)(2,1)S(1)}, u32[]{:S(2)}, u32[]{:S(2)}) %collective-permute-start.6) | collective-permute-done | bytes 196640 | tf_op jit(solution)/shard_map/ppermute | solution.py:232
  53.2 2.8 %collective-permute-done.2.refs_2_ = bf16[2,192,256]{2,1,0:T(8,128)(2,1)} collective-permute-done((bf16[2,192,256]{2,1,0:T(8,128)(2,1)S(1)}, bf16[2,192,256]{2,1,0:T(8,128)(2,1)}, u32[]{:S(2)}, u32[]{:S(2)}) %collective-permute-start.2) | collective-permute-done | bytes 196640 | tf_op jit(solution)/shard_map/ppermute | solution.py:232
  56.0 2.7 %join_cot.1.cot_ref = bf16[4,768,256]{2,1,0:T(8,128)(2,1)} custom-call(s32[1]{0:T(128)} %bitcast.1.x_ref, bf16[2,192,256]{2,1,0:T(8,128)(2,1)} %copy-done.10, bf16[2,192,256]{2,1,0:T(8,128)(2,1)} %copy-done.12, bf16[2,192,256]{2,1,0:T(8,128)(2,1)} %collective-permute-done.2.refs_2_, bf16[2,192,256]{2,1,0:T(8,128)(2,1)} %collective-permute-done.3.refs_3_, ...), custom_call_target="tpu_custom_call" | custom-call | tf_op jit(solution)/shard_map/join_cot/pallas_call | solution.py:244
  58.7 2.2 %collective-permute-start.9 = (bf16[4,768,256]{2,1,0:T(8,128)(2,1)}, bf16[4,768,256]{2,1,0:T(8,128)(2,1)}, u32[]{:S(2)}, u32[]{:S(2)}) collective-permute-start(bf16[4,768,256]{2,1,0:T(8,128)(2,1)} %join_cot.1.cot_ref), channel_id=1, source_target_pairs={{0,4},{4,0},{1,5},{5,1},{2,6},{6,2},{3,7},{7,3},{8,12},{12,8},{9,1... | collective-permute-start | bytes 4718600 | tf_op jit(solution)/shard_map/ppermute | solution.py:232
  60.9 3.9 %d_parts.1 = (bf16[256,768]{1,0:T(8,128)(2,1)}, bf16[256,768]{1,0:T(8,128)(2,1)}, bf16[256,768]{1,0:T(8,128)(2,1)}, bf16[256,768]{1,0:T(8,128)(2,1)}) custom-call(bf16[4,768,256]{2,1,0:T(8,128)(2,1)} %join_cot.1.cot_ref, bf16[768,768]{1,0:T(8,128)(2,1)} %all-gather.2.cloned.1.call-done.weight_ref), custom_call_target="tpu_custom_call" | custom-call | flops 17999998976 | bytes 54000000 | tf_op jit(solution)/shard_map/d_parts/pallas_call | solution.py:244
  64.8 10.6 %all-to-all-done.slots_ref = bf16[64,112,128]{2,1,0:T(8,128)(2,1)S(1)} async-done(((bf16[64,112,128]{2,1,0:T(8,128)(2,1)}), bf16[64,112,128]{2,1,0:T(8,128)(2,1)S(1)}, u32[]{:S(2)}, u32[]{:S(2)}) %all-to-all-start) | async-done | bytes 1835040 | tf_op jit(solution)/shard_map/all_to_all | solution.py:276
  76.3 2.3 %forward.1 = (bf16[256,2304]{1,0:T(8,128)(2,1)S(1)}, bf16[256,384]{1,0:T(8,128)(2,1)S(1)}, bf16[256,384]{1,0:T(8,128)(2,1)S(1)}) custom-call(s32[1]{0:T(128)} %bitcast.8.core_ref, bf16[64,112,128]{2,1,0:T(8,128)(2,1)S(1)} %all-to-all-done.slots_ref, s32[1,256]{1,0:T(1,128)S(1)} %bitcast.38, s32[256,1]{1,0:T(8,128)S(1)} %copy-done.2, s32[1,256]{1,0:T(1,128)S(1)} %bitcast.34, ...), custom_call_target="tpu_custom_call" | custom-call | tf_op jit(solution)/shard_map/forward/pallas_call | solution.py:244
  79.9 2.7 %collective-permute-start.12 = (bf16[256,384]{1,0:T(8,128)(2,1)S(1)}, bf16[256,384]{1,0:T(8,128)(2,1)S(1)}, u32[]{:S(2)}, u32[]{:S(2)}) collective-permute-start(bf16[256,384]{1,0:T(8,128)(2,1)S(1)} %get-tuple-element.51), channel_id=1, source_target_pairs={{0,28},{4,24},{8,4},{12,0},{16,12},{20,8},{24,20},{28,16},{1,29},{... | collective-permute-start | bytes 589832 | tf_op jit(solution)/shard_map/ppermute | solution.py:237
  85.2 2.9 %collective-permute-done.12.refs_11_ = bf16[256,384]{1,0:T(8,128)(2,1)S(1)} collective-permute-done((bf16[256,384]{1,0:T(8,128)(2,1)S(1)}, bf16[256,384]{1,0:T(8,128)(2,1)S(1)}, u32[]{:S(2)}, u32[]{:S(2)}) %collective-permute-start.12) | collective-permute-done | bytes 196640 | tf_op jit(solution)/shard_map/ppermute | solution.py:237
  89.4 1.8 %slice_bitcast_fusion = (bf16[768,256]{1,0:T(8,128)(2,1)S(1)}, bf16[768,256]{1,0:T(8,128)(2,1)S(1)}, bf16[768,256]{1,0:T(8,128)(2,1)S(1)}, bf16[768,256]{1,0:T(8...) fusion(bf16[4,768,256]{2,1,0:T(8,128)(2,1)} %collective-permute, ...), kind=kLoop, calls=%fused_computation.4 | loop fusion | bytes 6291456 | tf_op jit(solution)/shard_map/squeeze | solution.py:349
  92.3 1.4 grad_near.1.near_ref
  93.7 2.8 %collective-permute-done.11.own_far = bf16[256,384]{1,0:T(8,128)(2,1)S(1)} collective-permute-done((bf16[256,384]{1,0:T(8,128)(2,1)S(1)}, bf16[256,384]{1,0:T(8,128)(2,1)S(1)}, u32[]{:S(2)}, u32[]{:S(2)}) %collective-permute-start.11) | collective-permute-done | bytes 196640 | tf_op jit(solution)/shard_map/ppermute | solution.py:232
  96.5 1.4 grad_far.1
  97.9 3.7 %all-to-all-start.1 = ((bf16[8,96,384]{2,1,0:T(8,128)(2,1)}), bf16[8,96,384]{2,1,0:T(8,128)(2,1)S(1)}, u32[]{:S(2)}, u32[]{:S(2)}) async-start(bf16[8,96,384]{2,1,0:T(8,128)(2,1)} %grad_far.1), calls=%async_computation.1 | async-start | bytes 1179648 | tf_op jit(solution)/shard_map/all_to_all | solution.py:369
  104.2 16.7 %all-to-all-done.1.parts_ref = bf16[8,96,384]{2,1,0:T(8,128)(2,1)S(1)} async-done(((bf16[8,96,384]{2,1,0:T(8,128)(2,1)}), bf16[8,96,384]{2,1,0:T(8,128)(2,1)S(1)}, u32[]{:S(2)}, u32[]{:S(2)}) %all-to-all-start.1) | async-done | bytes 589856 | tf_op jit(solution)/shard_map/all_to_all | solution.py:369
  122.6 3.6 %all-to-all-start.2 = ((f32[8,48,128]{2,1,0:T(8,128)}), f32[8,48,128]{2,1,0:T(8,128)S(1)}, u32[]{:S(2)}, u32[]{:S(2)}) async-start(f32[8,48,128]{2,1,0:T(8,128)} %bitcast.32), calls=%async_computation.2 | async-start | bytes 393216 | tf_op jit(solution)/shard_map/all_to_all | solution.py:405
  126.3 4.7 %backward.2 = (bf16[256,768]{1,0:T(8,128)(2,1)}, bf16[256,768]{1,0:T(8,128)(2,1)}, bf16[256,768]{1,0:T(8,128)(2,1)}) custom-call(s32[1,256]{1,0:T(1,128)S(1)} %bitcast.35, s32[256,1]{1,0:T(8,128)S(1)} %copy.16.col_ref, bf16[256,2304]{1,0:T(8,128)(2,1)S(1)} %get-tuple-element.58.q_ref.k_ref.v_ref, bf16[256,2304]{1,0:T(8,128)(2,1)S(1)} %get-tuple-element.58.q_ref.k_ref.v_ref, ...), custom_call_target="tpu_custom_call" | custom-call | tf_op jit(solution)/shard_map/backward/pallas_call | solution.py:377
  131.0 4.9 %all-to-all-done.2 = f32[8,48,128]{2,1,0:T(8,128)S(1)} async-done(((f32[8,48,128]{2,1,0:T(8,128)}), f32[8,48,128]{2,1,0:T(8,128)S(1)}, u32[]{:S(2)}, u32[]{:S(2)}) %all-to-all-start.2) | async-done | bytes 196640 | tf_op jit(solution)/shard_map/all_to_all | solution.py:405
  137.2 2.0 %collective-permute-start.22 = (f32[48,128]{1,0:T(8,128)S(1)}, f32[48,128]{1,0:T(8,128)S(1)}, u32[]{:S(2)}, u32[]{:S(2)}) collective-permute-start(f32[48,128]{1,0:T(8,128)S(1)} %reduce_sum.9), channel_id=1, source_target_pairs={{0,24},{8,0},{16,8},{24,16},{1,25},{9,1},{17,9},{25,17},{2,26},{10... | collective-permute-start | bytes 73736 | tf_op jit(solution)/shard_map/ppermute | solution.py:232
  141.8 3.4 %all-to-all-start.3 = ((f32[8,48,128]{2,1,0:T(8,128)}), f32[8,48,128]{2,1,0:T(8,128)S(1)}, u32[]{:S(2)}, u32[]{:S(2)}) async-start(f32[8,48,128]{2,1,0:T(8,128)} %broadcast_in_dim.27), calls=%async_computation.3 | async-start | bytes 393216 | tf_op jit(solution)/shard_map/all_to_all | solution.py:409
  145.2 4.7 %backward.3 = (bf16[256,768]{1,0:T(8,128)(2,1)}, bf16[256,768]{1,0:T(8,128)(2,1)}, bf16[256,768]{1,0:T(8,128)(2,1)}) custom-call(s32[1,256]{1,0:T(1,128)S(1)} %bitcast.36, s32[256,1]{1,0:T(8,128)S(1)} %copy.16.col_ref, bf16[256,2304]{1,0:T(8,128)(2,1)S(1)} %get-tuple-element.58.q_ref.k_ref.v_ref, ...), custom_call_target="tpu_custom_call", output_to_operand_aliasing={{0}: (9, {}), {1}: (10, {}), {2}: (11, {})} | custom-call | tf_op jit(solution)/shard_map/backward/pallas_call | solution.py:377
  149.9 3.9 %all-to-all-done.3 = f32[8,48,128]{2,1,0:T(8,128)S(1)} async-done(((f32[8,48,128]{2,1,0:T(8,128)}), f32[8,48,128]{2,1,0:T(8,128)S(1)}, u32[]{:S(2)}, u32[]{:S(2)}) %all-to-all-start.3) | async-done | bytes 196640 | tf_op jit(solution)/shard_map/all_to_all | solution.py:409
  154.7 2.5 %update.1 = (f32[48,384]{1,0:T(8,128)S(1)}, f32[48,384]{1,0:T(8,128)S(1)}) custom-call(s32[1]{0:T(128)} %bitcast.8.core_ref, f32[384,128]{1,0:T(8,128)S(1)} %bitcast.31, f32[96,384]{1,0:T(8,128)S(1)} %copy-done.5), custom_call_target="tpu_custom_call" | custom-call | tf_op jit(solution)/shard_map/update/pallas_call | solution.py:244
  157.2 4.1 %collective-permute-start.23 = (f32[48,384]{1,0:T(8,128)S(1)}, f32[48,384]{1,0:T(8,128)S(1)}, u32[]{:S(2)}, u32[]{:S(2)}) collective-permute-start(f32[48,384]{1,0:T(8,128)S(1)} %get-tuple-element.79), channel_id=1, source_target_pairs={{0,4},{4,0},{1,5},{5,1},{2,6},{6,2},{3,7},{7,3},{8,12},{12,8},{9,1... | collective-permute-start | bytes 221192 | tf_op jit(solution)/shard_map/ppermute | solution.py:232
  (83 shorter events, 24.8 us)
Async XLA Ops:
  7.2 53.7 %all-gather.2.cloned.1.call-start = ((), (), s32[]{:S(2)}) async-start(), calls=%async_computation.4 | async-start | bytes 1253376 | tf_op jit(solution)/shard_map/all_gather | solution.py:310
  12.2 63.2 %all-to-all-start = ((bf16[64,112,128]{2,1,0:T(8,128)(2,1)}), bf16[64,112,128]{2,1,0:T(8,128)(2,1)S(1)}, u32[]{:S(2)}, u32[]{:S(2)}) async-start(bf16[64,112,128]{2,1,0:T(8,128)(2,1)} %place.1), calls=%async_computation | async-start | bytes 3670016 | tf_op jit(solution)/shard_map/all_to_all | solution.py:276
  25.7 22.6 %copy-start.6 = (s32[256]{0:T(256)S(1)}, s32[256]{0:T(256)}, u32[]{:S(2)}) copy-start(s32[256]{0:T(256)} %param.13) | copy-start | bytes 3076
  25.7 22.8 %copy-start.7 = (s32[256]{0:T(256)S(1)}, s32[256]{0:T(256)}, u32[]{:S(2)}) copy-start(s32[256]{0:T(256)} %param.12) | copy-start | bytes 3076
  26.3 8.2 %collective-permute-start.4 = (bf16[192,256]{1,0:T(8,128)(2,1)S(1)}, bf16[192,256]{1,0:T(8,128)(2,1)S(1)}, u32[]{:S(2)}, u32[]{:S(2)}) collective-permute-start(bf16[192,256]{1,0:T(8,128)(2,1)S(1)} %get-tuple-element.88), channel_id=1, source_target_pairs={{0,16},{8,24},{16,0},{24,8},{1,17},{9,25},{17,1},{25,9},{2,18},{10... | collective-permute-start | bytes 294920 | tf_op jit(solution)/shard_map/ppermute | solution.py:232
  29.3 9.1 %collective-permute-start.5 = (bf16[192,256]{1,0:T(8,128)(2,1)S(1)}, bf16[192,256]{1,0:T(8,128)(2,1)S(1)}, u32[]{:S(2)}, u32[]{:S(2)}) collective-permute-start(bf16[192,256]{1,0:T(8,128)(2,1)S(1)} %get-tuple-element.89), channel_id=1, source_target_pairs={{0,24},{8,0},{16,8},{24,16},{1,25},{9,1},{17,9},{25,17},{2,26},{10... | collective-permute-start | bytes 294920 | tf_op jit(solution)/shard_map/ppermute | solution.py:232
  30.1 10.8 %collective-permute-start = (bf16[192,256]{1,0:T(8,128)(2,1)S(1)}, bf16[192,256]{1,0:T(8,128)(2,1)S(1)}, u32[]{:S(2)}, u32[]{:S(2)}) collective-permute-start(bf16[192,256]{1,0:T(8,128)(2,1)S(1)} %get-tuple-element.90), channel_id=1, source_target_pairs={{0,8},{8,16},{16,24},{24,0},{1,9},{9,17},{17,25},{25,1},{2,10},{10... | collective-permute-start | bytes 294920 | tf_op jit(solution)/shard_map/ppermute | solution.py:232
  38.4 6.4 %collective-permute-start.7 = (bf16[2,192,256]{2,1,0:T(8,128)(2,1)S(1)}, bf16[2,192,256]{2,1,0:T(8,128)(2,1)S(1)}, u32[]{:S(2)}, u32[]{:S(2)}) collective-permute-start(bf16[2,192,256]{2,1,0:T(8,128)(2,1)S(1)} %pad_maximum_fusion.1.refs_4_), channel_id=1, source_target_pairs={{0,3},{1,0},{2,1},{3,2},{4,7},{5,4},{6,5},{7,6},{8,11},{9,8},{10,9... | collective-permute-start | bytes 589832 | tf_op jit(solution)/shard_map/ppermute | solution.py:232
  41.0 7.3 %collective-permute-start.1 = (bf16[2,192,256]{2,1,0:T(8,128)(2,1)S(1)}, bf16[2,192,256]{2,1,0:T(8,128)(2,1)S(1)}, u32[]{:S(2)}, u32[]{:S(2)}) collective-permute-start(bf16[2,192,256]{2,1,0:T(8,128)(2,1)S(1)} %pad_maximum_fusion.refs_0_), channel_id=1, source_target_pairs={{0,1},{1,2},{2,3},{3,0},{4,5},{5,6},{6,7},{7,4},{8,9},{9,10},{10,1... | collective-permute-start | bytes 589832 | tf_op jit(solution)/shard_map/ppermute | solution.py:232
  41.1 11.3 %collective-permute-start.6 = (bf16[2,192,256]{2,1,0:T(8,128)(2,1)S(1)}, bf16[2,192,256]{2,1,0:T(8,128)(2,1)S(1)}, u32[]{:S(2)}, u32[]{:S(2)}) collective-permute-start(bf16[2,192,256]{2,1,0:T(8,128)(2,1)S(1)} %pad_maximum_fusion.1.refs_4_), channel_id=1, source_target_pairs={{0,1},{1,2},{2,3},{3,0},{4,5},{5,6},{6,7},{7,4},{8,9},{9,10},{10,1... | collective-permute-start | bytes 589832 | tf_op jit(solution)/shard_map/ppermute | solution.py:232
  41.9 10.5 %collective-permute-start.3 = (bf16[2,192,256]{2,1,0:T(8,128)(2,1)S(1)}, bf16[2,192,256]{2,1,0:T(8,128)(2,1)}, u32[]{:S(2)}, u32[]{:S(2)}) collective-permute-start(bf16[2,192,256]{2,1,0:T(8,128)(2,1)S(1)} %pad_maximum_fusion.refs_0_), channel_id=1, source_target_pairs={{0,3},{1,0},{2,1},{3,2},{4,7},{5,4},{6,5},{7,6},{8,11},{9,8},{10,9... | collective-permute-start | bytes 589832 | tf_op jit(solution)/shard_map/ppermute | solution.py:232
  44.9 8.3 %collective-permute-start.8 = (bf16[2,192,256]{2,1,0:T(8,128)(2,1)S(1)}, bf16[2,192,256]{2,1,0:T(8,128)(2,1)}, u32[]{:S(2)}, u32[]{:S(2)}) collective-permute-start(bf16[2,192,256]{2,1,0:T(8,128)(2,1)S(1)} %collective-permute-done.7.refs_7_), channel_id=1, source_target_pairs={{0,3},{1,0},{2,1},{3,2},{4,7},{5,4},{6,5},{7,6},{8,11},{9,8},{10,9... | collective-permute-start | bytes 589832 | tf_op jit(solution)/shard_map/ppermute | solution.py:232
  48.3 7.7 %collective-permute-start.2 = (bf16[2,192,256]{2,1,0:T(8,128)(2,1)S(1)}, bf16[2,192,256]{2,1,0:T(8,128)(2,1)}, u32[]{:S(2)}, u32[]{:S(2)}) collective-permute-start(bf16[2,192,256]{2,1,0:T(8,128)(2,1)S(1)} %collective-permute-done.1.refs_1_), channel_id=1, source_target_pairs={{0,1},{1,2},{2,3},{3,0},{4,5},{5,6},{6,7},{7,4},{8,9},{9,10},{10,1... | collective-permute-start | bytes 589832 | tf_op jit(solution)/shard_map/ppermute | solution.py:232
  58.7 6.1 %collective-permute-start.9 = (bf16[4,768,256]{2,1,0:T(8,128)(2,1)}, bf16[4,768,256]{2,1,0:T(8,128)(2,1)}, u32[]{:S(2)}, u32[]{:S(2)}) collective-permute-start(bf16[4,768,256]{2,1,0:T(8,128)(2,1)} %join_cot.1.cot_ref), channel_id=1, source_target_pairs={{0,4},{4,0},{1,5},{5,1},{2,6},{6,2},{3,7},{7,3},{8,12},{12,8},{9,1... | collective-permute-start | bytes 4718600 | tf_op jit(solution)/shard_map/ppermute | solution.py:232
  78.6 6.6 %collective-permute-start.10 = (bf16[256,384]{1,0:T(8,128)(2,1)S(1)}, bf16[256,384]{1,0:T(8,128)(2,1)S(1)}, u32[]{:S(2)}, u32[]{:S(2)}) collective-permute-start(bf16[256,384]{1,0:T(8,128)(2,1)S(1)} %get-tuple-element.50.refs_6_), channel_id=1, source_target_pairs={{0,8},{8,16},{16,24},{24,0},{1,9},{9,17},{17,25},{25,1},{2,10},{10... | collective-permute-start | bytes 589832 | tf_op jit(solution)/shard_map/ppermute | solution.py:232
  79.9 8.2 %collective-permute-start.12 = (bf16[256,384]{1,0:T(8,128)(2,1)S(1)}, bf16[256,384]{1,0:T(8,128)(2,1)S(1)}, u32[]{:S(2)}, u32[]{:S(2)}) collective-permute-start(bf16[256,384]{1,0:T(8,128)(2,1)S(1)} %get-tuple-element.51), channel_id=1, source_target_pairs={{0,28},{4,24},{8,4},{12,0},{16,12},{20,8},{24,20},{28,16},{1,29},{... | collective-permute-start | bytes 589832 | tf_op jit(solution)/shard_map/ppermute | solution.py:237
  82.7 9.6 %collective-permute-start.14 = (bf16[256,384]{1,0:T(8,128)(2,1)S(1)}, bf16[256,384]{1,0:T(8,128)(2,1)S(1)}, u32[]{:S(2)}, u32[]{:S(2)}) collective-permute-start(bf16[256,384]{1,0:T(8,128)(2,1)S(1)} %get-tuple-element.50.refs_6_), channel_id=1, source_target_pairs={{0,24},{8,0},{16,8},{24,16},{1,25},{9,1},{17,9},{25,17},{2,26},{10... | collective-permute-start | bytes 589832 | tf_op jit(solution)/shard_map/ppermute | solution.py:232
  83.9 8.4 %collective-permute-start.15 = (bf16[256,384]{1,0:T(8,128)(2,1)S(1)}, bf16[256,384]{1,0:T(8,128)(2,1)S(1)}, u32[]{:S(2)}, u32[]{:S(2)}) collective-permute-start(bf16[256,384]{1,0:T(8,128)(2,1)S(1)} %get-tuple-element.51), channel_id=1, source_target_pairs={{0,4},{4,0},{1,5},{5,1},{2,6},{6,2},{3,7},{7,3},{8,12},{12,8},{9,1... | collective-permute-start | bytes 589832 | tf_op jit(solution)/shard_map/ppermute | solution.py:232
  83.9 8.4 %collective-permute-start.16 = (bf16[256,384]{1,0:T(8,128)(2,1)S(1)}, bf16[256,384]{1,0:T(8,128)(2,1)S(1)}, u32[]{:S(2)}, u32[]{:S(2)}) collective-permute-start(bf16[256,384]{1,0:T(8,128)(2,1)S(1)} %get-tuple-element.51), channel_id=1, source_target_pairs={{0,12},{4,8},{8,20},{12,16},{16,28},{20,24},{24,4},{28,0},{1,13},{... | collective-permute-start | bytes 589832 | tf_op jit(solution)/shard_map/ppermute | solution.py:237
  85.2 11.3 %collective-permute-start.11 = (bf16[256,384]{1,0:T(8,128)(2,1)S(1)}, bf16[256,384]{1,0:T(8,128)(2,1)S(1)}, u32[]{:S(2)}, u32[]{:S(2)}) collective-permute-start(bf16[256,384]{1,0:T(8,128)(2,1)S(1)} %collective-permute-done.10.refs_7_), channel_id=1, source_target_pairs={{0,8},{8,16},{16,24},{24,0},{1,9},{9,17},{17,25},{25,1},{2,10},{10... | collective-permute-start | bytes 589832 | tf_op jit(solution)/shard_map/ppermute | solution.py:232
  88.1 8.4 %collective-permute-start.13 = (bf16[256,384]{1,0:T(8,128)(2,1)S(1)}, bf16[256,384]{1,0:T(8,128)(2,1)S(1)}, u32[]{:S(2)}, u32[]{:S(2)}) collective-permute-start(bf16[256,384]{1,0:T(8,128)(2,1)S(1)} %collective-permute-done.12.refs_11_), channel_id=1, source_target_pairs={{0,24},{8,0},{16,8},{24,16},{1,25},{9,1},{17,9},{25,17},{2,26},{10... | collective-permute-start | bytes 589832 | tf_op jit(solution)/shard_map/ppermute | solution.py:232
  97.9 28.4 %copy-start.1 = (bf16[256,768]{1,0:T(8,128)(2,1)S(1)}, bf16[256,768]{1,0:T(8,128)(2,1)}, u32[]{:S(2)}) copy-start(bf16[256,768]{1,0:T(8,128)(2,1)} %get-tuple-element.59.d0) | copy-start | bytes 1179652
  97.9 23.0 %all-to-all-start.1 = ((bf16[8,96,384]{2,1,0:T(8,128)(2,1)}), bf16[8,96,384]{2,1,0:T(8,128)(2,1)S(1)}, u32[]{:S(2)}, u32[]{:S(2)}) async-start(bf16[8,96,384]{2,1,0:T(8,128)(2,1)} %grad_far.1), calls=%async_computation.1 | async-start | bytes 1179648 | tf_op jit(solution)/shard_map/all_to_all | solution.py:369
  101.6 24.6 %collective-permute-start.17 = (bf16[256,768]{1,0:T(8,128)(2,1)}, bf16[256,768]{1,0:T(8,128)(2,1)S(1)}, u32[]{:S(2)}, u32[]{:S(2)}) collective-permute-start(bf16[256,768]{1,0:T(8,128)(2,1)} %get-tuple-element.60), channel_id=1, source_target_pairs={{0,24},{8,0},{16,8},{24,16},{1,25},{9,1},{17,9},{25,17},{2,26},{10... | collective-permute-start | bytes 1179656 | tf_op jit(solution)/shard_map/ppermute | solution.py:232
  102.9 23.3 %collective-permute-start.18 = (bf16[256,768]{1,0:T(8,128)(2,1)}, bf16[256,768]{1,0:T(8,128)(2,1)S(1)}, u32[]{:S(2)}, u32[]{:S(2)}) collective-permute-start(bf16[256,768]{1,0:T(8,128)(2,1)} %get-tuple-element.61), channel_id=1, source_target_pairs={{0,16},{8,24},{16,0},{24,8},{1,17},{9,25},{17,1},{25,9},{2,18},{10... | collective-permute-start | bytes 1179656 | tf_op jit(solution)/shard_map/ppermute | solution.py:232
  104.2 22.1 %collective-permute-start.19 = (bf16[256,768]{1,0:T(8,128)(2,1)}, bf16[256,768]{1,0:T(8,128)(2,1)}, u32[]{:S(2)}, u32[]{:S(2)}) collective-permute-start(bf16[256,768]{1,0:T(8,128)(2,1)} %get-tuple-element.62), channel_id=1, source_target_pairs={{0,8},{8,16},{16,24},{24,0},{1,9},{9,17},{17,25},{25,1},{2,10},{10... | collective-permute-start | bytes 1179656 | tf_op jit(solution)/shard_map/ppermute | solution.py:232
  122.6 13.2 %all-to-all-start.2 = ((f32[8,48,128]{2,1,0:T(8,128)}), f32[8,48,128]{2,1,0:T(8,128)S(1)}, u32[]{:S(2)}, u32[]{:S(2)}) async-start(f32[8,48,128]{2,1,0:T(8,128)} %bitcast.32), calls=%async_computation.2 | async-start | bytes 393216 | tf_op jit(solution)/shard_map/all_to_all | solution.py:405
  135.9 4.0 %collective-permute-start.20 = (f32[48,128]{1,0:T(8,128)S(1)}, f32[48,128]{1,0:T(8,128)S(1)}, u32[]{:S(2)}, u32[]{:S(2)}) collective-permute-start(f32[48,128]{1,0:T(8,128)S(1)} %reduce_sum.9), channel_id=1, source_target_pairs={{0,8},{8,16},{16,24},{24,0},{1,9},{9,17},{17,25},{25,1},{2,10},{10... | collective-permute-start | bytes 73736 | tf_op jit(solution)/shard_map/ppermute | solution.py:232
  136.7 4.3 %collective-permute-start.21 = (f32[48,128]{1,0:T(8,128)S(1)}, f32[48,128]{1,0:T(8,128)S(1)}, u32[]{:S(2)}, u32[]{:S(2)}) collective-permute-start(f32[48,128]{1,0:T(8,128)S(1)} %reduce_sum.9), channel_id=1, source_target_pairs={{0,16},{8,24},{16,0},{24,8},{1,17},{9,25},{17,1},{25,9},{2,18},{10... | collective-permute-start | bytes 73736 | tf_op jit(solution)/shard_map/ppermute | solution.py:232
  137.2 3.9 %collective-permute-start.22 = (f32[48,128]{1,0:T(8,128)S(1)}, f32[48,128]{1,0:T(8,128)S(1)}, u32[]{:S(2)}, u32[]{:S(2)}) collective-permute-start(f32[48,128]{1,0:T(8,128)S(1)} %reduce_sum.9), channel_id=1, source_target_pairs={{0,24},{8,0},{16,8},{24,16},{1,25},{9,1},{17,9},{25,17},{2,26},{10... | collective-permute-start | bytes 73736 | tf_op jit(solution)/shard_map/ppermute | solution.py:232
  141.8 12.0 %all-to-all-start.3 = ((f32[8,48,128]{2,1,0:T(8,128)}), f32[8,48,128]{2,1,0:T(8,128)S(1)}, u32[]{:S(2)}, u32[]{:S(2)}) async-start(f32[8,48,128]{2,1,0:T(8,128)} %broadcast_in_dim.27), calls=%async_computation.3 | async-start | bytes 393216 | tf_op jit(solution)/shard_map/all_to_all | solution.py:409
  157.2 5.0 %collective-permute-start.23 = (f32[48,384]{1,0:T(8,128)S(1)}, f32[48,384]{1,0:T(8,128)S(1)}, u32[]{:S(2)}, u32[]{:S(2)}) collective-permute-start(f32[48,384]{1,0:T(8,128)S(1)} %get-tuple-element.79), channel_id=1, source_target_pairs={{0,4},{4,0},{1,5},{5,1},{2,6},{6,2},{3,7},{7,3},{8,12},{12,8},{9,1... | collective-permute-start | bytes 221192 | tf_op jit(solution)/shard_map/ppermute | solution.py:232
  (11 other events, 89.8 us)
Sparse Core Ops, SparseCore 0:
  9.8 49.0 all-gather.1

commit v4 on v3

--- a/solution.py
+++ b/solution.py
@@ -85,10 +85,15 @@
 
 def parts_kernel(cot_ref, weight_ref, *out_refs):
     weight = weight_ref[...]
-    for k, out_ref in enumerate(out_refs):
+    for k, out_ref in zip((0, 1, 3), out_refs):
         out_ref[...] = lax.dot_general(
             cot_ref[k], weight, (((0,), (0,)), ((), ())), preferred_element_type=f32
         ).astype(bf16)
+    far = lax.dot_general(
+        cot_ref[2], weight, (((0,), (0,)), ((), ())), preferred_element_type=f32
+    ).astype(bf16)
+    out_refs[3][...] = far[: ROWS // 2]
+    out_refs[4][...] = far[ROWS // 2 :]
 
 
 def soft(q, k, same):
@@ -209,12 +214,13 @@
     out_ref[:, pl.ds(pl.multiple_of((1 - core) * HALF, HD), HALF)] = there_ref[...]
 
 
-def backward_kernel(row_ref, col_ref, q_ref, k_ref, v_ref, d0, d1, d2, d3, *refs):
+def backward_kernel(row_ref, col_ref, q_ref, k_ref, v_ref, d0, d1, d3, d2a, d2b, *refs):
     gq_ref, gk_ref, gv_ref = refs[-3:]
     same = row_ref[...] == col_ref[...]
     q, k, v = q_ref[...], k_ref[...], v_ref[...]
+    d2 = jnp.concatenate([d2a[...], d2b[...]], axis=0)
     near = d0[...].astype(f32) + d1[...].astype(f32)
-    d_out = (near + (d2[...].astype(f32) + d3[...].astype(f32))).astype(bf16)
+    d_out = (near + (d2.astype(f32) + d3[...].astype(f32))).astype(bf16)
     prob = soft(q, k, same)
     first = (((0,), (0,)), ((), ()))
     gv_ref[...] = lax.dot_general(
@@ -309,8 +315,9 @@
 
     weight = lax.all_gather(out_weight, ("z", "c"), axis=0, tiled=True)
     part = array((ROWS, HEADS_HERE * HD), bf16)
+    some = array((ROWS // 2, HEADS_HERE * HD), bf16)
     work = pl.CostEstimate(flops=18 * 10**9, bytes_accessed=54 * 10**6, transcendentals=0)
-    d_parts = local(parts_kernel, "d_parts", (part,) * Y, cot_own, weight, room=60, cost_estimate=work)
+    d_parts = local(parts_kernel, "d_parts", (part,) * 3 + (some,) * 2, cot_own, weight, room=60, cost_estimate=work)
     arrived, cot_own, cot_other, *d_parts = lax.optimization_barrier(
         (arrived, cot_own, cot_other, *d_parts)
     )
@@ -365,7 +372,9 @@
         grad,
     )
     grad, *d_parts = lax.optimization_barrier((grad, *d_parts))
-    d_parts = [d_parts[0]] + [shift(d_parts[k], "y", -k) for k in range(1, Y)]
+    d_parts[3], d_parts[4] = shift(d_parts[3], "y", -1), shift(d_parts[4], "y", 1)
+    d_parts[1], d_parts[2] = shift(d_parts[1], "y", -1), shift(d_parts[2], "y", 1)
+    d_parts[3], d_parts[4] = shift(d_parts[3], "y", -1), shift(d_parts[4], "y", 1)
     parts = lax.all_to_all(grad, "z", split_axis=0, concat_axis=0, tiled=True)
 
     out = array((ROWS, HEADS_HERE * HD), bf16)
@@ -383,12 +392,13 @@
                 column(0),
                 column(HEADS_HERE),
                 column(2 * HEADS_HERE),
-                *[column(0)] * Y,
+                *[column(0)] * 3,
+                *[pl.BlockSpec((ROWS // 2, HD), lambda h: (0, heads + h))] * 2,
                 *[pl.BlockSpec(memory_space=pl.ANY)] * len(held),
             ],
             out_specs=(column(0),) * 3,
             out_shape=(out,) * 3,
-            input_output_aliases={5 + Y + n: n for n in range(len(held))},
+            input_output_aliases={10 + n: n for n in range(len(held))},
             compiler_params=pltpu.CompilerParams(vmem_limit_bytes=24 * 1024 * 1024),
             name="backward",
         )(seg_row, seg_col, packed, packed, packed, *d_parts, *held)

time: 170 us -> 176 us (1.035)
  starting transfers between devices: 56.5 us -> 65 us
    ppermute x22 -> x25, starting transfers between devices: 29.3 us -> 35.1 us  [shift(): lax.ppermute(field, axis, [(i, (i + step) % size) for i in range(size)])]
    all_to_all x1, waiting for transfers between devices: 4.87 us -> 0.01 us  [shards(): lax.all_to_all(gram, 'z', split_axis=0, concat_axis=0, tiled=True)]
    ppermute x22 -> x25, waiting for transfers between devices: 22.8 us -> 26.7 us  [shift(): lax.ppermute(field, axis, [(i, (i + step) % size) for i in range(size)])]
    all_to_all x1, starting transfers between devices: 3.39 us -> 6.17 us  [shards(): gram = lax.all_to_all(gram, 'z', split_axis=0, concat_axis=0, tiled=True)]
  transfers between devices with their start and end apart: 29 -> 32, of which waited for: 17 -> 17; matrix products, arithmetic and copies ran while one was open for 2% -> 2% of each run, Pallas kernels for 13% -> 12%
where the time goes in v4:
time: 176 us; the launch traced here: 175 us
  starting transfers between devices  65 us (37%)
  waiting for transfers between devices  60.8 us (35%)
  Pallas kernels  27.5 us (16%)
  between operations  14.3 us (8%)
  local copies, waits for them, and re-layouts  6.86 us (4%)
    ppermute x25, starting transfers between devices, shift(): lax.ppermute(field, axis, [(i, (i + step) % size) for i in range(size)])  35.1 us
    ppermute x25, waiting for transfers between devices, shift(): lax.ppermute(field, axis, [(i, (i + step) % size) for i in range(size)])  26.7 us
    pallas_call x9, Pallas kernels, local(): pl.pallas_call(kernel, in_specs=[smem] * scalars + [hbm] * far + [vmem] *...  19.5 us
    all_to_all x1, waiting for transfers between devices, shards(): parts = lax.all_to_all(grad, 'z', split_axis=0, concat_axis=0, tiled=True)  15.2 us
    all_to_all x1, starting transfers between devices, shards(): lax.all_to_all(slots, everything, split_axis=0, concat_axis=0, tiled=True)  13.2 us
    all_to_all x1, waiting for transfers between devices, shards(): lax.all_to_all(slots, everything, split_axis=0, concat_axis=0, tiled=True)  10.6 us
    pallas_call x2, Pallas kernels, backward(): pl.pallas_call(backward_kernel, grid=(3,), in_specs=[pl.BlockSpec((1, ROW...  8.01 us
    all_to_all x1, starting transfers between devices, shards(): gram = lax.all_to_all(gram, 'z', split_axis=0, concat_axis=0, tiled=True)  6.17 us
  transfers between devices with their start and end apart: 32, of which 17 were waited for; matrix products, arithmetic and copies ran while one was open for 2% of the time, Pallas kernels for 12%

profile of v4, /device:TPU:1, one launch (start us, length us, event | category | flops | bytes accessed | tf_op | source)
XLA Modules:
  0.0 175.2 jit_solution(5150863855008930662)
XLA Ops:
  7.9 4.2 %place.1 = bf16[64,112,128]{2,1,0:T(8,128)(2,1)} custom-call(bf16[256,768]{1,0:T(8,128)(2,1)} %q_hbm.1, bf16[256,768]{1,0:T(8,128)(2,1)} %k_hbm.1, bf16[256,768]{1,0:T(8,128)(2,1)} %v_hbm.1, s32[1,256]{1,0:T(1,128)} %bitcast.42), custom_call_target="tpu_custom_call" | custom-call | tf_op jit(solution)/shard_map/place/pallas_call | solution.py:250
  12.1 13.2 %all-to-all-start = ((bf16[64,112,128]{2,1,0:T(8,128)(2,1)}), bf16[64,112,128]{2,1,0:T(8,128)(2,1)S(1)}, u32[]{:S(2)}, u32[]{:S(2)}) async-start(bf16[64,112,128]{2,1,0:T(8,128)(2,1)} %place.1), calls=%async_computation | async-start | bytes 3670016 | tf_op jit(solution)/shard_map/all_to_all | solution.py:282
  26.3 3.0 %collective-permute-start.4 = (bf16[192,256]{1,0:T(8,128)(2,1)S(1)}, bf16[192,256]{1,0:T(8,128)(2,1)S(1)}, u32[]{:S(2)}, u32[]{:S(2)}) collective-permute-start(bf16[192,256]{1,0:T(8,128)(2,1)S(1)} %get-tuple-element.94), channel_id=1, source_target_pairs={{0,16},{8,24},{16,0},{24,8},{1,17},{9,25},{17,1},{25,9},{2,18},{10... | collective-permute-start | bytes 294920 | tf_op jit(solution)/shard_map/ppermute | solution.py:238
  30.7 3.7 %collective-permute-done.4 = bf16[192,256]{1,0:T(8,128)(2,1)S(1)} collective-permute-done((bf16[192,256]{1,0:T(8,128)(2,1)S(1)}, bf16[192,256]{1,0:T(8,128)(2,1)S(1)}, u32[]{:S(2)}, u32[]{:S(2)}) %collective-permute-start.4) | collective-permute-done | bytes 98336 | tf_op jit(solution)/shard_map/ppermute | solution.py:238
  34.4 3.9 %collective-permute-done.5 = bf16[192,256]{1,0:T(8,128)(2,1)S(1)} collective-permute-done((bf16[192,256]{1,0:T(8,128)(2,1)S(1)}, bf16[192,256]{1,0:T(8,128)(2,1)S(1)}, u32[]{:S(2)}, u32[]{:S(2)}) %collective-permute-start.5) | collective-permute-done | bytes 98336 | tf_op jit(solution)/shard_map/ppermute | solution.py:238
  38.3 2.6 %collective-permute-start.7 = (bf16[2,192,256]{2,1,0:T(8,128)(2,1)S(1)}, bf16[2,192,256]{2,1,0:T(8,128)(2,1)S(1)}, u32[]{:S(2)}, u32[]{:S(2)}) collective-permute-start(bf16[2,192,256]{2,1,0:T(8,128)(2,1)S(1)} %pad_maximum_fusion.1.refs_4_), channel_id=1, source_target_pairs={{0,3},{1,0},{2,1},{3,2},{4,7},{5,4},{6,5},{7,6},{8,11},{9,8},{10,9... | collective-permute-start | bytes 589832 | tf_op jit(solution)/shard_map/ppermute | solution.py:238
  41.8 2.0 %collective-permute-start.3 = (bf16[2,192,256]{2,1,0:T(8,128)(2,1)S(1)}, bf16[2,192,256]{2,1,0:T(8,128)(2,1)}, u32[]{:S(2)}, u32[]{:S(2)}) collective-permute-start(bf16[2,192,256]{2,1,0:T(8,128)(2,1)S(1)} %pad_maximum_fusion.refs_0_), channel_id=1, source_target_pairs={{0,3},{1,0},{2,1},{3,2},{4,7},{5,4},{6,5},{7,6},{8,11},{9,8},{10,9... | collective-permute-start | bytes 589832 | tf_op jit(solution)/shard_map/ppermute | solution.py:238
  44.9 3.4 %collective-permute-start.8 = (bf16[2,192,256]{2,1,0:T(8,128)(2,1)S(1)}, bf16[2,192,256]{2,1,0:T(8,128)(2,1)}, u32[]{:S(2)}, u32[]{:S(2)}) collective-permute-start(bf16[2,192,256]{2,1,0:T(8,128)(2,1)S(1)} %collective-permute-done.7.refs_7_), channel_id=1, source_target_pairs={{0,3},{1,0},{2,1},{3,2},{4,7},{5,4},{6,5},{7,6},{8,11},{9,8},{10,9... | collective-permute-start | bytes 589832 | tf_op jit(solution)/shard_map/ppermute | solution.py:238
  49.2 3.1 %collective-permute-done.6.refs_5_ = bf16[2,192,256]{2,1,0:T(8,128)(2,1)S(1)} collective-permute-done((bf16[2,192,256]{2,1,0:T(8,128)(2,1)S(1)}, bf16[2,192,256]{2,1,0:T(8,128)(2,1)S(1)}, u32[]{:S(2)}, u32[]{:S(2)}) %collective-permute-start.6) | collective-permute-done | bytes 196640 | tf_op jit(solution)/shard_map/ppermute | solution.py:238
  53.1 2.9 %collective-permute-done.2.refs_2_ = bf16[2,192,256]{2,1,0:T(8,128)(2,1)} collective-permute-done((bf16[2,192,256]{2,1,0:T(8,128)(2,1)S(1)}, bf16[2,192,256]{2,1,0:T(8,128)(2,1)}, u32[]{:S(2)}, u32[]{:S(2)}) %collective-permute-start.2) | collective-permute-done | bytes 196640 | tf_op jit(solution)/shard_map/ppermute | solution.py:238
  56.0 2.7 %join_cot.1.cot_ref = bf16[4,768,256]{2,1,0:T(8,128)(2,1)} custom-call(s32[1]{0:T(128)} %bitcast.1.x_ref, bf16[2,192,256]{2,1,0:T(8,128)(2,1)} %copy-done.10, bf16[2,192,256]{2,1,0:T(8,128)(2,1)} %copy-done.12, bf16[2,192,256]{2,1,0:T(8,128)(2,1)} %collective-permute-done.2.refs_2_, bf16[2,192,256]{2,1,0:T(8,128)(2,1)} %collective-permute-done.3.refs_3_, ...), custom_call_target="tpu_custom_call" | custom-call | tf_op jit(solution)/shard_map/join_cot/pallas_call | solution.py:250
  58.7 2.2 %collective-permute-start.9 = (bf16[4,768,256]{2,1,0:T(8,128)(2,1)}, bf16[4,768,256]{2,1,0:T(8,128)(2,1)}, u32[]{:S(2)}, u32[]{:S(2)}) collective-permute-start(bf16[4,768,256]{2,1,0:T(8,128)(2,1)} %join_cot.1.cot_ref), channel_id=1, source_target_pairs={{0,4},{4,0},{1,5},{5,1},{2,6},{6,2},{3,7},{7,3},{8,12},{12,8},{9,1... | collective-permute-start | bytes 4718600 | tf_op jit(solution)/shard_map/ppermute | solution.py:238
  60.9 3.9 %d_parts.1 = (bf16[256,768]{1,0:T(8,128)(2,1)}, bf16[256,768]{1,0:T(8,128)(2,1)}, bf16[256,768]{1,0:T(8,128)(2,1)}, bf16[128,768]{1,0:T(8,128)(2,1)}, bf16[128,768]{1,0:T(8,128)(2,1)}) custom-call(bf16[4,768,256]{2,1,0:T(8,128)(2,1)} %join_cot.1.cot_ref, bf16[768,768]{1,0:T(8,128)(2,1)} %all-gather.2.cloned.1.call-done.weight_ref), custom_call_target="tpu_custom_call" | custom-call | flops 17999998976 | bytes 54000000 | tf_op jit(solution)/shard_map/d_parts/pallas_call | solution.py:250
  64.8 10.6 %all-to-all-done.slots_ref = bf16[64,112,128]{2,1,0:T(8,128)(2,1)S(1)} async-done(((bf16[64,112,128]{2,1,0:T(8,128)(2,1)}), bf16[64,112,128]{2,1,0:T(8,128)(2,1)S(1)}, u32[]{:S(2)}, u32[]{:S(2)}) %all-to-all-start) | async-done | bytes 1835040 | tf_op jit(solution)/shard_map/all_to_all | solution.py:282
  76.2 2.3 %forward.1 = (bf16[256,2304]{1,0:T(8,128)(2,1)S(1)}, bf16[256,384]{1,0:T(8,128)(2,1)S(1)}, bf16[256,384]{1,0:T(8,128)(2,1)S(1)}) custom-call(s32[1]{0:T(128)} %bitcast.8.core_ref, bf16[64,112,128]{2,1,0:T(8,128)(2,1)S(1)} %all-to-all-done.slots_ref, s32[1,256]{1,0:T(1,128)S(1)} %bitcast.38, s32[256,1]{1,0:T(8,128)S(1)} %copy-done.2, s32[1,256]{1,0:T(1,128)S(1)} %bitcast.34, ...), custom_call_target="tpu_custom_call" | custom-call | tf_op jit(solution)/shard_map/forward/pallas_call | solution.py:250
  79.9 2.8 %collective-permute-start.12 = (bf16[256,384]{1,0:T(8,128)(2,1)S(1)}, bf16[256,384]{1,0:T(8,128)(2,1)S(1)}, u32[]{:S(2)}, u32[]{:S(2)}) collective-permute-start(bf16[256,384]{1,0:T(8,128)(2,1)S(1)} %get-tuple-element.55), channel_id=1, source_target_pairs={{0,28},{4,24},{8,4},{12,0},{16,12},{20,8},{24,20},{28,16},{1,29},{... | collective-permute-start | bytes 589832 | tf_op jit(solution)/shard_map/ppermute | solution.py:243
  85.1 3.0 %collective-permute-done.12.refs_11_ = bf16[256,384]{1,0:T(8,128)(2,1)S(1)} collective-permute-done((bf16[256,384]{1,0:T(8,128)(2,1)S(1)}, bf16[256,384]{1,0:T(8,128)(2,1)S(1)}, u32[]{:S(2)}, u32[]{:S(2)}) %collective-permute-start.12) | collective-permute-done | bytes 196640 | tf_op jit(solution)/shard_map/ppermute | solution.py:243
  89.3 1.8 %slice_bitcast_fusion = (bf16[768,256]{1,0:T(8,128)(2,1)S(1)}, bf16[768,256]{1,0:T(8,128)(2,1)S(1)}, bf16[768,256]{1,0:T(8,128)(2,1)S(1)}, bf16[768,256]{1,0:T(8...) fusion(bf16[4,768,256]{2,1,0:T(8,128)(2,1)} %collective-permute, ...), kind=kLoop, calls=%fused_computation.4 | loop fusion | bytes 6291456 | tf_op jit(solution)/shard_map/squeeze | solution.py:356
  93.7 2.8 %collective-permute-done.11.own_far = bf16[256,384]{1,0:T(8,128)(2,1)S(1)} collective-permute-done((bf16[256,384]{1,0:T(8,128)(2,1)S(1)}, bf16[256,384]{1,0:T(8,128)(2,1)S(1)}, u32[]{:S(2)}, u32[]{:S(2)}) %collective-permute-start.11) | collective-permute-done | bytes 196640 | tf_op jit(solution)/shard_map/ppermute | solution.py:238
  96.5 1.4 grad_far.1
  97.9 3.7 %all-to-all-start.1 = ((bf16[8,96,384]{2,1,0:T(8,128)(2,1)}), bf16[8,96,384]{2,1,0:T(8,128)(2,1)S(1)}, u32[]{:S(2)}, u32[]{:S(2)}) async-start(bf16[8,96,384]{2,1,0:T(8,128)(2,1)} %grad_far.1), calls=%async_computation.1 | async-start | bytes 1179648 | tf_op jit(solution)/shard_map/all_to_all | solution.py:378
  103.2 2.5 %collective-permute-start.17 = (bf16[256,768]{1,0:T(8,128)(2,1)}, bf16[256,768]{1,0:T(8,128)(2,1)S(1)}, u32[]{:S(2)}, u32[]{:S(2)}) collective-permute-start(bf16[256,768]{1,0:T(8,128)(2,1)} %get-tuple-element.65), channel_id=1, source_target_pairs={{0,24},{8,0},{16,8},{24,16},{1,25},{9,1},{17,9},{25,17},{2,26},{10... | collective-permute-start | bytes 1179656 | tf_op jit(solution)/shard_map/ppermute | solution.py:238
  105.7 15.2 %all-to-all-done.1.parts_ref = bf16[8,96,384]{2,1,0:T(8,128)(2,1)S(1)} async-done(((bf16[8,96,384]{2,1,0:T(8,128)(2,1)}), bf16[8,96,384]{2,1,0:T(8,128)(2,1)S(1)}, u32[]{:S(2)}, u32[]{:S(2)}) %all-to-all-start.1) | async-done | bytes 589856 | tf_op jit(solution)/shard_map/all_to_all | solution.py:378
  122.6 3.4 %all-to-all-start.2 = ((f32[8,48,128]{2,1,0:T(8,128)}), f32[8,48,128]{2,1,0:T(8,128)S(1)}, u32[]{:S(2)}, u32[]{:S(2)}) async-start(f32[8,48,128]{2,1,0:T(8,128)} %bitcast.32), calls=%async_computation.2 | async-start | bytes 393216 | tf_op jit(solution)/shard_map/all_to_all | solution.py:415
  127.6 4.7 %collective-permute-done.20.d2a = bf16[128,768]{1,0:T(8,128)(2,1)S(1)} collective-permute-done((bf16[128,768]{1,0:T(8,128)(2,1)}, bf16[128,768]{1,0:T(8,128)(2,1)S(1)}, u32[]{:S(2)}, u32[]{:S(2)}) %collective-permute-start.20) | collective-permute-done | bytes 196640 | tf_op jit(solution)/shard_map/ppermute | solution.py:238
  132.5 4.0 %backward.2 = (bf16[256,768]{1,0:T(8,128)(2,1)}, bf16[256,768]{1,0:T(8,128)(2,1)}, bf16[256,768]{1,0:T(8,128)(2,1)}) custom-call(s32[1,256]{1,0:T(1,128)S(1)} %bitcast.35, s32[256,1]{1,0:T(8,128)S(1)} %copy.16.col_ref, bf16[256,2304]{1,0:T(8,128)(2,1)S(1)} %get-tuple-element.63.q_ref.k_ref.v_ref, bf16[256,2304]{1,0:T(8,128)(2,1)S(1)} %get-tuple-element.63.q_ref.k_ref.v_ref, ...), custom_call_target="tpu_custom_call" | custom-call | tf_op jit(solution)/shard_map/backward/pallas_call | solution.py:386
  138.7 2.0 %collective-permute-start.25 = (f32[48,128]{1,0:T(8,128)S(1)}, f32[48,128]{1,0:T(8,128)S(1)}, u32[]{:S(2)}, u32[]{:S(2)}) collective-permute-start(f32[48,128]{1,0:T(8,128)S(1)} %reduce_sum.9), channel_id=1, source_target_pairs={{0,24},{8,0},{16,8},{24,16},{1,25},{9,1},{17,9},{25,17},{2,26},{10... | collective-permute-start | bytes 73736 | tf_op jit(solution)/shard_map/ppermute | solution.py:238
  142.4 6.2 %all-to-all-start.3 = ((f32[8,48,128]{2,1,0:T(8,128)}), f32[8,48,128]{2,1,0:T(8,128)S(1)}, u32[]{:S(2)}, u32[]{:S(2)}) async-start(f32[8,48,128]{2,1,0:T(8,128)} %broadcast_in_dim.27), calls=%async_computation.3 | async-start | bytes 393216 | tf_op jit(solution)/shard_map/all_to_all | solution.py:419
  148.6 4.0 %backward.3 = (bf16[256,768]{1,0:T(8,128)(2,1)}, bf16[256,768]{1,0:T(8,128)(2,1)}, bf16[256,768]{1,0:T(8,128)(2,1)}) custom-call(s32[1,256]{1,0:T(1,128)S(1)} %bitcast.36, s32[256,1]{1,0:T(8,128)S(1)} %copy.16.col_ref, bf16[256,2304]{1,0:T(8,128)(2,1)S(1)} %get-tuple-element.63.q_ref.k_ref.v_ref, ...), custom_call_target="tpu_custom_call", output_to_operand_aliasing={{0}: (10, {}), {1}: (11, {}), {2}: (12, {})} | custom-call | tf_op jit(solution)/shard_map/backward/pallas_call | solution.py:386
  152.6 4.6 %all-to-all-done.3 = f32[8,48,128]{2,1,0:T(8,128)S(1)} async-done(((f32[8,48,128]{2,1,0:T(8,128)}), f32[8,48,128]{2,1,0:T(8,128)S(1)}, u32[]{:S(2)}, u32[]{:S(2)}) %all-to-all-start.3) | async-done | bytes 196640 | tf_op jit(solution)/shard_map/all_to_all | solution.py:419
  158.2 2.5 %update.1 = (f32[48,384]{1,0:T(8,128)S(1)}, f32[48,384]{1,0:T(8,128)S(1)}) custom-call(s32[1]{0:T(128)} %bitcast.8.core_ref, f32[384,128]{1,0:T(8,128)S(1)} %bitcast.31, f32[96,384]{1,0:T(8,128)S(1)} %copy-done.5), custom_call_target="tpu_custom_call" | custom-call | tf_op jit(solution)/shard_map/update/pallas_call | solution.py:250
  160.6 6.1 %collective-permute-start.26 = (f32[48,384]{1,0:T(8,128)S(1)}, f32[48,384]{1,0:T(8,128)S(1)}, u32[]{:S(2)}, u32[]{:S(2)}) collective-permute-start(f32[48,384]{1,0:T(8,128)S(1)} %get-tuple-element.85), channel_id=1, source_target_pairs={{0,4},{4,0},{1,5},{5,1},{2,6},{6,2},{3,7},{7,3},{8,12},{12,8},{9,1... | collective-permute-start | bytes 221192 | tf_op jit(solution)/shard_map/ppermute | solution.py:238
  (89 shorter events, 26.6 us)
Async XLA Ops:
  7.2 53.7 %all-gather.2.cloned.1.call-start = ((), (), s32[]{:S(2)}) async-start(), calls=%async_computation.4 | async-start | bytes 1253376 | tf_op jit(solution)/shard_map/all_gather | solution.py:316
  12.1 63.2 %all-to-all-start = ((bf16[64,112,128]{2,1,0:T(8,128)(2,1)}), bf16[64,112,128]{2,1,0:T(8,128)(2,1)S(1)}, u32[]{:S(2)}, u32[]{:S(2)}) async-start(bf16[64,112,128]{2,1,0:T(8,128)(2,1)} %place.1), calls=%async_computation | async-start | bytes 3670016 | tf_op jit(solution)/shard_map/all_to_all | solution.py:282
  26.3 8.1 %collective-permute-start.4 = (bf16[192,256]{1,0:T(8,128)(2,1)S(1)}, bf16[192,256]{1,0:T(8,128)(2,1)S(1)}, u32[]{:S(2)}, u32[]{:S(2)}) collective-permute-start(bf16[192,256]{1,0:T(8,128)(2,1)S(1)} %get-tuple-element.94), channel_id=1, source_target_pairs={{0,16},{8,24},{16,0},{24,8},{1,17},{9,25},{17,1},{25,9},{2,18},{10... | collective-permute-start | bytes 294920 | tf_op jit(solution)/shard_map/ppermute | solution.py:238
  29.2 9.0 %collective-permute-start.5 = (bf16[192,256]{1,0:T(8,128)(2,1)S(1)}, bf16[192,256]{1,0:T(8,128)(2,1)S(1)}, u32[]{:S(2)}, u32[]{:S(2)}) collective-permute-start(bf16[192,256]{1,0:T(8,128)(2,1)S(1)} %get-tuple-element.95), channel_id=1, source_target_pairs={{0,24},{8,0},{16,8},{24,16},{1,25},{9,1},{17,9},{25,17},{2,26},{10... | collective-permute-start | bytes 294920 | tf_op jit(solution)/shard_map/ppermute | solution.py:238
  30.1 10.8 %collective-permute-start = (bf16[192,256]{1,0:T(8,128)(2,1)S(1)}, bf16[192,256]{1,0:T(8,128)(2,1)S(1)}, u32[]{:S(2)}, u32[]{:S(2)}) collective-permute-start(bf16[192,256]{1,0:T(8,128)(2,1)S(1)} %get-tuple-element.96), channel_id=1, source_target_pairs={{0,8},{8,16},{16,24},{24,0},{1,9},{9,17},{17,25},{25,1},{2,10},{10... | collective-permute-start | bytes 294920 | tf_op jit(solution)/shard_map/ppermute | solution.py:238
  38.3 6.5 %collective-permute-start.7 = (bf16[2,192,256]{2,1,0:T(8,128)(2,1)S(1)}, bf16[2,192,256]{2,1,0:T(8,128)(2,1)S(1)}, u32[]{:S(2)}, u32[]{:S(2)}) collective-permute-start(bf16[2,192,256]{2,1,0:T(8,128)(2,1)S(1)} %pad_maximum_fusion.1.refs_4_), channel_id=1, source_target_pairs={{0,3},{1,0},{2,1},{3,2},{4,7},{5,4},{6,5},{7,6},{8,11},{9,8},{10,9... | collective-permute-start | bytes 589832 | tf_op jit(solution)/shard_map/ppermute | solution.py:238
  41.0 7.3 %collective-permute-start.1 = (bf16[2,192,256]{2,1,0:T(8,128)(2,1)S(1)}, bf16[2,192,256]{2,1,0:T(8,128)(2,1)S(1)}, u32[]{:S(2)}, u32[]{:S(2)}) collective-permute-start(bf16[2,192,256]{2,1,0:T(8,128)(2,1)S(1)} %pad_maximum_fusion.refs_0_), channel_id=1, source_target_pairs={{0,1},{1,2},{2,3},{3,0},{4,5},{5,6},{6,7},{7,4},{8,9},{9,10},{10,1... | collective-permute-start | bytes 589832 | tf_op jit(solution)/shard_map/ppermute | solution.py:238
  41.1 11.3 %collective-permute-start.6 = (bf16[2,192,256]{2,1,0:T(8,128)(2,1)S(1)}, bf16[2,192,256]{2,1,0:T(8,128)(2,1)S(1)}, u32[]{:S(2)}, u32[]{:S(2)}) collective-permute-start(bf16[2,192,256]{2,1,0:T(8,128)(2,1)S(1)} %pad_maximum_fusion.1.refs_4_), channel_id=1, source_target_pairs={{0,1},{1,2},{2,3},{3,0},{4,5},{5,6},{6,7},{7,4},{8,9},{9,10},{10,1... | collective-permute-start | bytes 589832 | tf_op jit(solution)/shard_map/ppermute | solution.py:238
  41.8 10.6 %collective-permute-start.3 = (bf16[2,192,256]{2,1,0:T(8,128)(2,1)S(1)}, bf16[2,192,256]{2,1,0:T(8,128)(2,1)}, u32[]{:S(2)}, u32[]{:S(2)}) collective-permute-start(bf16[2,192,256]{2,1,0:T(8,128)(2,1)S(1)} %pad_maximum_fusion.refs_0_), channel_id=1, source_target_pairs={{0,3},{1,0},{2,1},{3,2},{4,7},{5,4},{6,5},{7,6},{8,11},{9,8},{10,9... | collective-permute-start | bytes 589832 | tf_op jit(solution)/shard_map/ppermute | solution.py:238
  44.9 8.3 %collective-permute-start.8 = (bf16[2,192,256]{2,1,0:T(8,128)(2,1)S(1)}, bf16[2,192,256]{2,1,0:T(8,128)(2,1)}, u32[]{:S(2)}, u32[]{:S(2)}) collective-permute-start(bf16[2,192,256]{2,1,0:T(8,128)(2,1)S(1)} %collective-permute-done.7.refs_7_), channel_id=1, source_target_pairs={{0,3},{1,0},{2,1},{3,2},{4,7},{5,4},{6,5},{7,6},{8,11},{9,8},{10,9... | collective-permute-start | bytes 589832 | tf_op jit(solution)/shard_map/ppermute | solution.py:238
  48.3 7.7 %collective-permute-start.2 = (bf16[2,192,256]{2,1,0:T(8,128)(2,1)S(1)}, bf16[2,192,256]{2,1,0:T(8,128)(2,1)}, u32[]{:S(2)}, u32[]{:S(2)}) collective-permute-start(bf16[2,192,256]{2,1,0:T(8,128)(2,1)S(1)} %collective-permute-done.1.refs_1_), channel_id=1, source_target_pairs={{0,1},{1,2},{2,3},{3,0},{4,5},{5,6},{6,7},{7,4},{8,9},{9,10},{10,1... | collective-permute-start | bytes 589832 | tf_op jit(solution)/shard_map/ppermute | solution.py:238
  58.7 6.1 %collective-permute-start.9 = (bf16[4,768,256]{2,1,0:T(8,128)(2,1)}, bf16[4,768,256]{2,1,0:T(8,128)(2,1)}, u32[]{:S(2)}, u32[]{:S(2)}) collective-permute-start(bf16[4,768,256]{2,1,0:T(8,128)(2,1)} %join_cot.1.cot_ref), channel_id=1, source_target_pairs={{0,4},{4,0},{1,5},{5,1},{2,6},{6,2},{3,7},{7,3},{8,12},{12,8},{9,1... | collective-permute-start | bytes 4718600 | tf_op jit(solution)/shard_map/ppermute | solution.py:238
  78.6 6.5 %collective-permute-start.10 = (bf16[256,384]{1,0:T(8,128)(2,1)S(1)}, bf16[256,384]{1,0:T(8,128)(2,1)S(1)}, u32[]{:S(2)}, u32[]{:S(2)}) collective-permute-start(bf16[256,384]{1,0:T(8,128)(2,1)S(1)} %get-tuple-element.54.refs_6_), channel_id=1, source_target_pairs={{0,8},{8,16},{16,24},{24,0},{1,9},{9,17},{17,25},{25,1},{2,10},{10... | collective-permute-start | bytes 589832 | tf_op jit(solution)/shard_map/ppermute | solution.py:238
  79.9 8.2 %collective-permute-start.12 = (bf16[256,384]{1,0:T(8,128)(2,1)S(1)}, bf16[256,384]{1,0:T(8,128)(2,1)S(1)}, u32[]{:S(2)}, u32[]{:S(2)}) collective-permute-start(bf16[256,384]{1,0:T(8,128)(2,1)S(1)} %get-tuple-element.55), channel_id=1, source_target_pairs={{0,28},{4,24},{8,4},{12,0},{16,12},{20,8},{24,20},{28,16},{1,29},{... | collective-permute-start | bytes 589832 | tf_op jit(solution)/shard_map/ppermute | solution.py:243
  82.7 9.6 %collective-permute-start.14 = (bf16[256,384]{1,0:T(8,128)(2,1)S(1)}, bf16[256,384]{1,0:T(8,128)(2,1)S(1)}, u32[]{:S(2)}, u32[]{:S(2)}) collective-permute-start(bf16[256,384]{1,0:T(8,128)(2,1)S(1)} %get-tuple-element.54.refs_6_), channel_id=1, source_target_pairs={{0,24},{8,0},{16,8},{24,16},{1,25},{9,1},{17,9},{25,17},{2,26},{10... | collective-permute-start | bytes 589832 | tf_op jit(solution)/shard_map/ppermute | solution.py:238
  83.9 8.4 %collective-permute-start.15 = (bf16[256,384]{1,0:T(8,128)(2,1)S(1)}, bf16[256,384]{1,0:T(8,128)(2,1)S(1)}, u32[]{:S(2)}, u32[]{:S(2)}) collective-permute-start(bf16[256,384]{1,0:T(8,128)(2,1)S(1)} %get-tuple-element.55), channel_id=1, source_target_pairs={{0,4},{4,0},{1,5},{5,1},{2,6},{6,2},{3,7},{7,3},{8,12},{12,8},{9,1... | collective-permute-start | bytes 589832 | tf_op jit(solution)/shard_map/ppermute | solution.py:238
  83.9 8.4 %collective-permute-start.16 = (bf16[256,384]{1,0:T(8,128)(2,1)S(1)}, bf16[256,384]{1,0:T(8,128)(2,1)S(1)}, u32[]{:S(2)}, u32[]{:S(2)}) collective-permute-start(bf16[256,384]{1,0:T(8,128)(2,1)S(1)} %get-tuple-element.55), channel_id=1, source_target_pairs={{0,12},{4,8},{8,20},{12,16},{16,28},{20,24},{24,4},{28,0},{1,13},{... | collective-permute-start | bytes 589832 | tf_op jit(solution)/shard_map/ppermute | solution.py:243
  85.1 11.4 %collective-permute-start.11 = (bf16[256,384]{1,0:T(8,128)(2,1)S(1)}, bf16[256,384]{1,0:T(8,128)(2,1)S(1)}, u32[]{:S(2)}, u32[]{:S(2)}) collective-permute-start(bf16[256,384]{1,0:T(8,128)(2,1)S(1)} %collective-permute-done.10.refs_7_), channel_id=1, source_target_pairs={{0,8},{8,16},{16,24},{24,0},{1,9},{9,17},{17,25},{25,1},{2,10},{10... | collective-permute-start | bytes 589832 | tf_op jit(solution)/shard_map/ppermute | solution.py:238
  88.1 8.4 %collective-permute-start.13 = (bf16[256,384]{1,0:T(8,128)(2,1)S(1)}, bf16[256,384]{1,0:T(8,128)(2,1)S(1)}, u32[]{:S(2)}, u32[]{:S(2)}) collective-permute-start(bf16[256,384]{1,0:T(8,128)(2,1)S(1)} %collective-permute-done.12.refs_11_), channel_id=1, source_target_pairs={{0,24},{8,0},{16,8},{24,16},{1,25},{9,1},{17,9},{25,17},{2,26},{10... | collective-permute-start | bytes 589832 | tf_op jit(solution)/shard_map/ppermute | solution.py:238
  97.9 23.0 %all-to-all-start.1 = ((bf16[8,96,384]{2,1,0:T(8,128)(2,1)}), bf16[8,96,384]{2,1,0:T(8,128)(2,1)S(1)}, u32[]{:S(2)}, u32[]{:S(2)}) async-start(bf16[8,96,384]{2,1,0:T(8,128)(2,1)} %grad_far.1), calls=%async_computation.1 | async-start | bytes 1179648 | tf_op jit(solution)/shard_map/all_to_all | solution.py:378
  101.6 24.4 %collective-permute-start.19 = (bf16[128,768]{1,0:T(8,128)(2,1)}, bf16[128,768]{1,0:T(8,128)(2,1)}, u32[]{:S(2)}, u32[]{:S(2)}) collective-permute-start(bf16[128,768]{1,0:T(8,128)(2,1)} %get-tuple-element.67), channel_id=1, source_target_pairs={{0,24},{8,0},{16,8},{24,16},{1,25},{9,1},{17,9},{25,17},{2,26},{10... | collective-permute-start | bytes 589832 | tf_op jit(solution)/shard_map/ppermute | solution.py:238
  103.0 23.3 %collective-permute-start.21 = (bf16[128,768]{1,0:T(8,128)(2,1)}, bf16[128,768]{1,0:T(8,128)(2,1)}, u32[]{:S(2)}, u32[]{:S(2)}) collective-permute-start(bf16[128,768]{1,0:T(8,128)(2,1)} %get-tuple-element.68), channel_id=1, source_target_pairs={{0,8},{8,16},{16,24},{24,0},{1,9},{9,17},{17,25},{25,1},{2,10},{10... | collective-permute-start | bytes 589832 | tf_op jit(solution)/shard_map/ppermute | solution.py:238
  103.2 29.3 %collective-permute-start.17 = (bf16[256,768]{1,0:T(8,128)(2,1)}, bf16[256,768]{1,0:T(8,128)(2,1)S(1)}, u32[]{:S(2)}, u32[]{:S(2)}) collective-permute-start(bf16[256,768]{1,0:T(8,128)(2,1)} %get-tuple-element.65), channel_id=1, source_target_pairs={{0,24},{8,0},{16,8},{24,16},{1,25},{9,1},{17,9},{25,17},{2,26},{10... | collective-permute-start | bytes 1179656 | tf_op jit(solution)/shard_map/ppermute | solution.py:238
  105.7 26.8 %collective-permute-start.18 = (bf16[256,768]{1,0:T(8,128)(2,1)}, bf16[256,768]{1,0:T(8,128)(2,1)S(1)}, u32[]{:S(2)}, u32[]{:S(2)}) collective-permute-start(bf16[256,768]{1,0:T(8,128)(2,1)} %get-tuple-element.66), channel_id=1, source_target_pairs={{0,8},{8,16},{16,24},{24,0},{1,9},{9,17},{17,25},{25,1},{2,10},{10... | collective-permute-start | bytes 1179656 | tf_op jit(solution)/shard_map/ppermute | solution.py:238
  122.6 13.9 %all-to-all-start.2 = ((f32[8,48,128]{2,1,0:T(8,128)}), f32[8,48,128]{2,1,0:T(8,128)S(1)}, u32[]{:S(2)}, u32[]{:S(2)}) async-start(f32[8,48,128]{2,1,0:T(8,128)} %bitcast.32), calls=%async_computation.2 | async-start | bytes 393216 | tf_op jit(solution)/shard_map/all_to_all | solution.py:415
  126.0 6.3 %collective-permute-start.20 = (bf16[128,768]{1,0:T(8,128)(2,1)}, bf16[128,768]{1,0:T(8,128)(2,1)S(1)}, u32[]{:S(2)}, u32[]{:S(2)}) collective-permute-start(bf16[128,768]{1,0:T(8,128)(2,1)} %collective-permute-done.19), channel_id=1, source_target_pairs={{0,24},{8,0},{16,8},{24,16},{1,25},{9,1},{17,9},{25,17},{2,26},{10... | collective-permute-start | bytes 589832 | tf_op jit(solution)/shard_map/ppermute | solution.py:238
  126.2 6.2 %collective-permute-start.22 = (bf16[128,768]{1,0:T(8,128)(2,1)}, bf16[128,768]{1,0:T(8,128)(2,1)S(1)}, u32[]{:S(2)}, u32[]{:S(2)}) collective-permute-start(bf16[128,768]{1,0:T(8,128)(2,1)} %collective-permute-done.21), channel_id=1, source_target_pairs={{0,8},{8,16},{16,24},{24,0},{1,9},{9,17},{17,25},{25,1},{2,10},{10... | collective-permute-start | bytes 589832 | tf_op jit(solution)/shard_map/ppermute | solution.py:238
  136.5 4.2 %collective-permute-start.23 = (f32[48,128]{1,0:T(8,128)S(1)}, f32[48,128]{1,0:T(8,128)S(1)}, u32[]{:S(2)}, u32[]{:S(2)}) collective-permute-start(f32[48,128]{1,0:T(8,128)S(1)} %reduce_sum.9), channel_id=1, source_target_pairs={{0,8},{8,16},{16,24},{24,0},{1,9},{9,17},{17,25},{25,1},{2,10},{10... | collective-permute-start | bytes 73736 | tf_op jit(solution)/shard_map/ppermute | solution.py:238
  137.6 4.2 %collective-permute-start.24 = (f32[48,128]{1,0:T(8,128)S(1)}, f32[48,128]{1,0:T(8,128)S(1)}, u32[]{:S(2)}, u32[]{:S(2)}) collective-permute-start(f32[48,128]{1,0:T(8,128)S(1)} %reduce_sum.9), channel_id=1, source_target_pairs={{0,16},{8,24},{16,0},{24,8},{1,17},{9,25},{17,1},{25,9},{2,18},{10... | collective-permute-start | bytes 73736 | tf_op jit(solution)/shard_map/ppermute | solution.py:238
  138.7 3.0 %collective-permute-start.25 = (f32[48,128]{1,0:T(8,128)S(1)}, f32[48,128]{1,0:T(8,128)S(1)}, u32[]{:S(2)}, u32[]{:S(2)}) collective-permute-start(f32[48,128]{1,0:T(8,128)S(1)} %reduce_sum.9), channel_id=1, source_target_pairs={{0,24},{8,0},{16,8},{24,16},{1,25},{9,1},{17,9},{25,17},{2,26},{10... | collective-permute-start | bytes 73736 | tf_op jit(solution)/shard_map/ppermute | solution.py:238
  142.4 14.8 %all-to-all-start.3 = ((f32[8,48,128]{2,1,0:T(8,128)}), f32[8,48,128]{2,1,0:T(8,128)S(1)}, u32[]{:S(2)}, u32[]{:S(2)}) async-start(f32[8,48,128]{2,1,0:T(8,128)} %broadcast_in_dim.27), calls=%async_computation.3 | async-start | bytes 393216 | tf_op jit(solution)/shard_map/all_to_all | solution.py:419
  160.6 7.0 %collective-permute-start.26 = (f32[48,384]{1,0:T(8,128)S(1)}, f32[48,384]{1,0:T(8,128)S(1)}, u32[]{:S(2)}, u32[]{:S(2)}) collective-permute-start(f32[48,384]{1,0:T(8,128)S(1)} %get-tuple-element.85), channel_id=1, source_target_pairs={{0,4},{4,0},{1,5},{5,1},{2,6},{6,2},{3,7},{7,3},{8,12},{12,8},{9,1... | collective-permute-start | bytes 221192 | tf_op jit(solution)/shard_map/ppermute | solution.py:238
  (14 other events, 169.8 us)
Sparse Core Ops, SparseCore 0:
  9.8 49.2 all-gather.1
